TPU v7x, 32 devices: a whole 2x2x4 slice. The times are simulated.
32 devices in a mesh: groups: 2 (over x), row: 16 (over z, y, core).
Axes of the slice: x: 2, y: 2, z: 4, core: 2. Of those that a mesh axis runs over, the one named last changes fastest.
Arguments:
- frames: bfloat16 [6, 64, 128, 16], P('groups', 'row'), parts along dimension 0, may hold values from -6 to 6
- coverage: int32 [64, 256], P('row', 'groups'), parts along dimension 1, may hold values 0 or 1
- h_init: bfloat16 [64, 256, 128], P('row', 'groups'), parts along dimension 1, may hold values from -1 to 1
- c_init: float32 [64, 256, 128], P('row', 'groups'), parts along dimension 1, may hold values from -6 to 6
- m_init: float32 [64, 256, 128], P('row', 'groups'), parts along dimension 1, may hold values from -6 to 6
- w_x: bfloat16 [5, 5, 16, 896], replicated, may hold values from -0.3125 to 0.3125
- w_h: bfloat16 [5, 5, 128, 512], replicated, may hold values from -0.109375 to 0.109375
- w_m: bfloat16 [5, 5, 128, 384], replicated, may hold values from -0.109375 to 0.109375
- w_o: bfloat16 [5, 5, 256, 128], replicated, may hold values from -0.078125 to 0.078125
- w_last: bfloat16 [256, 128], replicated, may hold values from -0.375 to 0.375
- w_out: bfloat16 [128, 16], replicated, may hold values from -0.5 to 0.5
Outputs:
- predicted: bfloat16 [6, 64, 128, 16], P('groups', 'row'), parts along dimension 0
- c_final: float32 [64, 256, 128], P('row', 'groups'), parts along dimension 1
- m_final: float32 [64, 256, 128], P('row', 'groups'), parts along dimension 1
There are 2 independent parts, one for each index of `groups`. A program takes and returns all parts, laid end to end along the dimension named above; an argument that names none is the same for every part. Nothing has to cross between parts.
All inputs are finite; a program needn't handle non-finite values. No bound on the sum of `coverage` on one device may be relied on, other than what follows from the above.
Results may differ from a plain program's by a relative error of at most 0.0061.
Values may be sent and summed in bfloat16 or wider, within the bound.
No kernel may reach another device: no remote copies, remote signals or barrier semaphores. Data moves between devices by JAX's collectives and lax.ppermute only.
A program may use at most 64 MiB of HBM per device.

v0:
```python
import functools

import jax
import jax.numpy as jnp
from jax import lax
from jax.experimental import pallas as pl
from jax.experimental.pallas import tpu as pltpu
from jax.sharding import PartitionSpec as P

STEPS = 3
TAPS = 5
REACH = 2
LANES = 128
BF = jnp.bfloat16
F32 = jnp.float32


def odd_device():
    return lax.rem(lax.axis_index("row"), 2)


def own_row(e):
    odd = odd_device()
    return e + odd * (3 - 2 * e)


def tap_row(p):
    odd = odd_device()
    return p + odd * (TAPS - 1 - 2 * p)


def sigmoid(x):
    return 0.5 * jnp.tanh(0.5 * x) + 0.5


def clear_pad(pad):
    rows, height = pad.shape[0], pad.shape[1]
    pad[:, :8] = jnp.zeros((rows, 8, LANES), F32)
    pad[:, height - 8 :] = jnp.zeros((rows, 8, LANES), F32)


def put_row(pad, slot, im, row, value, stride, lane0):
    cols = value.shape[0]
    pad[slot, 8 : 8 + cols] = value.astype(F32)
    for s in range(TAPS):
        im[row, :, s * stride + lane0 : s * stride + lane0 + LANES] = pad[
            slot, 6 + s : 6 + s + cols
        ].astype(BF)


def put_frame(pad, slot, im, row, packed, half, moment, width):
    cols = packed.shape[0]
    group = width * (STEPS * half + moment)
    value = packed.astype(F32)
    if group:
        value = pltpu.roll(value, LANES - group, 1)
    lane = lax.broadcasted_iota(jnp.int32, (cols, LANES), 1)
    value = jnp.where(lane < width, value, 0.0)
    pad[slot, 8 : 8 + cols] = value
    total = pad[slot, 6 : 6 + cols]
    for s in range(1, TAPS):
        total = total + pltpu.roll(pad[slot, 6 + s : 6 + s + cols], width * s, 1)
    im[row] = total.astype(BF)


H_PARTS = (
    (0, 256, ((0, 256),), ((0, 256, 0),)),
    (256, 512, ((256, 384), (768, 896)), ((256, 384, 0), (768, 896, 128))),
)
M_PARTS = (
    (0, 256, ((384, 640),), ((384, 640, 0),)),
    (256, 384, ((640, 768),), ((640, 768, 0),)),
)


def add_taps(acc, base, im, im_x, row0, x_row0, weight, w_x, parts, low, high, rows):
    cols = im.shape[1]
    order = range(TAPS) if low == 0 else range(TAPS - 1, -1, -1)
    begun = False
    for p in order:
        r0, r1 = max(0, low - p), min(rows, high - p)
        if r0 >= r1:
            continue
        count = (r1 - r0) * cols
        j = r0 + p
        lhs = jnp.concatenate(
            [
                im[j - row0 : j - row0 + r1 - r0].reshape(count, im.shape[2]),
                im_x[j - x_row0 : j - x_row0 + r1 - r0].reshape(count, LANES),
            ],
            axis=1,
        )
        tap = tap_row(p)
        here = slice(r0 * cols, r1 * cols)
        for c0, c1, x_cols, targets in parts:
            frame = jnp.concatenate([w_x[tap, :, x0:x1] for x0, x1 in x_cols], axis=1)
            fill = jnp.zeros((LANES - w_x.shape[1], c1 - c0), BF)
            rhs = jnp.concatenate([weight[tap, :, c0:c1], frame, fill], axis=0)
            part = jnp.dot(lhs, rhs, preferred_element_type=F32)
            for a0, a1, b0 in targets:
                value = part[:, b0 : b0 + a1 - a0]
                if begun:
                    acc[here, a0:a1] += value
                elif base is None:
                    acc[here, a0:a1] = value
                else:
                    acc[here, a0:a1] = base[here, a0:a1] + value
        begun = True


def new_state(gates, m_gates, width, c_old, m_old):
    def c_gate(k):
        return gates[:, k * width : (k + 1) * width]

    def m_gate(k):
        return m_gates[:, k * width : (k + 1) * width]

    c_new = sigmoid(c_gate(1) + 1.0) * c_old + sigmoid(c_gate(0)) * jnp.tanh(c_gate(2))
    m_new = sigmoid(m_gate(4) + 1.0) * m_old + sigmoid(m_gate(3)) * jnp.tanh(m_gate(5))
    return c_new, m_new


def pack_kernel(h_hbm, c_hbm, m_hbm, f_hbm, cov_hbm, far, near, c_own, m_own, f_ref, cov_ref, sems):
    cols = far.shape[1]
    width = f_ref.shape[2]
    copies = []
    for e in range(4):
        row = own_row(e)
        copies.append((m_hbm.at[row], m_own.at[e]))
        copies.append((c_hbm.at[row], c_own.at[e]))
        copies.append((h_hbm.at[row], far.at[e]))
        if e >= 2:
            copies.append((h_hbm.at[row], near.at[e - 2]))
    copies.append((f_hbm, f_ref))
    copies.append((cov_hbm, cov_ref))
    copies = [pltpu.make_async_copy(a, b, sems.at[i]) for i, (a, b) in enumerate(copies)]
    for copy in copies:
        copy.start()
    for copy in copies:
        copy.wait()
    for e in range(4):
        m = m_own[e].astype(BF)
        far[4 + e] = m
        if e < 2:
            far[8 + e] = c_own[e].astype(BF)
        else:
            near[e] = m
    for unit in range(2):
        parts = []
        for half in range(2):
            row = own_row(2 * unit + half)
            cover = cov_ref[pl.ds(row, 1), :].astype(F32)
            for moment in range(STEPS):
                parts.append(f_ref[moment, row].astype(F32) * cover)
        parts.append(jnp.zeros((LANES - 2 * STEPS * width, cols), F32))
        packed = jnp.concatenate(parts, axis=0).T.astype(BF)
        far[10 + unit] = packed
        if unit == 1:
            near[4] = packed


def local_kernel(moment, width_in, *refs):
    first = moment == 0
    if first:
        (
            far0, near0, c_own, m_own, x_hbm, h_hbm, m_hbm, o_hbm, last_hbm,
            acc, low_ref, c_out, m_out, w_x, w_h, w_m, w_o, w_last,
            pad, im_h, im_m, im_x, sems,
        ) = refs
        copies = [
            pltpu.make_async_copy(a, b, sems.at[i])
            for i, (a, b) in enumerate(
                ((x_hbm, w_x), (h_hbm, w_h), (m_hbm, w_m), (o_hbm, w_o), (last_hbm, w_last))
            )
        ]
        for copy in copies:
            copy.start()
    else:
        (
            far0, near0, arrived0, hid, hid_in, c_edge, m_edge, c_mid, m_mid, low_mid, low_in,
            w_x, w_h, w_m, acc, low_ref, c_out, m_out, im_x, pad, im_h, im_m,
        ) = refs
    cols = far0.shape[1]
    width = far0.shape[2]
    clear_pad(pad)
    for e in range(4):
        put_row(pad, e, im_h, e, far0[e] if first else hid[e], width, 0)
    for k in range(2):
        put_row(pad, 4 + k, im_h, 4 + k, near0[1 - k] if first else hid_in[1 - k], width, 0)
    base = 4 if first else 2
    slot = 16
    for e in range(4):
        put_frame(pad, slot + e, im_x, 4 + e - (4 if first else 0), far0[10 + e // 2], e % 2, moment, width_in)
    for k in range(2):
        put_frame(pad, slot + 4 + k, im_x, 8 + k - (4 if first else 0), near0[4], 1 - k, moment, width_in)
    if not first:
        for k in range(4):
            put_frame(pad, slot + 6 + k, im_x, 3 - k, arrived0[10 + k // 2], k % 2, moment, width_in)
    x_base = 4 if first else 0
    if first:
        for e in range(4):
            put_row(pad, 8 + e, im_m, e, far0[4 + e], width, 0)
        for k in range(2):
            put_row(pad, 12 + k, im_m, 4 + k, near0[3 - k], width, 0)
    else:
        for e in range(4):
            put_row(pad, 8 + e, im_m, e, m_edge[e].astype(BF), width, 0)
        for k in range(2):
            put_row(pad, 12 + k, im_m, 4 + k, low_mid[1, k], width, 0)
            put_row(pad, 14 + k, im_m, 6 + k, low_in[1, 1 - k], width, 0)
    if first:
        copies[0].wait()
        copies[1].wait()
    add_taps(acc, None, im_h, im_x, 4, x_base, w_h, w_x, H_PARTS, 4, 10, 6)
    if first:
        copies[2].wait()
    add_taps(acc, None, im_m, im_x, base, x_base, w_m, w_x, M_PARTS, base, 10, 6)
    for k in range(2):
        c_old, m_old = (c_own[2 + k], m_own[2 + k]) if first else (c_mid[k], m_mid[k])
        gates = acc[(4 + k) * cols : (5 + k) * cols, :]
        c_new, m_new = new_state(gates, gates, width, c_old, m_old)
        c_out[k] = c_new
        m_out[k] = m_new
        low_ref[0, k] = c_new.astype(BF)
        low_ref[1, k] = m_new.astype(BF)
    if first:
        copies[3].wait()
        copies[4].wait()


def final_kernel(moment, last, width_in, *refs):
    first = moment == 0
    refs = list(refs)
    if first:
        arrived, c_edge, m_edge = refs[:3]
        refs = refs[3:]
    else:
        arrived, c_edge, m_edge, im_x = refs[:4]
        refs = refs[4:]
    acc_in, low_mid, low_in, w_x, w_h, w_m, w_o, w_last = refs[:8]
    refs = refs[8:]
    if last:
        hid1, hid2, c_mid, m_mid, w_out, predicted, c_fin, m_fin = refs[:8]
        refs = refs[8:]
    else:
        far, near, c_out, m_out = refs[:4]
        refs = refs[4:]
    pad, im_h, im_m, im_j, acc, gate = refs[:6]
    if first:
        im_x = refs[6]
    if last:
        keep_c, keep_m, sems = refs[6:]
    cols = arrived.shape[1]
    width = arrived.shape[2]
    m_rows = 4 if first else 2
    clear_pad(pad)
    for k in range(4):
        put_row(pad, k, im_h, 3 - k, arrived[k], width, 0)
    for k in range(m_rows):
        put_row(pad, 4 + k, im_m, 3 - k if first else 1 - k, arrived[4 + k], width, 0)
    if first:
        for k in range(4):
            put_frame(pad, 24 + k, im_x, 3 - k, arrived[10 + k // 2], k % 2, moment, width_in)
    for k in range(2):
        for part in range(2):
            put_row(pad, 8 + 2 * k + part, im_j, 4 + k, low_mid[part, k], 2 * width, part * width)
            put_row(pad, 12 + 2 * k + part, im_j, 6 + k, low_in[part, 1 - k], 2 * width, part * width)
    add_taps(acc, acc_in, im_h, im_x, 0, 0, w_h, w_x, H_PARTS, 0, 4, 4)
    add_taps(acc, acc_in, im_m, im_x, 0, 0, w_m, w_x, M_PARTS, 0, m_rows, 4)
    place = lax.axis_index("row")
    inside = jnp.logical_and(place > 0, place < lax.axis_size("row") - 1)
    keep = jnp.where(inside, 1.0, 0.0).astype(F32)
    copies = []
    for r in range(4):
        if first and r < 2:
            c_old, m_old = arrived[9 - r].astype(F32), arrived[5 - r].astype(F32)
        elif first:
            c_old, m_old = c_edge[r - 2], m_edge[r - 2]
        else:
            c_old, m_old = c_edge[r], m_edge[r]
        here = slice(r * cols, (r + 1) * cols)
        gates = acc[here, :]
        m_gates = gates if r < m_rows else acc_in[here, :]
        c_new, m_new = new_state(gates, m_gates, width, c_old, m_old)
        if r < 2:
            c_new, m_new = c_new * keep, m_new * keep
        put_row(pad, 16 + 2 * r, im_j, r, c_new.astype(BF), 2 * width, 0)
        put_row(pad, 17 + 2 * r, im_j, r, m_new.astype(BF), 2 * width, width)
        if not last:
            c_out[r] = c_new
            m_out[r] = m_new
        elif r >= 2:
            keep_c[r - 2] = c_new
            keep_m[r - 2] = m_new
    if last:
        for e in range(4):
            sources = (keep_c.at[e], keep_m.at[e]) if e < 2 else (c_mid.at[e - 2], m_mid.at[e - 2])
            for n, (source, target) in enumerate(zip(sources, (c_fin, m_fin))):
                copies.append(pltpu.make_async_copy(source, target.at[own_row(e)], sems.at[2 * e + n]))
        for copy in copies:
            copy.start()
    for q in range(TAPS + 1):
        lhs = jnp.concatenate([im_j[q], im_j[q + 2]], axis=0)
        if q == 0:
            part = jnp.dot(lhs, w_o[tap_row(0)], preferred_element_type=F32)
            gate[:, :width] = part
        elif q == TAPS:
            part = jnp.dot(lhs, w_o[tap_row(TAPS - 1)], preferred_element_type=F32)
            gate[:, width:] += part
        else:
            rhs = jnp.concatenate([w_o[tap_row(q)], w_o[tap_row(q - 1)]], axis=1)
            part = jnp.dot(lhs, rhs, preferred_element_type=F32)
            gate[:, :width] += part[:, :width]
            if q == 1:
                gate[:, width:] = part[:, width:]
            else:
                gate[:, width:] += part[:, width:]
    rows = []
    for e in range(4):
        joined = im_j[2 + e, :, REACH * 2 * width : (REACH + 1) * 2 * width]
        mixed = jnp.dot(joined, w_last[...], preferred_element_type=F32)
        source = acc if e < 2 else acc_in
        pre = source[(2 + e) * cols : (3 + e) * cols, 6 * width :]
        half = e % 2
        pre = pre + gate[(e // 2) * cols : (e // 2 + 1) * cols, half * width : (half + 1) * width]
        hidden = (sigmoid(pre) * jnp.tanh(mixed)).astype(BF)
        if last:
            rows.append(hidden)
        else:
            far[e] = hidden
            if e >= 2:
                near[e - 2] = hidden
    if not last:
        for k in range(2):
            far[4 + k] = low_mid[1, k]
    else:
        for t, source in enumerate((hid1, hid2, rows)):
            for e in range(4):
                predicted[t, own_row(e)] = lax.dot_general(
                    w_out[...], source[e], (((1,), (1,)), ((), ())), preferred_element_type=F32
                ).astype(BF)
        for copy in copies:
            copy.wait()


VMEM = pl.BlockSpec(memory_space=pltpu.VMEM)
HBM = pl.BlockSpec(memory_space=pltpu.HBM)


def call(body, outs, scratch, args, flops, far_args=(), far_outs=()):
    return pl.pallas_call(
        body,
        out_shape=[jax.ShapeDtypeStruct(shape, kind) for shape, kind in outs],
        in_specs=[HBM if i in far_args else VMEM for i in range(len(args))],
        out_specs=[HBM if i in far_outs else VMEM for i in range(len(outs))],
        scratch_shapes=scratch,
        compiler_params=pltpu.CompilerParams(vmem_limit_bytes=16 * 2**20),
        cost_estimate=pl.CostEstimate(flops=flops, bytes_accessed=4 * 2**20, transcendentals=0),
    )(*args)


def per_device(frames, coverage, h_init, c_init, m_init, w_x, w_h, w_m, w_o, w_last, w_out):
    cols, width = h_init.shape[1], h_init.shape[2]
    width_in = frames.shape[3]
    count = lax.axis_size("row")
    across = [(i, i + 1) for i in range(1, count - 1, 2)]
    across += [(j, i) for i, j in across]
    beside = [(i, i ^ 1) for i in range(count)]
    w_x = w_x.reshape(TAPS, TAPS * width_in, -1)
    w_h = w_h.reshape(TAPS, TAPS * width, -1)
    w_m = w_m.reshape(TAPS, TAPS * width, -1)
    w_o = w_o.reshape(TAPS, TAPS * 2 * width, -1)
    w_out = w_out.T
    gates = w_x.shape[2]

    def rows(n, kind=BF):
        return ((n, cols, width), kind)

    def shaped(w):
        return (w.shape, w.dtype)

    flat = frames.transpose(0, 1, 3, 2)
    h_init, c_init, m_init, flat, coverage, w_x, w_h, w_m, w_o, w_last = (
        pltpu.with_memory_space_constraint(x, pltpu.HBM)
        for x in (h_init, c_init, m_init, flat, coverage, w_x, w_h, w_m, w_o, w_last)
    )
    far0, near0, c_edge, m_edge = call(
        pack_kernel,
        [rows(12), rows(5), rows(4, F32), rows(4, F32)],
        [
            pltpu.VMEM(flat.shape, flat.dtype),
            pltpu.VMEM(coverage.shape, coverage.dtype),
            pltpu.SemaphoreType.DMA((16,)),
        ],
        (h_init, c_init, m_init, flat, coverage),
        10**6,
        far_args=range(5),
    )
    near0_in = lax.ppermute(near0, "row", beside)
    arrived0 = lax.ppermute(far0, "row", across)
    arrived = arrived0
    hiddens = []
    for moment in range(STEPS):
        first, last = moment == 0, moment == STEPS - 1
        outs = [((6 * cols, gates), F32), ((2, 2, cols, width), BF), rows(2, F32), rows(2, F32)]
        scratch = [
            pltpu.VMEM((26, cols + 16, LANES), F32),
            pltpu.VMEM((6, cols, TAPS * width), BF),
            pltpu.VMEM((6 if first else 8, cols, TAPS * width), BF),
        ]
        if first:
            args = (far0, near0_in, c_edge, m_edge, w_x, w_h, w_m, w_o, w_last)
            outs += [shaped(w) for w in args[4:]]
            scratch += [pltpu.VMEM((6, cols, LANES), BF), pltpu.SemaphoreType.DMA((5,))]
            far_args = range(4, 9)
        else:
            args = (far0, near0_in, arrived0, far, near_in, c_edge, m_edge, c_mid, m_mid, low_mid, low_in)
            args += (w_x, w_h, w_m)
            outs.append(((10, cols, LANES), BF))
            far_args = ()
        done = call(
            functools.partial(local_kernel, moment, width_in), outs, scratch, args, 4 * 10**9, far_args
        )
        acc, low_mid, c_mid, m_mid = done[:4]
        if first:
            w_x, w_h, w_m, w_o, w_last = done[4:]
        low_in = lax.ppermute(low_mid, "row", beside)
        args = (arrived, c_edge, m_edge)
        if not first:
            args += (done[4],)
        args += (acc, low_mid, low_in, w_x, w_h, w_m, w_o, w_last)
        far_outs = ()
        if last:
            args += (hiddens[0], hiddens[1], c_mid, m_mid, w_out)
            outs = [((STEPS, 4, width_in, cols), BF), rows(4, F32), rows(4, F32)]
            far_outs = (1, 2)
        else:
            outs = [rows(6), rows(2), rows(4, F32), rows(4, F32)]
        scratch = [
            pltpu.VMEM((32, cols + 16, LANES), F32),
            pltpu.VMEM((4, cols, TAPS * width), BF),
            pltpu.VMEM((4 if first else 2, cols, TAPS * width), BF),
            pltpu.VMEM((8, cols, 2 * TAPS * width), BF),
            pltpu.VMEM((4 * cols, gates), F32),
            pltpu.VMEM((2 * cols, 2 * width), F32),
        ]
        if first:
            scratch.append(pltpu.VMEM((4, cols, LANES), BF))
        if last:
            scratch += [pltpu.VMEM(*rows(2, F32)), pltpu.VMEM(*rows(2, F32)), pltpu.SemaphoreType.DMA((8,))]
        done = call(
            functools.partial(final_kernel, moment, last, width_in),
            outs, scratch, args, 3 * 10**9, far_outs=far_outs,
        )
        if last:
            predicted, c_final, m_final = done
            return predicted.transpose(0, 1, 3, 2), c_final, m_final
        far, near, c_edge, m_edge = done
        hiddens.append(far)
        near_in = lax.ppermute(near, "row", beside)
        arrived = lax.ppermute(far, "row", across)


def solution(mesh):
    placed = (
        P("groups", "row", None, None),
        P("row", "groups"),
        P("row", "groups", None),
        P("row", "groups", None),
        P("row", "groups", None),
        P(),
        P(),
        P(),
        P(),
        P(),
        P(),
    )
    return jax.shard_map(
        per_device,
        mesh=mesh,
        in_specs=placed,
        out_specs=(
            P("groups", "row", None, None),
            P("row", "groups", None),
            P("row", "groups", None),
        ),
        check_vma=False,
    )
```

profile of v0, /device:TPU:0, one launch (start us, length us, event | category | flops | bytes accessed | tf_op | source)
XLA Modules:
  0.0 49.2 jit_solution(17638457812163342353)
XLA Ops:
  0.6 1.4 %shard_map.130 = (bf16[12,128,128]{2,1,0:T(8,128)(2,1)S(1)}, bf16[5,128,128]{2,1,0:T(8,128)(2,1)S(1)}, f32[4,128,128]{2,1,0:T(8,128)S(1)}, f32[4,128,128]{2,1,0:T(8,128)S(1)}) custom-call(bf16[4,128,128]{2,1,0:T(8,128)(2,1)} %h_hbm.1, f32[4,128,128]{2,1,0:T(8,128)} %c_hbm.1, f32[4,128,128]{2,1,0:T(8,128)} %m_hbm.1, bf16[3,4,16,128]{3,2,1,0:T(8,128)(2,1)} %bitcast.8, ...), custom_call_target="tpu_custom_call" | custom-call | flops 1000000 | bytes 4194304 | tf_op jit(solution)/shard_map/pallas_call | solution.py:351
  2.0 0.5 %collective-permute-start.1 = (bf16[5,128,128]{2,1,0:T(8,128)(2,1)S(1)}, bf16[5,128,128]{2,1,0:T(8,128)(2,1)S(1)}, u32[]{:S(2)}, u32[]{:S(2)}) collective-permute-start(bf16[5,128,128]{2,1,0:T(8,128)(2,1)S(1)} %get-tuple-element.40), channel_id=1, source_target_pairs={{0,1},{1,0},{2,3},{3,2},{4,5},{5,4},{6,7},{7,6},{8,9},{9,8},{10,11... | collective-permute-start | bytes 491528 | tf_op jit(solution)/shard_map/ppermute | solution.py:399
  2.6 0.7 %collective-permute-start = (bf16[12,128,128]{2,1,0:T(8,128)(2,1)S(1)}, bf16[12,128,128]{2,1,0:T(8,128)(2,1)S(1)}, u32[]{:S(2)}, u32[]{:S(2)}) collective-permute-start(bf16[12,128,128]{2,1,0:T(8,128)(2,1)S(1)} %get-tuple-element.37.refs_0_), channel_id=1, source_target_pairs={{1,2},{3,4},{5,6},{7,8},{9,10},{11,12},{13,14},{2,1},{4,3},{6,5},{... | collective-permute-start | bytes 1179656 | tf_op jit(solution)/shard_map/ppermute | solution.py:400
  3.2 0.3 collective-permute-done.1.refs_1_
  3.6 7.4 %shard_map.131 = (f32[768,896]{1,0:T(8,128)S(1)}, bf16[2,2,128,128]{3,2,1,0:T(8,128)(2,1)S(1)}, f32[2,128,128]{2,1,0:T(8,128)S(1)}, f32[2,128,128]{2,1,0:T(8,128...) custom-call(bf16[12,128,128]{2,1,0:T(8,128)(2,1)S(1)} %get-tuple-ele, ...), custom_call_target="tpu_custom_call" | custom-call | flops 4000000000 | bytes 4194304 | tf_op jit(solution)/shard_map/pallas_call | solution.py:351
  11.0 3.6 %collective-permute-start.2 = (bf16[2,2,128,128]{3,2,1,0:T(8,128)(2,1)S(1)}, bf16[2,2,128,128]{3,2,1,0:T(8,128)(2,1)S(1)}, u32[]{:S(2)}, u32[]{:S(2)}) collective-permute-start(bf16[2,2,128,128]{3,2,1,0:T(8,128)(2,1)S(1)} %get-tuple-element.42.refs_4_.refs_9_), channel_id=1, source_target_pairs={{0,1},{1,0},{2,3},{3,2},{4,5},{5,4},{6,7},{7,6},{8,9},{9,8},{10,11... | collective-permute-start | bytes 393224 | tf_op jit(solution)/shard_map/ppermute | solution.py:427
  14.6 1.0 %collective-permute-done.2.refs_5_.refs_10_ = bf16[2,2,128,128]{3,2,1,0:T(8,128)(2,1)S(1)} collective-permute-done((bf16[2,2,128,128]{3,2,1,0:T(8,128)(2,1)S(1)}, bf16[2,2,128,128]{3,2,1,0:T(8,128)(2,1)S(1)}, u32[]{:S(2)}, u32[]{:S(2)}) %collective-permute-start.2) | collective-permute-done | bytes 131104 | tf_op jit(solution)/shard_map/ppermute | solution.py:427
  15.6 0.0 collective-permute-done.refs_0_.refs_2_
  15.6 3.7 %shard_map.132 = (bf16[6,128,128]{2,1,0:T(8,128)(2,1)S(1)}, bf16[2,128,128]{2,1,0:T(8,128)(2,1)S(1)}, f32[4,128,128]{2,1,0:T(8,128)S(1)}, f32[4,128,128]{2,1,0:T(8,128)S(1)}) custom-call(bf16[12,128,128]{2,1,0:T(8,128)(2,1)S(1)} %collective-permute-done.refs_0_.refs_2_, f32[4,128,128]{2,1,0:T(8,128)S(1)} %get-tuple-element.38.refs_2_.refs_1_, ...), custom_call_target="tpu_custom_call" | custom-call | flops 3000000000 | bytes 4194304 | tf_op jit(solution)/shard_map/pallas_call | solution.py:351
  19.3 0.5 %collective-permute-start.4 = (bf16[2,128,128]{2,1,0:T(8,128)(2,1)S(1)}, bf16[2,128,128]{2,1,0:T(8,128)(2,1)S(1)}, u32[]{:S(2)}, u32[]{:S(2)}) collective-permute-start(bf16[2,128,128]{2,1,0:T(8,128)(2,1)S(1)} %get-tuple-element.51), channel_id=1, source_target_pairs={{0,1},{1,0},{2,3},{3,2},{4,5},{5,4},{6,7},{7,6},{8,9},{9,8},{10,11... | collective-permute-start | bytes 196616 | tf_op jit(solution)/shard_map/ppermute | solution.py:460
  19.9 0.8 %collective-permute-start.3 = (bf16[6,128,128]{2,1,0:T(8,128)(2,1)S(1)}, bf16[6,128,128]{2,1,0:T(8,128)(2,1)S(1)}, u32[]{:S(2)}, u32[]{:S(2)}) collective-permute-start(bf16[6,128,128]{2,1,0:T(8,128)(2,1)S(1)} %get-tuple-element.48.refs_3_.refs_12_), channel_id=1, source_target_pairs={{1,2},{3,4},{5,6},{7,8},{9,10},{11,12},{13,14},{2,1},{4,3},{6,5},{... | collective-permute-start | bytes 589832 | tf_op jit(solution)/shard_map/ppermute | solution.py:461
  20.7 0.1 collective-permute-done.4.refs_4_
  20.8 5.2 %shard_map.133 = (f32[768,896]{1,0:T(8,128)S(1)}, bf16[2,2,128,128]{3,2,1,0:T(8,128)(2,1)S(1)}, f32[2,128,128]{2,1,0:T(8,128)S(1)}, f32[2,128,128]{2,1,0:T(8,128)S(1)}, bf16[10,128,128]{2,1,0:T(8,128)(2,1)S(1)}) custom-call(bf16[12,128,128]{2,1,0:T(8,128)(2,1)S(1)} %get-tuple-element.37.refs_0_, bf16[5,128,128]{2,1,0:T(8,128)(2,1)S(1)} %collective-permute-done.1.refs_1_, ...), custom_call_target="tpu_custom_call" | custom-call | flops 4000000000 | bytes 4194304 | tf_op jit(solution)/shard_map/pallas_call | solution.py:351
  26.0 3.8 %collective-permute-start.5 = (bf16[2,2,128,128]{3,2,1,0:T(8,128)(2,1)S(1)}, bf16[2,2,128,128]{3,2,1,0:T(8,128)(2,1)S(1)}, u32[]{:S(2)}, u32[]{:S(2)}) collective-permute-start(bf16[2,2,128,128]{3,2,1,0:T(8,128)(2,1)S(1)} %get-tuple-element.56.refs_5_.refs_9_), channel_id=1, source_target_pairs={{0,1},{1,0},{2,3},{3,2},{4,5},{5,4},{6,7},{7,6},{8,9},{9,8},{10,11... | collective-permute-start | bytes 393224 | tf_op jit(solution)/shard_map/ppermute | solution.py:427
  29.8 0.0 collective-permute-done.3.refs_0_
  29.8 1.0 %collective-permute-done.5.refs_6_.refs_10_ = bf16[2,2,128,128]{3,2,1,0:T(8,128)(2,1)S(1)} collective-permute-done((bf16[2,2,128,128]{3,2,1,0:T(8,128)(2,1)S(1)}, bf16[2,2,128,128]{3,2,1,0:T(8,128)(2,1)S(1)}, u32[]{:S(2)}, u32[]{:S(2)}) %collective-permute-start.5) | collective-permute-done | bytes 131104 | tf_op jit(solution)/shard_map/ppermute | solution.py:427
  30.7 3.0 %shard_map.134 = (bf16[6,128,128]{2,1,0:T(8,128)(2,1)S(1)}, bf16[2,128,128]{2,1,0:T(8,128)(2,1)S(1)}, f32[4,128,128]{2,1,0:T(8,128)S(1)}, f32[4,128,128]{2,1,0:T(8,128)S(1)}) custom-call(bf16[6,128,128]{2,1,0:T(8,128)(2,1)S(1)} %collective-permute-done.3.refs_0_, f32[4,128,128]{2,1,0:T(8,128)S(1)} %get-tuple-element.49.refs_5_.refs_1_, ...), custom_call_target="tpu_custom_call" | custom-call | flops 3000000000 | bytes 4194304 | tf_op jit(solution)/shard_map/pallas_call | solution.py:351
  33.8 0.4 collective-permute-start.7
  34.2 0.7 %collective-permute-start.6 = (bf16[6,128,128]{2,1,0:T(8,128)(2,1)S(1)}, bf16[6,128,128]{2,1,0:T(8,128)(2,1)S(1)}, u32[]{:S(2)}, u32[]{:S(2)}) collective-permute-start(bf16[6,128,128]{2,1,0:T(8,128)(2,1)S(1)} %get-tuple-element.57.refs_3_.refs_13_), channel_id=1, source_target_pairs={{1,2},{3,4},{5,6},{7,8},{9,10},{11,12},{13,14},{2,1},{4,3},{6,5},{... | collective-permute-start | bytes 589832 | tf_op jit(solution)/shard_map/ppermute | solution.py:461
  34.9 0.2 collective-permute-done.7.refs_4_
  35.1 0.0 copy-start
  35.1 5.2 %shard_map.135 = (f32[768,896]{1,0:T(8,128)S(1)}, bf16[2,2,128,128]{3,2,1,0:T(8,128)(2,1)S(1)}, f32[2,128,128]{2,1,0:T(8,128)S(1)}, f32[2,128,128]{2,1,0:T(8,128)S(1)}, bf16[10,128,128]{2,1,0:T(8,128)(2,1)S(1)}) custom-call(bf16[12,128,128]{2,1,0:T(8,128)(2,1)S(1)} %get-tuple-element.37.refs_0_, bf16[5,128,128]{2,1,0:T(8,128)(2,1)S(1)} %collective-permute-done.1.refs_1_, ...), custom_call_target="tpu_custom_call" | custom-call | flops 4000000000 | bytes 4194304 | tf_op jit(solution)/shard_map/pallas_call | solution.py:351
  40.4 3.2 %collective-permute-start.8 = (bf16[2,2,128,128]{3,2,1,0:T(8,128)(2,1)S(1)}, bf16[2,2,128,128]{3,2,1,0:T(8,128)(2,1)S(1)}, u32[]{:S(2)}, u32[]{:S(2)}) collective-permute-start(bf16[2,2,128,128]{3,2,1,0:T(8,128)(2,1)S(1)} %get-tuple-element.65.refs_5_), channel_id=1, source_target_pairs={{0,1},{1,0},{2,3},{3,2},{4,5},{5,4},{6,7},{7,6},{8,9},{9,8},{10,11... | collective-permute-start | bytes 393224 | tf_op jit(solution)/shard_map/ppermute | solution.py:427
  43.6 0.0 collective-permute-done.6.refs_0_
  43.6 1.0 %collective-permute-done.8.refs_6_ = bf16[2,2,128,128]{3,2,1,0:T(8,128)(2,1)S(1)} collective-permute-done((bf16[2,2,128,128]{3,2,1,0:T(8,128)(2,1)S(1)}, bf16[2,2,128,128]{3,2,1,0:T(8,128)(2,1)S(1)}, u32[]{:S(2)}, u32[]{:S(2)}) %collective-permute-start.8) | collective-permute-done | bytes 131104 | tf_op jit(solution)/shard_map/ppermute | solution.py:427
  44.5 0.0 copy-done
  44.6 4.5 %shard_map.136 = (bf16[3,4,16,128]{3,2,1,0:T(8,128)(2,1)}, f32[4,128,128]{2,1,0:T(8,128)}, f32[4,128,128]{2,1,0:T(8,128)}) custom-call(bf16[6,128,128]{2,1,0:T(8,128)(2,1)S(1)} %collective-permute-done.6.refs_0_, f32[4,128,128]{2,1,0:T(8,128)S(1)} %get-tuple-element.58.refs_5_.refs_1_, f32[4,128,128]{2,1,0:T(8,128)S(1)} %get-tuple-element.59.refs_6_.refs_2_, ...), custom_call_target="tpu_custom_call" | custom-call | flops 3000000000 | bytes 4194304 | tf_op jit(solution)/shard_map/pallas_call | solution.py:351
Async XLA Ops:
  2.0 1.5 %collective-permute-start.1 = (bf16[5,128,128]{2,1,0:T(8,128)(2,1)S(1)}, bf16[5,128,128]{2,1,0:T(8,128)(2,1)S(1)}, u32[]{:S(2)}, u32[]{:S(2)}) collective-permute-start(bf16[5,128,128]{2,1,0:T(8,128)(2,1)S(1)} %get-tuple-element.40), channel_id=1, source_target_pairs={{0,1},{1,0},{2,3},{3,2},{4,5},{5,4},{6,7},{7,6},{8,9},{9,8},{10,11... | collective-permute-start | bytes 491528 | tf_op jit(solution)/shard_map/ppermute | solution.py:399
  2.6 13.0 %collective-permute-start = (bf16[12,128,128]{2,1,0:T(8,128)(2,1)S(1)}, bf16[12,128,128]{2,1,0:T(8,128)(2,1)S(1)}, u32[]{:S(2)}, u32[]{:S(2)}) collective-permute-start(bf16[12,128,128]{2,1,0:T(8,128)(2,1)S(1)} %get-tuple-element.37.refs_0_), channel_id=1, source_target_pairs={{1,2},{3,4},{5,6},{7,8},{9,10},{11,12},{13,14},{2,1},{4,3},{6,5},{... | collective-permute-start | bytes 1179656 | tf_op jit(solution)/shard_map/ppermute | solution.py:400
  11.0 4.6 %collective-permute-start.2 = (bf16[2,2,128,128]{3,2,1,0:T(8,128)(2,1)S(1)}, bf16[2,2,128,128]{3,2,1,0:T(8,128)(2,1)S(1)}, u32[]{:S(2)}, u32[]{:S(2)}) collective-permute-start(bf16[2,2,128,128]{3,2,1,0:T(8,128)(2,1)S(1)} %get-tuple-element.42.refs_4_.refs_9_), channel_id=1, source_target_pairs={{0,1},{1,0},{2,3},{3,2},{4,5},{5,4},{6,7},{7,6},{8,9},{9,8},{10,11... | collective-permute-start | bytes 393224 | tf_op jit(solution)/shard_map/ppermute | solution.py:427
  19.3 1.4 %collective-permute-start.4 = (bf16[2,128,128]{2,1,0:T(8,128)(2,1)S(1)}, bf16[2,128,128]{2,1,0:T(8,128)(2,1)S(1)}, u32[]{:S(2)}, u32[]{:S(2)}) collective-permute-start(bf16[2,128,128]{2,1,0:T(8,128)(2,1)S(1)} %get-tuple-element.51), channel_id=1, source_target_pairs={{0,1},{1,0},{2,3},{3,2},{4,5},{5,4},{6,7},{7,6},{8,9},{9,8},{10,11... | collective-permute-start | bytes 196616 | tf_op jit(solution)/shard_map/ppermute | solution.py:460
  19.9 9.9 %collective-permute-start.3 = (bf16[6,128,128]{2,1,0:T(8,128)(2,1)S(1)}, bf16[6,128,128]{2,1,0:T(8,128)(2,1)S(1)}, u32[]{:S(2)}, u32[]{:S(2)}) collective-permute-start(bf16[6,128,128]{2,1,0:T(8,128)(2,1)S(1)} %get-tuple-element.48.refs_3_.refs_12_), channel_id=1, source_target_pairs={{1,2},{3,4},{5,6},{7,8},{9,10},{11,12},{13,14},{2,1},{4,3},{6,5},{... | collective-permute-start | bytes 589832 | tf_op jit(solution)/shard_map/ppermute | solution.py:461
  26.0 4.8 %collective-permute-start.5 = (bf16[2,2,128,128]{3,2,1,0:T(8,128)(2,1)S(1)}, bf16[2,2,128,128]{3,2,1,0:T(8,128)(2,1)S(1)}, u32[]{:S(2)}, u32[]{:S(2)}) collective-permute-start(bf16[2,2,128,128]{3,2,1,0:T(8,128)(2,1)S(1)} %get-tuple-element.56.refs_5_.refs_9_), channel_id=1, source_target_pairs={{0,1},{1,0},{2,3},{3,2},{4,5},{5,4},{6,7},{7,6},{8,9},{9,8},{10,11... | collective-permute-start | bytes 393224 | tf_op jit(solution)/shard_map/ppermute | solution.py:427
  33.8 1.3 %collective-permute-start.7 = (bf16[2,128,128]{2,1,0:T(8,128)(2,1)S(1)}, bf16[2,128,128]{2,1,0:T(8,128)(2,1)S(1)}, u32[]{:S(2)}, u32[]{:S(2)}) collective-permute-start(bf16[2,128,128]{2,1,0:T(8,128)(2,1)S(1)} %get-tuple-element.60), channel_id=1, source_target_pairs={{0,1},{1,0},{2,3},{3,2},{4,5},{5,4},{6,7},{7,6},{8,9},{9,8},{10,11... | collective-permute-start | bytes 196616 | tf_op jit(solution)/shard_map/ppermute | solution.py:460
  34.2 9.4 %collective-permute-start.6 = (bf16[6,128,128]{2,1,0:T(8,128)(2,1)S(1)}, bf16[6,128,128]{2,1,0:T(8,128)(2,1)S(1)}, u32[]{:S(2)}, u32[]{:S(2)}) collective-permute-start(bf16[6,128,128]{2,1,0:T(8,128)(2,1)S(1)} %get-tuple-element.57.refs_3_.refs_13_), channel_id=1, source_target_pairs={{1,2},{3,4},{5,6},{7,8},{9,10},{11,12},{13,14},{2,1},{4,3},{6,5},{... | collective-permute-start | bytes 589832 | tf_op jit(solution)/shard_map/ppermute | solution.py:461
  35.1 9.4 %copy-start = (bf16[128,16]{0,1:T(8,128)(2,1)S(1)}, bf16[128,16]{0,1:T(8,128)(2,1)}, u32[]{:S(2)}) copy-start(bf16[128,16]{0,1:T(8,128)(2,1)} %param.21) | copy-start | bytes 12292
  40.4 4.2 %collective-permute-start.8 = (bf16[2,2,128,128]{3,2,1,0:T(8,128)(2,1)S(1)}, bf16[2,2,128,128]{3,2,1,0:T(8,128)(2,1)S(1)}, u32[]{:S(2)}, u32[]{:S(2)}) collective-permute-start(bf16[2,2,128,128]{3,2,1,0:T(8,128)(2,1)S(1)} %get-tuple-element.65.refs_5_), channel_id=1, source_target_pairs={{0,1},{1,0},{2,3},{3,2},{4,5},{5,4},{6,7},{7,6},{8,9},{9,8},{10,11... | collective-permute-start | bytes 393224 | tf_op jit(solution)/shard_map/ppermute | solution.py:427
where the time goes:
time: 49.4 us; the launch traced here: 49.2 us
  Pallas kernels  30.5 us (62%)
  starting transfers between devices  14.2 us (29%)
  waiting for transfers between devices  3.59 us (7%)
  between operations  0.87 us (2%)
    pallas_call x7, Pallas kernels, call(): pl.pallas_call(body, out_shape=[jax.ShapeDtypeStruct(shape, kind) for sha...  30.5 us
    ppermute x3, starting transfers between devices, per_device(): low_in = lax.ppermute(low_mid, 'row', beside)  10.6 us
    ppermute x3, waiting for transfers between devices, per_device(): low_in = lax.ppermute(low_mid, 'row', beside)  2.95 us
    ppermute x2, starting transfers between devices, per_device(): arrived = lax.ppermute(far, 'row', across)  1.5 us
  transfers between devices with their start and end apart: 9, of which 6 were waited for; matrix products, arithmetic and copies ran while one was open for 0% of the time, Pallas kernels for 36%

commit v1 on v0

--- a/solution.py
+++ b/solution.py
@@ -106,6 +106,56 @@
                 else:
                     acc[here, a0:a1] = base[here, a0:a1] + value
         begun = True
+
+
+def frame_rows(w_x, tap, spans):
+    values = jnp.concatenate([w_x[tap, :, a:b] for a, b in spans], axis=1)
+    fill = jnp.zeros((LANES - values.shape[0], values.shape[1]), BF)
+    return [values, fill]
+
+
+def add_memory_pairs(acc, im, im_x, row0, x_row0, weight, w_x, low, rows):
+    cols = im.shape[1]
+    width = weight.shape[2] // 3
+    gates = 3 * width
+
+    def lhs_of(j0, j1):
+        count = (j1 - j0) * cols
+        return jnp.concatenate(
+            [
+                im[j0 - row0 : j1 - row0].reshape(count, im.shape[2]),
+                im_x[j0 - x_row0 : j1 - x_row0].reshape(count, LANES),
+            ],
+            axis=1,
+        )
+
+    def rhs_of(p, a, b):
+        tap = tap_row(p)
+        rest = frame_rows(w_x, tap, ((gates + a, gates + b),))
+        return jnp.concatenate([weight[tap, :, a:b]] + rest, axis=0)
+
+    def product(lhs, rhs):
+        return jnp.dot(lhs, rhs, preferred_element_type=F32)
+
+    p = TAPS - 1
+    r0 = max(0, low - p)
+    lhs = lhs_of(r0 + p, rows + p)
+    for a, b in ((0, 2 * width), (2 * width, gates)):
+        acc[r0 * cols : rows * cols, gates + a : gates + b] = product(lhs, rhs_of(p, a, b))
+    for p in (2, 0):
+        q = p + 1
+        rp, rq = max(0, low - p), max(0, low - q)
+        part = product(lhs_of(rp + p, rows + p), rhs_of(p, 0, 2 * width))
+        acc[rp * cols : rows * cols, gates : gates + 2 * width] += part
+        part = product(lhs_of(rq + q, rows + q), rhs_of(q, width, gates))
+        acc[rq * cols : rows * cols, gates + width : 2 * gates] += part
+        j0 = min(rp + p, rq + q)
+        rhs = jnp.concatenate([rhs_of(p, 2 * width, gates), rhs_of(q, 0, width)], axis=1)
+        part = product(lhs_of(j0, rows + q), rhs)
+        a = (rp + p - j0) * cols
+        acc[rp * cols : rows * cols, gates + 2 * width : 2 * gates] += part[a : a + (rows - rp) * cols, :width]
+        a = (rq + q - j0) * cols
+        acc[rq * cols : rows * cols, gates : gates + width] += part[a : a + (rows - rq) * cols, width:]
 
 
 def new_state(gates, m_gates, width, c_old, m_old):
@@ -214,7 +264,7 @@
     add_taps(acc, None, im_h, im_x, 4, x_base, w_h, w_x, H_PARTS, 4, 10, 6)
     if first:
         copies[2].wait()
-    add_taps(acc, None, im_m, im_x, base, x_base, w_m, w_x, M_PARTS, base, 10, 6)
+    add_memory_pairs(acc, im_m, im_x, base, x_base, w_m, w_x, base, 6)
     for k in range(2):
         c_old, m_old = (c_own[2 + k], m_own[2 + k]) if first else (c_mid[k], m_mid[k])
         gates = acc[(4 + k) * cols : (5 + k) * cols, :]
@@ -228,6 +278,39 @@
         copies[4].wait()
 
 
+def two_taps(lhs, w_o, p, q):
+    rhs = jnp.concatenate([w_o[tap_row(p)], w_o[tap_row(q)]], axis=1)
+    return jnp.dot(lhs, rhs, preferred_element_type=F32)
+
+
+def predict(target, hidden, w_out):
+    for e in range(4):
+        target[e] = lax.dot_general(
+            w_out[...], hidden[e], (((1,), (1,)), ((), ())), preferred_element_type=F32
+        ).astype(BF)
+
+
+def inner_kernel(first, *refs):
+    if first:
+        low_mid, w_o, gate, pad, im = refs
+    else:
+        low_mid, w_o, hid, w_out, gate, predicted, pad, im = refs
+    cols, width = low_mid.shape[2], low_mid.shape[3]
+    clear_pad(pad)
+    for k in range(2):
+        for part in range(2):
+            put_row(pad, 2 * k + part, im, k, low_mid[part, k], 2 * width, part * width)
+    lhs = im[...].reshape(2 * cols, im.shape[2])
+    part = two_taps(lhs, w_o, 4, 3)
+    gate[:cols] = part[:cols, :width]
+    gate[cols : 2 * cols] = part[cols:, :width] + part[:cols, width:]
+    more = two_taps(lhs, w_o, 2, 1)
+    gate[2 * cols : 3 * cols] = part[cols:, width:] + more[:cols, :width]
+    gate[3 * cols :] = more[cols:, :width] + more[:cols, width:]
+    if not first:
+        predict(predicted, hid, w_out)
+
+
 def final_kernel(moment, last, width_in, *refs):
     first = moment == 0
     refs = list(refs)
@@ -237,19 +320,19 @@
     else:
         arrived, c_edge, m_edge, im_x = refs[:4]
         refs = refs[4:]
-    acc_in, low_mid, low_in, w_x, w_h, w_m, w_o, w_last = refs[:8]
-    refs = refs[8:]
+    acc_in, low_mid, low_in, gate_in, w_x, w_h, w_m, w_o, w_last = refs[:9]
+    refs = refs[9:]
     if last:
-        hid1, hid2, c_mid, m_mid, w_out, predicted, c_fin, m_fin = refs[:8]
+        pred1, pred2, c_mid, m_mid, w_out, predicted, c_fin, m_fin = refs[:8]
         refs = refs[8:]
     else:
         far, near, c_out, m_out = refs[:4]
         refs = refs[4:]
-    pad, im_h, im_m, im_j, acc, gate = refs[:6]
-    if first:
-        im_x = refs[6]
+    pad, im_h, im_m, im_j, im_i, acc, gate = refs[:7]
+    if first:
+        im_x = refs[7]
     if last:
-        keep_c, keep_m, sems = refs[6:]
+        keep_c, keep_m, sems = refs[7:]
     cols = arrived.shape[1]
     width = arrived.shape[2]
     m_rows = 4 if first else 2
@@ -263,8 +346,7 @@
             put_frame(pad, 24 + k, im_x, 3 - k, arrived[10 + k // 2], k % 2, moment, width_in)
     for k in range(2):
         for part in range(2):
-            put_row(pad, 8 + 2 * k + part, im_j, 4 + k, low_mid[part, k], 2 * width, part * width)
-            put_row(pad, 12 + 2 * k + part, im_j, 6 + k, low_in[part, 1 - k], 2 * width, part * width)
+            put_row(pad, 12 + 2 * k + part, im_i, k, low_in[part, 1 - k], 2 * width, part * width)
     add_taps(acc, acc_in, im_h, im_x, 0, 0, w_h, w_x, H_PARTS, 0, 4, 4)
     add_taps(acc, acc_in, im_m, im_x, 0, 0, w_m, w_x, M_PARTS, 0, m_rows, 4)
     place = lax.axis_index("row")
@@ -299,30 +381,25 @@
                 copies.append(pltpu.make_async_copy(source, target.at[own_row(e)], sems.at[2 * e + n]))
         for copy in copies:
             copy.start()
-    for q in range(TAPS + 1):
-        lhs = jnp.concatenate([im_j[q], im_j[q + 2]], axis=0)
-        if q == 0:
-            part = jnp.dot(lhs, w_o[tap_row(0)], preferred_element_type=F32)
-            gate[:, :width] = part
-        elif q == TAPS:
-            part = jnp.dot(lhs, w_o[tap_row(TAPS - 1)], preferred_element_type=F32)
-            gate[:, width:] += part
-        else:
-            rhs = jnp.concatenate([w_o[tap_row(q)], w_o[tap_row(q - 1)]], axis=1)
-            part = jnp.dot(lhs, rhs, preferred_element_type=F32)
-            gate[:, :width] += part[:, :width]
-            if q == 1:
-                gate[:, width:] = part[:, width:]
-            else:
-                gate[:, width:] += part[:, width:]
+    part = two_taps(im_j[0:4].reshape(4 * cols, -1), w_o, 0, 1)
+    gate[...] = part[:, :width] + gate_in[...]
+    gate[: 3 * cols] += part[cols:, width:]
+    part = two_taps(im_j[2:4].reshape(2 * cols, -1), w_o, 2, 3)
+    gate[: 2 * cols] += part[:, :width]
+    gate[:cols] += part[cols:, width:]
+    part = two_taps(im_i[...].reshape(2 * cols, -1), w_o, 4, 3)
+    gate[2 * cols :] += part[:, :width]
+    gate[3 * cols :] += part[:cols, width:]
     rows = []
     for e in range(4):
-        joined = im_j[2 + e, :, REACH * 2 * width : (REACH + 1) * 2 * width]
+        if e < 2:
+            joined = im_j[2 + e, :, REACH * 2 * width : (REACH + 1) * 2 * width]
+        else:
+            joined = jnp.concatenate([low_mid[0, e - 2], low_mid[1, e - 2]], axis=1)
         mixed = jnp.dot(joined, w_last[...], preferred_element_type=F32)
         source = acc if e < 2 else acc_in
         pre = source[(2 + e) * cols : (3 + e) * cols, 6 * width :]
-        half = e % 2
-        pre = pre + gate[(e // 2) * cols : (e // 2 + 1) * cols, half * width : (half + 1) * width]
+        pre = pre + gate[e * cols : (e + 1) * cols]
         hidden = (sigmoid(pre) * jnp.tanh(mixed)).astype(BF)
         if last:
             rows.append(hidden)
@@ -334,11 +411,12 @@
         for k in range(2):
             far[4 + k] = low_mid[1, k]
     else:
-        for t, source in enumerate((hid1, hid2, rows)):
-            for e in range(4):
-                predicted[t, own_row(e)] = lax.dot_general(
-                    w_out[...], source[e], (((1,), (1,)), ((), ())), preferred_element_type=F32
-                ).astype(BF)
+        for e in range(4):
+            frame = lax.dot_general(
+                w_out[...], rows[e], (((1,), (1,)), ((), ())), preferred_element_type=F32
+            )
+            for t, value in enumerate((pred1[e], pred2[e], frame.astype(BF))):
+                predicted[t, own_row(e)] = value
         for copy in copies:
             copy.wait()
 
@@ -399,7 +477,7 @@
     near0_in = lax.ppermute(near0, "row", beside)
     arrived0 = lax.ppermute(far0, "row", across)
     arrived = arrived0
-    hiddens = []
+    frames_out = []
     for moment in range(STEPS):
         first, last = moment == 0, moment == STEPS - 1
         outs = [((6 * cols, gates), F32), ((2, 2, cols, width), BF), rows(2, F32), rows(2, F32)]
@@ -425,13 +503,20 @@
         if first:
             w_x, w_h, w_m, w_o, w_last = done[4:]
         low_in = lax.ppermute(low_mid, "row", beside)
+        args, outs = (low_mid, w_o), [((4 * cols, width), F32)]
+        if not first:
+            args += (far, w_out)
+            outs.append(((4, width_in, cols), BF))
+        scratch = [pltpu.VMEM((4, cols + 16, LANES), F32), pltpu.VMEM((2, cols, 2 * TAPS * width), BF)]
+        edge = call(functools.partial(inner_kernel, first), outs, scratch, args, 10**9)
+        frames_out += edge[1:]
         args = (arrived, c_edge, m_edge)
         if not first:
             args += (done[4],)
-        args += (acc, low_mid, low_in, w_x, w_h, w_m, w_o, w_last)
+        args += (acc, low_mid, low_in, edge[0], w_x, w_h, w_m, w_o, w_last)
         far_outs = ()
         if last:
-            args += (hiddens[0], hiddens[1], c_mid, m_mid, w_out)
+            args += (frames_out[0], frames_out[1], c_mid, m_mid, w_out)
             outs = [((STEPS, 4, width_in, cols), BF), rows(4, F32), rows(4, F32)]
             far_outs = (1, 2)
         else:
@@ -440,9 +525,10 @@
             pltpu.VMEM((32, cols + 16, LANES), F32),
             pltpu.VMEM((4, cols, TAPS * width), BF),
             pltpu.VMEM((4 if first else 2, cols, TAPS * width), BF),
-            pltpu.VMEM((8, cols, 2 * TAPS * width), BF),
+            pltpu.VMEM((4, cols, 2 * TAPS * width), BF),
+            pltpu.VMEM((2, cols, 2 * TAPS * width), BF),
             pltpu.VMEM((4 * cols, gates), F32),
-            pltpu.VMEM((2 * cols, 2 * width), F32),
+            pltpu.VMEM((4 * cols, width), F32),
         ]
         if first:
             scratch.append(pltpu.VMEM((4, cols, LANES), BF))
@@ -456,7 +542,6 @@
             predicted, c_final, m_final = done
             return predicted.transpose(0, 1, 3, 2), c_final, m_final
         far, near, c_edge, m_edge = done
-        hiddens.append(far)
         near_in = lax.ppermute(near, "row", beside)
         arrived = lax.ppermute(far, "row", across)
 

time: 49.4 us -> 47.8 us (0.968)
  waiting for transfers between devices: 3.59 us -> 1.57 us
  starting transfers between devices: 14.2 us -> 14.7 us
    ppermute x3, waiting for transfers between devices: 2.95 us -> 1.15 us  [per_device(): low_in = lax.ppermute(low_mid, 'row', beside)]
    pallas_call x7 -> x10, Pallas kernels: 30.5 us -> 30.4 us  [call(): pl.pallas_call(body, out_shape=[jax.ShapeDtypeStruct(shape, kind) for sha...]
  transfers between devices with their start and end apart: 9 -> 9, of which waited for: 6 -> 5; matrix products, arithmetic and copies ran while one was open for 0% -> 0% of each run, Pallas kernels for 36% -> 40%
where the time goes in v1:
time: 47.8 us; the launch traced here: 47.6 us
  Pallas kernels  30.4 us (64%)
  starting transfers between devices  14.7 us (31%)
  waiting for transfers between devices  1.57 us (3%)
  between operations  0.9 us (2%)
    pallas_call x10, Pallas kernels, call(): pl.pallas_call(body, out_shape=[jax.ShapeDtypeStruct(shape, kind) for sha...  30.4 us
    ppermute x3, starting transfers between devices, per_device(): low_in = lax.ppermute(low_mid, 'row', beside)  10.8 us
    ppermute x2, starting transfers between devices, per_device(): arrived = lax.ppermute(far, 'row', across)  1.72 us
    ppermute x3, waiting for transfers between devices, per_device(): low_in = lax.ppermute(low_mid, 'row', beside)  1.15 us
    ppermute x2, starting transfers between devices, per_device(): near_in = lax.ppermute(near, 'row', beside)  0.96 us
  transfers between devices with their start and end apart: 9, of which 5 were waited for; matrix products, arithmetic and copies ran while one was open for 0% of the time, Pallas kernels for 40%

profile of v1, /device:TPU:0, one launch (start us, length us, event | category | flops | bytes accessed | tf_op | source)
XLA Modules:
  0.0 47.6 jit_solution(11730323444278581339)
XLA Ops:
  0.6 1.4 %shard_map.130 = (bf16[12,128,128]{2,1,0:T(8,128)(2,1)S(1)}, bf16[5,128,128]{2,1,0:T(8,128)(2,1)S(1)}, f32[4,128,128]{2,1,0:T(8,128)S(1)}, f32[4,128,128]{2,1,0:T(8,128)S(1)}) custom-call(bf16[4,128,128]{2,1,0:T(8,128)(2,1)} %h_hbm.1, f32[4,128,128]{2,1,0:T(8,128)} %c_hbm.1, f32[4,128,128]{2,1,0:T(8,128)} %m_hbm.1, bf16[3,4,16,128]{3,2,1,0:T(8,128)(2,1)} %bitcast.10, ...), custom_call_target="tpu_custom_call" | custom-call | flops 1000000 | bytes 4194304 | tf_op jit(solution)/shard_map/pallas_call | solution.py:429
  2.0 0.5 %collective-permute-start.1 = (bf16[5,128,128]{2,1,0:T(8,128)(2,1)S(1)}, bf16[5,128,128]{2,1,0:T(8,128)(2,1)S(1)}, u32[]{:S(2)}, u32[]{:S(2)}) collective-permute-start(bf16[5,128,128]{2,1,0:T(8,128)(2,1)S(1)} %get-tuple-element.44), channel_id=1, source_target_pairs={{0,1},{1,0},{2,3},{3,2},{4,5},{5,4},{6,7},{7,6},{8,9},{9,8},{10,11... | collective-permute-start | bytes 491528 | tf_op jit(solution)/shard_map/ppermute | solution.py:477
  2.6 0.7 %collective-permute-start = (bf16[12,128,128]{2,1,0:T(8,128)(2,1)S(1)}, bf16[12,128,128]{2,1,0:T(8,128)(2,1)S(1)}, u32[]{:S(2)}, u32[]{:S(2)}) collective-permute-start(bf16[12,128,128]{2,1,0:T(8,128)(2,1)S(1)} %get-tuple-element.41.refs_0_), channel_id=1, source_target_pairs={{1,2},{3,4},{5,6},{7,8},{9,10},{11,12},{13,14},{2,1},{4,3},{6,5},{... | collective-permute-start | bytes 1179656 | tf_op jit(solution)/shard_map/ppermute | solution.py:478
  3.2 0.3 collective-permute-done.1.refs_1_
  3.6 7.4 %shard_map.131 = (f32[768,896]{1,0:T(8,128)S(1)}, bf16[2,2,128,128]{3,2,1,0:T(8,128)(2,1)S(1)}, f32[2,128,128]{2,1,0:T(8,128)S(1)}, f32[2,128,128]{2,1,0:T(8,128...) custom-call(bf16[12,128,128]{2,1,0:T(8,128)(2,1)S(1)} %get-tuple-ele, ...), custom_call_target="tpu_custom_call" | custom-call | flops 4000000000 | bytes 4194304 | tf_op jit(solution)/shard_map/pallas_call | solution.py:429
  11.0 3.6 %collective-permute-start.2 = (bf16[2,2,128,128]{3,2,1,0:T(8,128)(2,1)S(1)}, bf16[2,2,128,128]{3,2,1,0:T(8,128)(2,1)S(1)}, u32[]{:S(2)}, u32[]{:S(2)}) collective-permute-start(bf16[2,2,128,128]{3,2,1,0:T(8,128)(2,1)S(1)} %get-tuple-element.46.refs_0_.refs_4_.refs_9_), channel_id=1, source_target_pairs={{0,1},{1,0},{2,3},{3,2},{4,5},{5,4},{6,7},{7,6},{8,9},{9,8},{10,11... | collective-permute-start | bytes 393224 | tf_op jit(solution)/shard_map/ppermute | solution.py:505
  14.6 0.6 %shard_map.132.refs_6_ = f32[512,128]{1,0:T(8,128)S(1)} custom-call(bf16[2,2,128,128]{3,2,1,0:T(8,128)(2,1)S(1)} %get-tuple-element.46.refs_0_.refs_4_.refs_9_, bf16[5,1280,128]{2,1,0:T(8,128)(2,1)S(1)} %get-tuple-element.47.refs_1_.refs_10_.refs_11_), custom_call_target="tpu_custom_call" | custom-call | flops 1000000000 | bytes 4194304 | tf_op jit(solution)/shard_map/pallas_call | solution.py:429
  15.2 0.4 collective-permute-done.2.refs_5_.refs_10_
  15.6 0.0 collective-permute-done.refs_0_.refs_2_
  15.6 3.4 %shard_map.133 = (bf16[6,128,128]{2,1,0:T(8,128)(2,1)S(1)}, bf16[2,128,128]{2,1,0:T(8,128)(2,1)S(1)}, f32[4,128,128]{2,1,0:T(8,128)S(1)}, f32[4,128,128]{2,1,0:T(8,128)S(1)}) custom-call(bf16[12,128,128]{2,1,0:T(8,128)(2,1)S(1)} %collective-permute-done.refs_0_.refs_2_, f32[4,128,128]{2,1,0:T(8,128)S(1)} %get-tuple-element.42.refs_2_.refs_1_, ...), custom_call_target="tpu_custom_call" | custom-call | flops 3000000000 | bytes 4194304 | tf_op jit(solution)/shard_map/pallas_call | solution.py:429
  18.9 0.5 %collective-permute-start.4 = (bf16[2,128,128]{2,1,0:T(8,128)(2,1)S(1)}, bf16[2,128,128]{2,1,0:T(8,128)(2,1)S(1)}, u32[]{:S(2)}, u32[]{:S(2)}) collective-permute-start(bf16[2,128,128]{2,1,0:T(8,128)(2,1)S(1)} %get-tuple-element.55), channel_id=1, source_target_pairs={{0,1},{1,0},{2,3},{3,2},{4,5},{5,4},{6,7},{7,6},{8,9},{9,8},{10,11... | collective-permute-start | bytes 196616 | tf_op jit(solution)/shard_map/ppermute | solution.py:545
  19.5 0.8 %collective-permute-start.3 = (bf16[6,128,128]{2,1,0:T(8,128)(2,1)S(1)}, bf16[6,128,128]{2,1,0:T(8,128)(2,1)S(1)}, u32[]{:S(2)}, u32[]{:S(2)}) collective-permute-start(bf16[6,128,128]{2,1,0:T(8,128)(2,1)S(1)} %get-tuple-element.52.refs_3_.refs_2_), channel_id=1, source_target_pairs={{1,2},{3,4},{5,6},{7,8},{9,10},{11,12},{13,14},{2,1},{4,3},{6,5},{... | collective-permute-start | bytes 589832 | tf_op jit(solution)/shard_map/ppermute | solution.py:546
  20.3 0.1 collective-permute-done.4.refs_4_
  20.4 0.0 copy-start
  20.4 4.9 %shard_map.134 = (f32[768,896]{1,0:T(8,128)S(1)}, bf16[2,2,128,128]{3,2,1,0:T(8,128)(2,1)S(1)}, f32[2,128,128]{2,1,0:T(8,128)S(1)}, f32[2,128,128]{2,1,0:T(8,128)S(1)}, bf16[10,128,128]{2,1,0:T(8,128)(2,1)S(1)}) custom-call(bf16[12,128,128]{2,1,0:T(8,128)(2,1)S(1)} %get-tuple-element.41.refs_0_, bf16[5,128,128]{2,1,0:T(8,128)(2,1)S(1)} %collective-permute-done.1.refs_1_, ...), custom_call_target="tpu_custom_call" | custom-call | flops 4000000000 | bytes 4194304 | tf_op jit(solution)/shard_map/pallas_call | solution.py:429
  25.3 3.8 %collective-permute-start.5 = (bf16[2,2,128,128]{3,2,1,0:T(8,128)(2,1)S(1)}, bf16[2,2,128,128]{3,2,1,0:T(8,128)(2,1)S(1)}, u32[]{:S(2)}, u32[]{:S(2)}) collective-permute-start(bf16[2,2,128,128]{3,2,1,0:T(8,128)(2,1)S(1)} %get-tuple-element.60.refs_0_.refs_5_.refs_9_), channel_id=1, source_target_pairs={{0,1},{1,0},{2,3},{3,2},{4,5},{5,4},{6,7},{7,6},{8,9},{9,8},{10,11... | collective-permute-start | bytes 393224 | tf_op jit(solution)/shard_map/ppermute | solution.py:505
  29.0 0.0 copy-done
  29.1 0.6 %shard_map.135 = (f32[512,128]{1,0:T(8,128)S(1)}, bf16[4,16,128]{2,1,0:T(8,128)(2,1)S(1)}) custom-call(bf16[2,2,128,128]{3,2,1,0:T(8,128)(2,1)S(1)} %get-tuple-element.60.refs_0_.refs_5_.refs_9_, bf16[5,1280,128]{2,1,0:T(8,128)(2,1)S(1)} %get-tuple-element.47.refs_1_.refs_10_.refs_11_, bf16[6,128,128]{2,1,0:T(8,128)(2,1)S(1)} %get-tuple-element.52.refs_3_.refs_2_, ...), custom_call_target="tpu_custom_call" | custom-call | flops 1000000000 | bytes 4194304 | tf_op jit(solution)/shard_map/pallas_call | solution.py:429
  29.7 0.0 collective-permute-done.3.refs_0_
  29.7 0.4 collective-permute-done.5.refs_6_.refs_10_
  30.0 2.7 %shard_map.136 = (bf16[6,128,128]{2,1,0:T(8,128)(2,1)S(1)}, bf16[2,128,128]{2,1,0:T(8,128)(2,1)S(1)}, f32[4,128,128]{2,1,0:T(8,128)S(1)}, f32[4,128,128]{2,1,0:T(8,128)S(1)}) custom-call(bf16[6,128,128]{2,1,0:T(8,128)(2,1)S(1)} %collective-permute-done.3.refs_0_, f32[4,128,128]{2,1,0:T(8,128)S(1)} %get-tuple-element.53.refs_5_.refs_1_, ...), custom_call_target="tpu_custom_call" | custom-call | flops 3000000000 | bytes 4194304 | tf_op jit(solution)/shard_map/pallas_call | solution.py:429
  32.7 0.4 collective-permute-start.7
  33.1 0.9 %collective-permute-start.6 = (bf16[6,128,128]{2,1,0:T(8,128)(2,1)S(1)}, bf16[6,128,128]{2,1,0:T(8,128)(2,1)S(1)}, u32[]{:S(2)}, u32[]{:S(2)}) collective-permute-start(bf16[6,128,128]{2,1,0:T(8,128)(2,1)S(1)} %get-tuple-element.62.refs_3_.refs_2_), channel_id=1, source_target_pairs={{1,2},{3,4},{5,6},{7,8},{9,10},{11,12},{13,14},{2,1},{4,3},{6,5},{... | collective-permute-start | bytes 589832 | tf_op jit(solution)/shard_map/ppermute | solution.py:546
  34.0 0.0 collective-permute-done.7.refs_4_
  34.0 4.9 %shard_map.137 = (f32[768,896]{1,0:T(8,128)S(1)}, bf16[2,2,128,128]{3,2,1,0:T(8,128)(2,1)S(1)}, f32[2,128,128]{2,1,0:T(8,128)S(1)}, f32[2,128,128]{2,1,0:T(8,128)S(1)}, bf16[10,128,128]{2,1,0:T(8,128)(2,1)S(1)}) custom-call(bf16[12,128,128]{2,1,0:T(8,128)(2,1)S(1)} %get-tuple-element.41.refs_0_, bf16[5,128,128]{2,1,0:T(8,128)(2,1)S(1)} %collective-permute-done.1.refs_1_, ...), custom_call_target="tpu_custom_call" | custom-call | flops 4000000000 | bytes 4194304 | tf_op jit(solution)/shard_map/pallas_call | solution.py:429
  38.9 3.4 %collective-permute-start.8 = (bf16[2,2,128,128]{3,2,1,0:T(8,128)(2,1)S(1)}, bf16[2,2,128,128]{3,2,1,0:T(8,128)(2,1)S(1)}, u32[]{:S(2)}, u32[]{:S(2)}) collective-permute-start(bf16[2,2,128,128]{3,2,1,0:T(8,128)(2,1)S(1)} %get-tuple-element.70.refs_0_.refs_5_), channel_id=1, source_target_pairs={{0,1},{1,0},{2,3},{3,2},{4,5},{5,4},{6,7},{7,6},{8,9},{9,8},{10,11... | collective-permute-start | bytes 393224 | tf_op jit(solution)/shard_map/ppermute | solution.py:505
  42.3 0.6 %shard_map.138 = (f32[512,128]{1,0:T(8,128)S(1)}, bf16[4,16,128]{2,1,0:T(8,128)(2,1)S(1)}) custom-call(bf16[2,2,128,128]{3,2,1,0:T(8,128)(2,1)S(1)} %get-tuple-element.70.refs_0_.refs_5_, bf16[5,1280,128]{2,1,0:T(8,128)(2,1)S(1)} %get-tuple-element.47.refs_1_.refs_10_.refs_11_, bf16[6,128,128]{2,1,0:T(8,128)(2,1)S(1)} %get-tuple-element.62.refs_3_.refs_2_, ...), custom_call_target="tpu_custom_call" | custom-call | flops 1000000000 | bytes 4194304 | tf_op jit(solution)/shard_map/pallas_call | solution.py:429
  43.0 0.0 collective-permute-done.6.refs_0_
  43.0 0.4 collective-permute-done.8.refs_6_
  43.3 4.0 %shard_map.139 = (bf16[3,4,16,128]{3,2,1,0:T(8,128)(2,1)}, f32[4,128,128]{2,1,0:T(8,128)}, f32[4,128,128]{2,1,0:T(8,128)}) custom-call(bf16[6,128,128]{2,1,0:T(8,128)(2,1)S(1)} %collective-permute-done.6.refs_0_, f32[4,128,128]{2,1,0:T(8,128)S(1)} %get-tuple-element.63.refs_5_.refs_1_, f32[4,128,128]{2,1,0:T(8,128)S(1)} %get-tuple-element.64.refs_6_.refs_2_, ...), custom_call_target="tpu_custom_call" | custom-call | flops 3000000000 | bytes 4194304 | tf_op jit(solution)/shard_map/pallas_call | solution.py:429
Async XLA Ops:
  2.0 1.5 %collective-permute-start.1 = (bf16[5,128,128]{2,1,0:T(8,128)(2,1)S(1)}, bf16[5,128,128]{2,1,0:T(8,128)(2,1)S(1)}, u32[]{:S(2)}, u32[]{:S(2)}) collective-permute-start(bf16[5,128,128]{2,1,0:T(8,128)(2,1)S(1)} %get-tuple-element.44), channel_id=1, source_target_pairs={{0,1},{1,0},{2,3},{3,2},{4,5},{5,4},{6,7},{7,6},{8,9},{9,8},{10,11... | collective-permute-start | bytes 491528 | tf_op jit(solution)/shard_map/ppermute | solution.py:477
  2.6 13.0 %collective-permute-start = (bf16[12,128,128]{2,1,0:T(8,128)(2,1)S(1)}, bf16[12,128,128]{2,1,0:T(8,128)(2,1)S(1)}, u32[]{:S(2)}, u32[]{:S(2)}) collective-permute-start(bf16[12,128,128]{2,1,0:T(8,128)(2,1)S(1)} %get-tuple-element.41.refs_0_), channel_id=1, source_target_pairs={{1,2},{3,4},{5,6},{7,8},{9,10},{11,12},{13,14},{2,1},{4,3},{6,5},{... | collective-permute-start | bytes 1179656 | tf_op jit(solution)/shard_map/ppermute | solution.py:478
  11.0 4.6 %collective-permute-start.2 = (bf16[2,2,128,128]{3,2,1,0:T(8,128)(2,1)S(1)}, bf16[2,2,128,128]{3,2,1,0:T(8,128)(2,1)S(1)}, u32[]{:S(2)}, u32[]{:S(2)}) collective-permute-start(bf16[2,2,128,128]{3,2,1,0:T(8,128)(2,1)S(1)} %get-tuple-element.46.refs_0_.refs_4_.refs_9_), channel_id=1, source_target_pairs={{0,1},{1,0},{2,3},{3,2},{4,5},{5,4},{6,7},{7,6},{8,9},{9,8},{10,11... | collective-permute-start | bytes 393224 | tf_op jit(solution)/shard_map/ppermute | solution.py:505
  18.9 1.4 %collective-permute-start.4 = (bf16[2,128,128]{2,1,0:T(8,128)(2,1)S(1)}, bf16[2,128,128]{2,1,0:T(8,128)(2,1)S(1)}, u32[]{:S(2)}, u32[]{:S(2)}) collective-permute-start(bf16[2,128,128]{2,1,0:T(8,128)(2,1)S(1)} %get-tuple-element.55), channel_id=1, source_target_pairs={{0,1},{1,0},{2,3},{3,2},{4,5},{5,4},{6,7},{7,6},{8,9},{9,8},{10,11... | collective-permute-start | bytes 196616 | tf_op jit(solution)/shard_map/ppermute | solution.py:545
  19.5 10.2 %collective-permute-start.3 = (bf16[6,128,128]{2,1,0:T(8,128)(2,1)S(1)}, bf16[6,128,128]{2,1,0:T(8,128)(2,1)S(1)}, u32[]{:S(2)}, u32[]{:S(2)}) collective-permute-start(bf16[6,128,128]{2,1,0:T(8,128)(2,1)S(1)} %get-tuple-element.52.refs_3_.refs_2_), channel_id=1, source_target_pairs={{1,2},{3,4},{5,6},{7,8},{9,10},{11,12},{13,14},{2,1},{4,3},{6,5},{... | collective-permute-start | bytes 589832 | tf_op jit(solution)/shard_map/ppermute | solution.py:546
  20.4 8.7 %copy-start = (bf16[128,16]{0,1:T(8,128)(2,1)S(1)}, bf16[128,16]{0,1:T(8,128)(2,1)}, u32[]{:S(2)}) copy-start(bf16[128,16]{0,1:T(8,128)(2,1)} %param.21) | copy-start | bytes 12292
  25.3 4.8 %collective-permute-start.5 = (bf16[2,2,128,128]{3,2,1,0:T(8,128)(2,1)S(1)}, bf16[2,2,128,128]{3,2,1,0:T(8,128)(2,1)S(1)}, u32[]{:S(2)}, u32[]{:S(2)}) collective-permute-start(bf16[2,2,128,128]{3,2,1,0:T(8,128)(2,1)S(1)} %get-tuple-element.60.refs_0_.refs_5_.refs_9_), channel_id=1, source_target_pairs={{0,1},{1,0},{2,3},{3,2},{4,5},{5,4},{6,7},{7,6},{8,9},{9,8},{10,11... | collective-permute-start | bytes 393224 | tf_op jit(solution)/shard_map/ppermute | solution.py:505
  32.7 1.3 %collective-permute-start.7 = (bf16[2,128,128]{2,1,0:T(8,128)(2,1)S(1)}, bf16[2,128,128]{2,1,0:T(8,128)(2,1)S(1)}, u32[]{:S(2)}, u32[]{:S(2)}) collective-permute-start(bf16[2,128,128]{2,1,0:T(8,128)(2,1)S(1)} %get-tuple-element.65), channel_id=1, source_target_pairs={{0,1},{1,0},{2,3},{3,2},{4,5},{5,4},{6,7},{7,6},{8,9},{9,8},{10,11... | collective-permute-start | bytes 196616 | tf_op jit(solution)/shard_map/ppermute | solution.py:545
  33.1 9.8 %collective-permute-start.6 = (bf16[6,128,128]{2,1,0:T(8,128)(2,1)S(1)}, bf16[6,128,128]{2,1,0:T(8,128)(2,1)S(1)}, u32[]{:S(2)}, u32[]{:S(2)}) collective-permute-start(bf16[6,128,128]{2,1,0:T(8,128)(2,1)S(1)} %get-tuple-element.62.refs_3_.refs_2_), channel_id=1, source_target_pairs={{1,2},{3,4},{5,6},{7,8},{9,10},{11,12},{13,14},{2,1},{4,3},{6,5},{... | collective-permute-start | bytes 589832 | tf_op jit(solution)/shard_map/ppermute | solution.py:546
  38.9 4.4 %collective-permute-start.8 = (bf16[2,2,128,128]{3,2,1,0:T(8,128)(2,1)S(1)}, bf16[2,2,128,128]{3,2,1,0:T(8,128)(2,1)S(1)}, u32[]{:S(2)}, u32[]{:S(2)}) collective-permute-start(bf16[2,2,128,128]{3,2,1,0:T(8,128)(2,1)S(1)} %get-tuple-element.70.refs_0_.refs_5_), channel_id=1, source_target_pairs={{0,1},{1,0},{2,3},{3,2},{4,5},{5,4},{6,7},{7,6},{8,9},{9,8},{10,11... | collective-permute-start | bytes 393224 | tf_op jit(solution)/shard_map/ppermute | solution.py:505

commit v2 on v1

--- a/solution.py
+++ b/solution.py
@@ -27,6 +27,12 @@
 def tap_row(p):
     odd = odd_device()
     return p + odd * (TAPS - 1 - 2 * p)
+
+
+def partner_exists():
+    place = lax.axis_index("row")
+    inside = jnp.logical_and(place > 0, place < lax.axis_size("row") - 1)
+    return jnp.where(inside, 1.0, 0.0).astype(F32)
 
 
 def sigmoid(x):
@@ -244,8 +250,10 @@
     for k in range(2):
         put_frame(pad, slot + 4 + k, im_x, 8 + k - (4 if first else 0), near0[4], 1 - k, moment, width_in)
     if not first:
+        keep = partner_exists()
         for k in range(4):
-            put_frame(pad, slot + 6 + k, im_x, 3 - k, arrived0[10 + k // 2], k % 2, moment, width_in)
+            packed = arrived0[10 + k // 2].astype(F32) * keep
+            put_frame(pad, slot + 6 + k, im_x, 3 - k, packed, k % 2, moment, width_in)
     x_base = 4 if first else 0
     if first:
         for e in range(4):
@@ -337,21 +345,23 @@
     width = arrived.shape[2]
     m_rows = 4 if first else 2
     clear_pad(pad)
+    keep = partner_exists()
+
+    def arrived_row(k):
+        return arrived[k].astype(F32) * keep
+
     for k in range(4):
-        put_row(pad, k, im_h, 3 - k, arrived[k], width, 0)
+        put_row(pad, k, im_h, 3 - k, arrived_row(k), width, 0)
     for k in range(m_rows):
-        put_row(pad, 4 + k, im_m, 3 - k if first else 1 - k, arrived[4 + k], width, 0)
+        put_row(pad, 4 + k, im_m, 3 - k if first else 1 - k, arrived_row(4 + k), width, 0)
     if first:
         for k in range(4):
-            put_frame(pad, 24 + k, im_x, 3 - k, arrived[10 + k // 2], k % 2, moment, width_in)
+            put_frame(pad, 24 + k, im_x, 3 - k, arrived_row(10 + k // 2), k % 2, moment, width_in)
     for k in range(2):
         for part in range(2):
             put_row(pad, 12 + 2 * k + part, im_i, k, low_in[part, 1 - k], 2 * width, part * width)
     add_taps(acc, acc_in, im_h, im_x, 0, 0, w_h, w_x, H_PARTS, 0, 4, 4)
     add_taps(acc, acc_in, im_m, im_x, 0, 0, w_m, w_x, M_PARTS, 0, m_rows, 4)
-    place = lax.axis_index("row")
-    inside = jnp.logical_and(place > 0, place < lax.axis_size("row") - 1)
-    keep = jnp.where(inside, 1.0, 0.0).astype(F32)
     copies = []
     for r in range(4):
         if first and r < 2:
@@ -441,7 +451,10 @@
     cols, width = h_init.shape[1], h_init.shape[2]
     width_in = frames.shape[3]
     count = lax.axis_size("row")
-    across = [(i, i + 1) for i in range(1, count - 1, 2)]
+    groups = lax.axis_size("groups")
+    across = [(g * count + i, g * count + i + 1) for g in range(groups) for i in range(1, count - 1, 2)]
+    if groups % 2 == 0:
+        across += [(g * count + i, (g + 1) * count + i) for g in range(0, groups, 2) for i in (0, count - 1)]
     across += [(j, i) for i, j in across]
     beside = [(i, i ^ 1) for i in range(count)]
     w_x = w_x.reshape(TAPS, TAPS * width_in, -1)
@@ -475,7 +488,7 @@
         far_args=range(5),
     )
     near0_in = lax.ppermute(near0, "row", beside)
-    arrived0 = lax.ppermute(far0, "row", across)
+    arrived0 = lax.ppermute(far0, ("groups", "row"), across)
     arrived = arrived0
     frames_out = []
     for moment in range(STEPS):
@@ -543,7 +556,7 @@
             return predicted.transpose(0, 1, 3, 2), c_final, m_final
         far, near, c_edge, m_edge = done
         near_in = lax.ppermute(near, "row", beside)
-        arrived = lax.ppermute(far, "row", across)
+        arrived = lax.ppermute(far, ("groups", "row"), across)
 
 
 def solution(mesh):

time: 47.8 us -> 41.8 us (0.87)
  starting transfers between devices: 14.7 us -> 8.74 us
    ppermute x3, starting transfers between devices: 10.8 us -> 1.9 us  [per_device(): low_in = lax.ppermute(low_mid, 'row', beside)]
    ppermute x3, starting transfers between devices: 2.4 us -> 5.54 us  [the longest x2 2.98 us: per_device(): arrived = lax.ppermute(far, ('groups', 'row'), across)]
  transfers between devices with their start and end apart: 9 -> 9, of which waited for: 5 -> 3; matrix products, arithmetic and copies ran while one was open for 0% -> 0% of each run, Pallas kernels for 40% -> 46%
where the time goes in v2:
time: 41.8 us; the launch traced here: 41.6 us
  Pallas kernels  30.6 us (73%)
  starting transfers between devices  8.74 us (21%)
  waiting for transfers between devices  1.38 us (3%)
  between operations  0.85 us (2%)
    pallas_call x10, Pallas kernels, call(): pl.pallas_call(body, out_shape=[jax.ShapeDtypeStruct(shape, kind) for sha...  30.6 us
    ppermute x2, starting transfers between devices, per_device(): arrived = lax.ppermute(far, ('groups', 'row'), across)  2.98 us
    ppermute x1, starting transfers between devices, per_device(): arrived0 = lax.ppermute(far0, ('groups', 'row'), across)  2.56 us
    ppermute x3, starting transfers between devices, per_device(): low_in = lax.ppermute(low_mid, 'row', beside)  1.9 us
    ppermute x3, waiting for transfers between devices, per_device(): low_in = lax.ppermute(low_mid, 'row', beside)  1.37 us
  transfers between devices with their start and end apart: 9, of which 3 were waited for; matrix products, arithmetic and copies ran while one was open for 0% of the time, Pallas kernels for 46%

profile of v2, /device:TPU:0, one launch (start us, length us, event | category | flops | bytes accessed | tf_op | source)
XLA Modules:
  0.0 41.6 jit_solution(10814980698145594761)
XLA Ops:
  0.6 1.4 %shard_map.130 = (bf16[12,128,128]{2,1,0:T(8,128)(2,1)S(1)}, bf16[5,128,128]{2,1,0:T(8,128)(2,1)S(1)}, f32[4,128,128]{2,1,0:T(8,128)S(1)}, f32[4,128,128]{2,1,0:T(8,128)S(1)}) custom-call(bf16[4,128,128]{2,1,0:T(8,128)(2,1)} %h_hbm.1, f32[4,128,128]{2,1,0:T(8,128)} %c_hbm.1, f32[4,128,128]{2,1,0:T(8,128)} %m_hbm.1, bf16[3,4,16,128]{3,2,1,0:T(8,128)(2,1)} %bitcast.10, ...), custom_call_target="tpu_custom_call" | custom-call | flops 1000000 | bytes 4194304 | tf_op jit(solution)/shard_map/pallas_call | solution.py:439
  2.0 0.5 %collective-permute-start.1 = (bf16[5,128,128]{2,1,0:T(8,128)(2,1)S(1)}, bf16[5,128,128]{2,1,0:T(8,128)(2,1)S(1)}, u32[]{:S(2)}, u32[]{:S(2)}) collective-permute-start(bf16[5,128,128]{2,1,0:T(8,128)(2,1)S(1)} %get-tuple-element.44), channel_id=1, source_target_pairs={{0,1},{1,0},{2,3},{3,2},{4,5},{5,4},{6,7},{7,6},{8,9},{9,8},{10,11... | collective-permute-start | bytes 491528 | tf_op jit(solution)/shard_map/ppermute | solution.py:490
  2.6 2.6 %collective-permute-start = (bf16[12,128,128]{2,1,0:T(8,128)(2,1)S(1)}, bf16[12,128,128]{2,1,0:T(8,128)(2,1)S(1)}, u32[]{:S(2)}, u32[]{:S(2)}) collective-permute-start(bf16[12,128,128]{2,1,0:T(8,128)(2,1)S(1)} %get-tuple-element.41.refs_0_), channel_id=1, source_target_pairs={{1,2},{3,4},{5,6},{7,8},{9,10},{11,12},{13,14},{17,18},{19,20},{21... | collective-permute-start | bytes 1179656 | tf_op jit(solution)/shard_map/ppermute | solution.py:491
  5.1 0.0 collective-permute-done.1.refs_1_
  5.1 7.4 %shard_map.131 = (f32[768,896]{1,0:T(8,128)S(1)}, bf16[2,2,128,128]{3,2,1,0:T(8,128)(2,1)S(1)}, f32[2,128,128]{2,1,0:T(8,128)S(1)}, f32[2,128,128]{2,1,0:T(8,128...) custom-call(bf16[12,128,128]{2,1,0:T(8,128)(2,1)S(1)} %get-tuple-ele, ...), custom_call_target="tpu_custom_call" | custom-call | flops 4000000000 | bytes 4194304 | tf_op jit(solution)/shard_map/pallas_call | solution.py:439
  12.5 0.2 collective-permute-start.2
  12.7 0.6 %shard_map.132.refs_6_ = f32[512,128]{1,0:T(8,128)S(1)} custom-call(bf16[2,2,128,128]{3,2,1,0:T(8,128)(2,1)S(1)} %get-tuple-element.46.refs_0_.refs_4_.refs_9_, bf16[5,1280,128]{2,1,0:T(8,128)(2,1)S(1)} %get-tuple-element.47.refs_1_.refs_10_.refs_11_), custom_call_target="tpu_custom_call" | custom-call | flops 1000000000 | bytes 4194304 | tf_op jit(solution)/shard_map/pallas_call | solution.py:439
  13.3 0.6 %collective-permute-done.2.refs_5_.refs_10_ = bf16[2,2,128,128]{3,2,1,0:T(8,128)(2,1)S(1)} collective-permute-done((bf16[2,2,128,128]{3,2,1,0:T(8,128)(2,1)S(1)}, bf16[2,2,128,128]{3,2,1,0:T(8,128)(2,1)S(1)}, u32[]{:S(2)}, u32[]{:S(2)}) %collective-permute-start.2) | collective-permute-done | bytes 131104 | tf_op jit(solution)/shard_map/ppermute | solution.py:518
  13.9 0.0 collective-permute-done.refs_0_.refs_2_
  13.9 3.3 %shard_map.133 = (bf16[6,128,128]{2,1,0:T(8,128)(2,1)S(1)}, bf16[2,128,128]{2,1,0:T(8,128)(2,1)S(1)}, f32[4,128,128]{2,1,0:T(8,128)S(1)}, f32[4,128,128]{2,1,0:T(8,128)S(1)}) custom-call(bf16[12,128,128]{2,1,0:T(8,128)(2,1)S(1)} %collective-permute-done.refs_0_.refs_2_, f32[4,128,128]{2,1,0:T(8,128)S(1)} %get-tuple-element.42.refs_2_.refs_1_, ...), custom_call_target="tpu_custom_call" | custom-call | flops 3000000000 | bytes 4194304 | tf_op jit(solution)/shard_map/pallas_call | solution.py:439
  17.3 0.3 collective-permute-start.4
  17.6 1.5 %collective-permute-start.3 = (bf16[6,128,128]{2,1,0:T(8,128)(2,1)S(1)}, bf16[6,128,128]{2,1,0:T(8,128)(2,1)S(1)}, u32[]{:S(2)}, u32[]{:S(2)}) collective-permute-start(bf16[6,128,128]{2,1,0:T(8,128)(2,1)S(1)} %get-tuple-element.52.refs_3_.refs_2_), channel_id=1, source_target_pairs={{1,2},{3,4},{5,6},{7,8},{9,10},{11,12},{13,14},{17,18},{19,20},{21... | collective-permute-start | bytes 589832 | tf_op jit(solution)/shard_map/ppermute | solution.py:559
  19.1 0.0 collective-permute-done.4.refs_4_
  19.1 0.0 copy-start
  19.1 4.9 %shard_map.134 = (f32[768,896]{1,0:T(8,128)S(1)}, bf16[2,2,128,128]{3,2,1,0:T(8,128)(2,1)S(1)}, f32[2,128,128]{2,1,0:T(8,128)S(1)}, f32[2,128,128]{2,1,0:T(8,128)S(1)}, bf16[10,128,128]{2,1,0:T(8,128)(2,1)S(1)}) custom-call(bf16[12,128,128]{2,1,0:T(8,128)(2,1)S(1)} %get-tuple-element.41.refs_0_, bf16[5,128,128]{2,1,0:T(8,128)(2,1)S(1)} %collective-permute-done.1.refs_1_, ...), custom_call_target="tpu_custom_call" | custom-call | flops 4000000000 | bytes 4194304 | tf_op jit(solution)/shard_map/pallas_call | solution.py:439
  24.0 1.1 %collective-permute-start.5 = (bf16[2,2,128,128]{3,2,1,0:T(8,128)(2,1)S(1)}, bf16[2,2,128,128]{3,2,1,0:T(8,128)(2,1)S(1)}, u32[]{:S(2)}, u32[]{:S(2)}) collective-permute-start(bf16[2,2,128,128]{3,2,1,0:T(8,128)(2,1)S(1)} %get-tuple-element.60.refs_0_.refs_5_.refs_9_), channel_id=1, source_target_pairs={{0,1},{1,0},{2,3},{3,2},{4,5},{5,4},{6,7},{7,6},{8,9},{9,8},{10,11... | collective-permute-start | bytes 393224 | tf_op jit(solution)/shard_map/ppermute | solution.py:518
  25.2 0.0 copy-done
  25.2 0.6 %shard_map.135 = (f32[512,128]{1,0:T(8,128)S(1)}, bf16[4,16,128]{2,1,0:T(8,128)(2,1)S(1)}) custom-call(bf16[2,2,128,128]{3,2,1,0:T(8,128)(2,1)S(1)} %get-tuple-element.60.refs_0_.refs_5_.refs_9_, bf16[5,1280,128]{2,1,0:T(8,128)(2,1)S(1)} %get-tuple-element.47.refs_1_.refs_10_.refs_11_, bf16[6,128,128]{2,1,0:T(8,128)(2,1)S(1)} %get-tuple-element.52.refs_3_.refs_2_, ...), custom_call_target="tpu_custom_call" | custom-call | flops 1000000000 | bytes 4194304 | tf_op jit(solution)/shard_map/pallas_call | solution.py:439
  25.8 0.0 collective-permute-done.3.refs_0_
  25.8 0.4 collective-permute-done.5.refs_6_.refs_10_
  26.1 2.8 %shard_map.136 = (bf16[6,128,128]{2,1,0:T(8,128)(2,1)S(1)}, bf16[2,128,128]{2,1,0:T(8,128)(2,1)S(1)}, f32[4,128,128]{2,1,0:T(8,128)S(1)}, f32[4,128,128]{2,1,0:T(8,128)S(1)}) custom-call(bf16[6,128,128]{2,1,0:T(8,128)(2,1)S(1)} %collective-permute-done.3.refs_0_, f32[4,128,128]{2,1,0:T(8,128)S(1)} %get-tuple-element.53.refs_5_.refs_1_, ...), custom_call_target="tpu_custom_call" | custom-call | flops 3000000000 | bytes 4194304 | tf_op jit(solution)/shard_map/pallas_call | solution.py:439
  29.0 0.4 %collective-permute-start.7 = (bf16[2,128,128]{2,1,0:T(8,128)(2,1)S(1)}, bf16[2,128,128]{2,1,0:T(8,128)(2,1)S(1)}, u32[]{:S(2)}, u32[]{:S(2)}) collective-permute-start(bf16[2,128,128]{2,1,0:T(8,128)(2,1)S(1)} %get-tuple-element.65), channel_id=1, source_target_pairs={{0,1},{1,0},{2,3},{3,2},{4,5},{5,4},{6,7},{7,6},{8,9},{9,8},{10,11... | collective-permute-start | bytes 196616 | tf_op jit(solution)/shard_map/ppermute | solution.py:558
  29.4 1.5 %collective-permute-start.6 = (bf16[6,128,128]{2,1,0:T(8,128)(2,1)S(1)}, bf16[6,128,128]{2,1,0:T(8,128)(2,1)S(1)}, u32[]{:S(2)}, u32[]{:S(2)}) collective-permute-start(bf16[6,128,128]{2,1,0:T(8,128)(2,1)S(1)} %get-tuple-element.62.refs_3_.refs_2_), channel_id=1, source_target_pairs={{1,2},{3,4},{5,6},{7,8},{9,10},{11,12},{13,14},{17,18},{19,20},{21... | collective-permute-start | bytes 589832 | tf_op jit(solution)/shard_map/ppermute | solution.py:559
  30.9 0.0 collective-permute-done.7.refs_4_
  30.9 4.9 %shard_map.137 = (f32[768,896]{1,0:T(8,128)S(1)}, bf16[2,2,128,128]{3,2,1,0:T(8,128)(2,1)S(1)}, f32[2,128,128]{2,1,0:T(8,128)S(1)}, f32[2,128,128]{2,1,0:T(8,128)S(1)}, bf16[10,128,128]{2,1,0:T(8,128)(2,1)S(1)}) custom-call(bf16[12,128,128]{2,1,0:T(8,128)(2,1)S(1)} %get-tuple-element.41.refs_0_, bf16[5,128,128]{2,1,0:T(8,128)(2,1)S(1)} %collective-permute-done.1.refs_1_, ...), custom_call_target="tpu_custom_call" | custom-call | flops 4000000000 | bytes 4194304 | tf_op jit(solution)/shard_map/pallas_call | solution.py:439
  35.8 0.6 %collective-permute-start.8 = (bf16[2,2,128,128]{3,2,1,0:T(8,128)(2,1)S(1)}, bf16[2,2,128,128]{3,2,1,0:T(8,128)(2,1)S(1)}, u32[]{:S(2)}, u32[]{:S(2)}) collective-permute-start(bf16[2,2,128,128]{3,2,1,0:T(8,128)(2,1)S(1)} %get-tuple-element.70.refs_0_.refs_5_), channel_id=1, source_target_pairs={{0,1},{1,0},{2,3},{3,2},{4,5},{5,4},{6,7},{7,6},{8,9},{9,8},{10,11... | collective-permute-start | bytes 393224 | tf_op jit(solution)/shard_map/ppermute | solution.py:518
  36.4 0.6 %shard_map.138 = (f32[512,128]{1,0:T(8,128)S(1)}, bf16[4,16,128]{2,1,0:T(8,128)(2,1)S(1)}) custom-call(bf16[2,2,128,128]{3,2,1,0:T(8,128)(2,1)S(1)} %get-tuple-element.70.refs_0_.refs_5_, bf16[5,1280,128]{2,1,0:T(8,128)(2,1)S(1)} %get-tuple-element.47.refs_1_.refs_10_.refs_11_, bf16[6,128,128]{2,1,0:T(8,128)(2,1)S(1)} %get-tuple-element.62.refs_3_.refs_2_, ...), custom_call_target="tpu_custom_call" | custom-call | flops 1000000000 | bytes 4194304 | tf_op jit(solution)/shard_map/pallas_call | solution.py:439
  37.0 0.0 collective-permute-done.6.refs_0_
  37.0 0.4 collective-permute-done.8.refs_6_
  37.4 4.0 %shard_map.139 = (bf16[3,4,16,128]{3,2,1,0:T(8,128)(2,1)}, f32[4,128,128]{2,1,0:T(8,128)}, f32[4,128,128]{2,1,0:T(8,128)}) custom-call(bf16[6,128,128]{2,1,0:T(8,128)(2,1)S(1)} %collective-permute-done.6.refs_0_, f32[4,128,128]{2,1,0:T(8,128)S(1)} %get-tuple-element.63.refs_5_.refs_1_, f32[4,128,128]{2,1,0:T(8,128)S(1)} %get-tuple-element.64.refs_6_.refs_2_, ...), custom_call_target="tpu_custom_call" | custom-call | flops 3000000000 | bytes 4194304 | tf_op jit(solution)/shard_map/pallas_call | solution.py:439
Async XLA Ops:
  2.0 3.1 %collective-permute-start.1 = (bf16[5,128,128]{2,1,0:T(8,128)(2,1)S(1)}, bf16[5,128,128]{2,1,0:T(8,128)(2,1)S(1)}, u32[]{:S(2)}, u32[]{:S(2)}) collective-permute-start(bf16[5,128,128]{2,1,0:T(8,128)(2,1)S(1)} %get-tuple-element.44), channel_id=1, source_target_pairs={{0,1},{1,0},{2,3},{3,2},{4,5},{5,4},{6,7},{7,6},{8,9},{9,8},{10,11... | collective-permute-start | bytes 491528 | tf_op jit(solution)/shard_map/ppermute | solution.py:490
  2.6 11.4 %collective-permute-start = (bf16[12,128,128]{2,1,0:T(8,128)(2,1)S(1)}, bf16[12,128,128]{2,1,0:T(8,128)(2,1)S(1)}, u32[]{:S(2)}, u32[]{:S(2)}) collective-permute-start(bf16[12,128,128]{2,1,0:T(8,128)(2,1)S(1)} %get-tuple-element.41.refs_0_), channel_id=1, source_target_pairs={{1,2},{3,4},{5,6},{7,8},{9,10},{11,12},{13,14},{17,18},{19,20},{21... | collective-permute-start | bytes 1179656 | tf_op jit(solution)/shard_map/ppermute | solution.py:491
  12.5 1.4 %collective-permute-start.2 = (bf16[2,2,128,128]{3,2,1,0:T(8,128)(2,1)S(1)}, bf16[2,2,128,128]{3,2,1,0:T(8,128)(2,1)S(1)}, u32[]{:S(2)}, u32[]{:S(2)}) collective-permute-start(bf16[2,2,128,128]{3,2,1,0:T(8,128)(2,1)S(1)} %get-tuple-element.46.refs_0_.refs_4_.refs_9_), channel_id=1, source_target_pairs={{0,1},{1,0},{2,3},{3,2},{4,5},{5,4},{6,7},{7,6},{8,9},{9,8},{10,11... | collective-permute-start | bytes 393224 | tf_op jit(solution)/shard_map/ppermute | solution.py:518
  17.3 1.8 %collective-permute-start.4 = (bf16[2,128,128]{2,1,0:T(8,128)(2,1)S(1)}, bf16[2,128,128]{2,1,0:T(8,128)(2,1)S(1)}, u32[]{:S(2)}, u32[]{:S(2)}) collective-permute-start(bf16[2,128,128]{2,1,0:T(8,128)(2,1)S(1)} %get-tuple-element.55), channel_id=1, source_target_pairs={{0,1},{1,0},{2,3},{3,2},{4,5},{5,4},{6,7},{7,6},{8,9},{9,8},{10,11... | collective-permute-start | bytes 196616 | tf_op jit(solution)/shard_map/ppermute | solution.py:558
  17.6 8.1 %collective-permute-start.3 = (bf16[6,128,128]{2,1,0:T(8,128)(2,1)S(1)}, bf16[6,128,128]{2,1,0:T(8,128)(2,1)S(1)}, u32[]{:S(2)}, u32[]{:S(2)}) collective-permute-start(bf16[6,128,128]{2,1,0:T(8,128)(2,1)S(1)} %get-tuple-element.52.refs_3_.refs_2_), channel_id=1, source_target_pairs={{1,2},{3,4},{5,6},{7,8},{9,10},{11,12},{13,14},{17,18},{19,20},{21... | collective-permute-start | bytes 589832 | tf_op jit(solution)/shard_map/ppermute | solution.py:559
  19.1 6.0 %copy-start = (bf16[128,16]{0,1:T(8,128)(2,1)S(1)}, bf16[128,16]{0,1:T(8,128)(2,1)}, u32[]{:S(2)}) copy-start(bf16[128,16]{0,1:T(8,128)(2,1)} %param.21) | copy-start | bytes 12292
  24.0 2.1 %collective-permute-start.5 = (bf16[2,2,128,128]{3,2,1,0:T(8,128)(2,1)S(1)}, bf16[2,2,128,128]{3,2,1,0:T(8,128)(2,1)S(1)}, u32[]{:S(2)}, u32[]{:S(2)}) collective-permute-start(bf16[2,2,128,128]{3,2,1,0:T(8,128)(2,1)S(1)} %get-tuple-element.60.refs_0_.refs_5_.refs_9_), channel_id=1, source_target_pairs={{0,1},{1,0},{2,3},{3,2},{4,5},{5,4},{6,7},{7,6},{8,9},{9,8},{10,11... | collective-permute-start | bytes 393224 | tf_op jit(solution)/shard_map/ppermute | solution.py:518
  29.0 1.9 %collective-permute-start.7 = (bf16[2,128,128]{2,1,0:T(8,128)(2,1)S(1)}, bf16[2,128,128]{2,1,0:T(8,128)(2,1)S(1)}, u32[]{:S(2)}, u32[]{:S(2)}) collective-permute-start(bf16[2,128,128]{2,1,0:T(8,128)(2,1)S(1)} %get-tuple-element.65), channel_id=1, source_target_pairs={{0,1},{1,0},{2,3},{3,2},{4,5},{5,4},{6,7},{7,6},{8,9},{9,8},{10,11... | collective-permute-start | bytes 196616 | tf_op jit(solution)/shard_map/ppermute | solution.py:558
  29.4 7.6 %collective-permute-start.6 = (bf16[6,128,128]{2,1,0:T(8,128)(2,1)S(1)}, bf16[6,128,128]{2,1,0:T(8,128)(2,1)S(1)}, u32[]{:S(2)}, u32[]{:S(2)}) collective-permute-start(bf16[6,128,128]{2,1,0:T(8,128)(2,1)S(1)} %get-tuple-element.62.refs_3_.refs_2_), channel_id=1, source_target_pairs={{1,2},{3,4},{5,6},{7,8},{9,10},{11,12},{13,14},{17,18},{19,20},{21... | collective-permute-start | bytes 589832 | tf_op jit(solution)/shard_map/ppermute | solution.py:559
  35.8 1.5 %collective-permute-start.8 = (bf16[2,2,128,128]{3,2,1,0:T(8,128)(2,1)S(1)}, bf16[2,2,128,128]{3,2,1,0:T(8,128)(2,1)S(1)}, u32[]{:S(2)}, u32[]{:S(2)}) collective-permute-start(bf16[2,2,128,128]{3,2,1,0:T(8,128)(2,1)S(1)} %get-tuple-element.70.refs_0_.refs_5_), channel_id=1, source_target_pairs={{0,1},{1,0},{2,3},{3,2},{4,5},{5,4},{6,7},{7,6},{8,9},{9,8},{10,11... | collective-permute-start | bytes 393224 | tf_op jit(solution)/shard_map/ppermute | solution.py:518

commit v3 on v2

v3 whole, which is shorter than its diff:
```python
import functools

import jax
import jax.numpy as jnp
from jax import lax
from jax.experimental import pallas as pl
from jax.experimental.pallas import tpu as pltpu
from jax.sharding import PartitionSpec as P

STEPS = 3
TAPS = 5
REACH = 2
LANES = 128
BF = jnp.bfloat16
F32 = jnp.float32


def odd_device():
    return lax.rem(lax.axis_index("row"), 2)


def own_row(e):
    odd = odd_device()
    return e + odd * (3 - 2 * e)


def tap_row(p):
    odd = odd_device()
    return p + odd * (TAPS - 1 - 2 * p)


def partner_exists():
    place = lax.axis_index("row")
    inside = jnp.logical_and(place > 0, place < lax.axis_size("row") - 1)
    return jnp.where(inside, 1.0, 0.0).astype(F32)


def sigmoid(x):
    return 0.5 * jnp.tanh(0.5 * x) + 0.5


def clear_pad(pad):
    rows, height = pad.shape[0], pad.shape[1]
    pad[:, :8] = jnp.zeros((rows, 8, LANES), F32)
    pad[:, height - 8 :] = jnp.zeros((rows, 8, LANES), F32)


def put_row(pad, slot, im, row, value, stride, lane0):
    cols = value.shape[0]
    pad[slot, 8 : 8 + cols] = value.astype(F32)
    for s in range(TAPS):
        im[row, :, s * stride + lane0 : s * stride + lane0 + LANES] = pad[
            slot, 6 + s : 6 + s + cols
        ].astype(BF)


def frame_lane(e, moment, width):
    return width * (2 * e + moment if moment < 2 else e)


def put_frame(pad, slot, im, row, packed, e, moment, width):
    cols = packed.shape[0]
    group = frame_lane(e, moment, width)
    value = packed.astype(F32)
    if group:
        value = pltpu.roll(value, LANES - group, 1)
    lane = lax.broadcasted_iota(jnp.int32, (cols, LANES), 1)
    value = jnp.where(lane < width, value, 0.0)
    pad[slot, 8 : 8 + cols] = value
    total = pad[slot, 6 : 6 + cols]
    for s in range(1, TAPS):
        total = total + pltpu.roll(pad[slot, 6 + s : 6 + s + cols], width * s, 1)
    im[row] = total.astype(BF)


H_PARTS = ((0, 256, ((0, 256),)), (256, 512, ((256, 384), (768, 896))))
M_PARTS = ((0, 256, ((384, 640),)), (256, 384, ((640, 768),)))


def add_last_tap(acc, im, im_x, row0, weight, w_x, parts, rows):
    cols = im.shape[1]
    p = TAPS - 1
    lhs = jnp.concatenate(
        [
            im[p - row0 : p - row0 + rows].reshape(rows * cols, im.shape[2]),
            im_x[p : p + rows].reshape(rows * cols, LANES),
        ],
        axis=1,
    )
    tap = tap_row(p)
    for c0, c1, x_cols in parts:
        rest = frame_rows(w_x, tap, x_cols)
        rhs = jnp.concatenate([weight[tap, :, c0:c1]] + rest, axis=0)
        acc[: rows * cols, c0:c1] += jnp.dot(lhs, rhs, preferred_element_type=F32)


def add_taps(acc, base, im, im_x, row0, x_row0, weight, w_x, parts, low, high, rows):
    cols = im.shape[1]
    order = range(TAPS) if low == 0 else range(TAPS - 1, -1, -1)
    begun = False
    for p in order:
        r0, r1 = max(0, low - p), min(rows, high - p)
        if low and p == TAPS - 1:
            r0 = TAPS - 1
            acc[: r0 * cols, :] = jnp.zeros((r0 * cols, acc.shape[1]), F32)
        if r0 >= r1:
            continue
        count = (r1 - r0) * cols
        j = r0 + p
        lhs = jnp.concatenate(
            [
                im[j - row0 : j - row0 + r1 - r0].reshape(count, im.shape[2]),
                im_x[j - x_row0 : j - x_row0 + r1 - r0].reshape(count, LANES),
            ],
            axis=1,
        )
        tap = tap_row(p)
        here = slice(r0 * cols, r1 * cols)
        for c0, c1, x_cols in parts:
            frame = jnp.concatenate([w_x[tap, :, x0:x1] for x0, x1 in x_cols], axis=1)
            fill = jnp.zeros((LANES - w_x.shape[1], c1 - c0), BF)
            rhs = jnp.concatenate([weight[tap, :, c0:c1], frame, fill], axis=0)
            part = jnp.dot(lhs, rhs, preferred_element_type=F32)
            if begun:
                acc[here, c0:c1] += part
            elif base is None:
                acc[here, c0:c1] = part
            else:
                acc[here, c0:c1] = base[here, c0:c1] + part
        begun = True


def frame_rows(w_x, tap, spans):
    values = jnp.concatenate([w_x[tap, :, a:b] for a, b in spans], axis=1)
    fill = jnp.zeros((LANES - values.shape[0], values.shape[1]), BF)
    return [values, fill]


def add_memory_pairs(acc, im, im_x, row0, x_row0, weight, w_x, low, rows):
    cols = im.shape[1]
    width = weight.shape[2] // 3
    gates = 3 * width

    def lhs_of(j0, j1):
        count = (j1 - j0) * cols
        return jnp.concatenate(
            [
                im[j0 - row0 : j1 - row0].reshape(count, im.shape[2]),
                im_x[j0 - x_row0 : j1 - x_row0].reshape(count, LANES),
            ],
            axis=1,
        )

    def rhs_of(p, a, b):
        tap = tap_row(p)
        rest = frame_rows(w_x, tap, ((gates + a, gates + b),))
        return jnp.concatenate([weight[tap, :, a:b]] + rest, axis=0)

    def product(lhs, rhs):
        return jnp.dot(lhs, rhs, preferred_element_type=F32)

    p = TAPS - 1
    r0 = 4
    acc[: r0 * cols, :] = jnp.zeros((r0 * cols, gates), F32)
    lhs = lhs_of(r0 + p, rows + p)
    for a, b in ((0, 2 * width), (2 * width, gates)):
        acc[r0 * cols : rows * cols, a:b] = product(lhs, rhs_of(p, a, b))
    for p in (2, 0):
        q = p + 1
        rp, rq = max(0, low - p), max(0, low - q)
        part = product(lhs_of(rp + p, rows + p), rhs_of(p, 0, 2 * width))
        acc[rp * cols : rows * cols, : 2 * width] += part
        part = product(lhs_of(rq + q, rows + q), rhs_of(q, width, gates))
        acc[rq * cols : rows * cols, width:gates] += part
        j0 = min(rp + p, rq + q)
        rhs = jnp.concatenate([rhs_of(p, 2 * width, gates), rhs_of(q, 0, width)], axis=1)
        part = product(lhs_of(j0, rows + q), rhs)
        a = (rp + p - j0) * cols
        acc[rp * cols : rows * cols, 2 * width : gates] += part[a : a + (rows - rp) * cols, :width]
        a = (rq + q - j0) * cols
        acc[rq * cols : rows * cols, :width] += part[a : a + (rows - rq) * cols, width:]


def new_state(gates, m_gates, width, c_old, m_old):
    def c_gate(k):
        return gates[:, k * width : (k + 1) * width]

    def m_gate(k):
        return m_gates[:, k * width : (k + 1) * width]

    c_new = sigmoid(c_gate(1) + 1.0) * c_old + sigmoid(c_gate(0)) * jnp.tanh(c_gate(2))
    m_new = sigmoid(m_gate(1) + 1.0) * m_old + sigmoid(m_gate(0)) * jnp.tanh(m_gate(2))
    return c_new, m_new


def pack_kernel(h_hbm, c_hbm, m_hbm, f_hbm, cov_hbm, far, near, c_own, m_own, later, f_ref, cov_ref, sems):
    cols = far.shape[1]
    width = f_ref.shape[2]
    copies = []
    for e in range(4):
        row = own_row(e)
        copies.append((m_hbm.at[row], m_own.at[e]))
        copies.append((c_hbm.at[row], c_own.at[e]))
        copies.append((h_hbm.at[row], far.at[e]))
        if e >= 2:
            copies.append((h_hbm.at[row], near.at[e - 2]))
    copies.append((f_hbm, f_ref))
    copies.append((cov_hbm, cov_ref))
    copies = [pltpu.make_async_copy(a, b, sems.at[i]) for i, (a, b) in enumerate(copies)]
    for copy in copies:
        copy.start()
    for copy in copies:
        copy.wait()
    for e in range(4):
        m = m_own[e].astype(BF)
        far[4 + e] = m
        if e < 2:
            far[8 + e] = c_own[e].astype(BF)
        else:
            near[e] = m
    for unit, moments in enumerate(((0, 1), (2,))):
        parts = []
        for e in range(4):
            row = own_row(e)
            cover = cov_ref[pl.ds(row, 1), :].astype(F32)
            for moment in moments:
                parts.append(f_ref[moment, row].astype(F32) * cover)
        if len(parts) * width < LANES:
            parts.append(jnp.zeros((LANES - len(parts) * width, cols), F32))
        packed = jnp.concatenate(parts, axis=0).T.astype(BF)
        near[4 + unit] = packed
        if unit == 0:
            far[10] = packed
        else:
            later[0] = packed


def memory_kernel(moment, width_in, *refs):
    first = moment == 0
    if first:
        far0, near0, x_hbm, m_hbm, h_hbm, o_hbm, last_hbm, acc, im_x, im, w_x, w_m, w_h, w_o, w_last, pad, sems = refs
        copies = [
            pltpu.make_async_copy(a, b, sems.at[i])
            for i, (a, b) in enumerate(
                ((x_hbm, w_x), (m_hbm, w_m), (h_hbm, w_h), (o_hbm, w_o), (last_hbm, w_last))
            )
        ]
        for copy in copies:
            copy.start()
    else:
        own_x, near0, arrived, m_edge, low_mid, low_in, w_x, w_m, acc, im_x, im, pad = refs
    cols = near0.shape[1]
    width = near0.shape[2]
    clear_pad(pad)
    own_frame = far0[10] if first else own_x[own_x.shape[0] - 1]
    low = 4 if first else 2
    for e in range(4):
        put_row(pad, e, im, e, far0[4 + e] if first else m_edge[e].astype(BF), width, 0)
    for k in range(2):
        if first:
            put_row(pad, 4 + k, im, 4 + k, near0[3 - k], width, 0)
        else:
            put_row(pad, 4 + k, im, 4 + k, low_mid[1, k], width, 0)
            put_row(pad, 6 + k, im, 6 + k, low_in[1, 1 - k], width, 0)
    for e in range(4):
        put_frame(pad, 8 + e, im_x, 4 + e, own_frame, e, moment, width_in)
    for k in range(2):
        put_frame(pad, 12 + k, im_x, 8 + k, near0[4 + moment // 2], 3 - k, moment, width_in)
    if first:
        copies[0].wait()
        copies[1].wait()
    else:
        keep = partner_exists()
        packed = arrived[arrived.shape[0] - 1].astype(F32) * keep
        for k in range(4):
            put_frame(pad, 14 + k, im_x, 3 - k, packed, k, moment, width_in)
    add_memory_pairs(acc, im, im_x, low, 0, w_m, w_x, low, 6)
    if first:
        for copy in copies[2:]:
            copy.wait()


def hidden_kernel(first, *refs):
    hid, hid_in, c_old, m_old, acc_m, im_x, w_x, w_h, acc, low_ref, c_out, m_out, im, pad = refs
    cols = hid.shape[1]
    width = hid.shape[2]
    clear_pad(pad)
    for e in range(4):
        put_row(pad, e, im, e, hid[e], width, 0)
    for k in range(2):
        put_row(pad, 4 + k, im, 4 + k, hid_in[1 - k], width, 0)
    add_taps(acc, None, im, im_x, 4, 0, w_h, w_x, H_PARTS, 4, 10, 6)
    for k in range(2):
        here = slice((4 + k) * cols, (5 + k) * cols)
        old = 2 + k if first else k
        c_new, m_new = new_state(acc[here, :], acc_m[here, :], width, c_old[old], m_old[old])
        c_out[k] = c_new
        m_out[k] = m_new
        low_ref[0, k] = c_new.astype(BF)
        low_ref[1, k] = m_new.astype(BF)


def two_taps(lhs, w_o, p, q):
    rhs = jnp.concatenate([w_o[tap_row(p)], w_o[tap_row(q)]], axis=1)
    return jnp.dot(lhs, rhs, preferred_element_type=F32)


def predict(target, hidden, w_out):
    for e in range(4):
        target[e] = lax.dot_general(
            w_out[...], hidden[e], (((1,), (1,)), ((), ())), preferred_element_type=F32
        ).astype(BF)


def inner_kernel(first, *refs):
    acc_old, acc_m_old, im_h, im_m, im_x, w_x, w_h, w_m, low_mid, w_o = refs[:10]
    if first:
        acc, acc_m, gate, pad, im = refs[10:]
    else:
        hid, w_out, acc, acc_m, gate, predicted, pad, im = refs[10:]
    cols, width = low_mid.shape[2], low_mid.shape[3]
    clear_pad(pad)
    for k in range(2):
        for part in range(2):
            put_row(pad, 2 * k + part, im, k, low_mid[part, k], 2 * width, part * width)
    lhs = im[...].reshape(2 * cols, im.shape[2])
    part = two_taps(lhs, w_o, 4, 3)
    gate[:cols] = part[:cols, :width]
    gate[cols : 2 * cols] = part[cols:, :width] + part[:cols, width:]
    more = two_taps(lhs, w_o, 2, 1)
    gate[2 * cols : 3 * cols] = part[cols:, width:] + more[:cols, :width]
    gate[3 * cols :] = more[cols:, :width] + more[:cols, width:]
    add_last_tap(acc, im_h, im_x, 4, w_h, w_x, H_PARTS, 4)
    add_last_tap(acc_m, im_m, im_x, 4 if first else 2, w_m, w_x, M_PARTS, 4)
    if not first:
        predict(predicted, hid, w_out)


def final_kernel(moment, last, width_in, *refs):
    first = moment == 0
    refs = list(refs)
    if first:
        arrived, c_edge, m_edge, later = refs[:4]
        refs = refs[4:]
    else:
        arrived, c_edge, m_edge, im_x = refs[:4]
        refs = refs[4:]
    acc_in, acc_m_in, low_mid, low_in, gate_in, w_x, w_h, w_m, w_o, w_last = refs[:10]
    refs = refs[10:]
    if last:
        pred1, pred2, c_mid, m_mid, w_out, predicted, c_fin, m_fin = refs[:8]
        refs = refs[8:]
    else:
        far, near, c_out, m_out = refs[:4]
        refs = refs[4:]
    pad, im_h, im_m, im_j, im_i, acc, acc_m, gate = refs[:8]
    if first:
        im_x = refs[8]
    if last:
        keep_c, keep_m, frame, sems = refs[8:]
    cols = arrived.shape[1]
    width = arrived.shape[2]
    m_rows = 4 if first else 2
    clear_pad(pad)
    keep = partner_exists()

    def arrived_row(k):
        return arrived[k].astype(F32) * keep

    for k in range(4):
        put_row(pad, k, im_h, 3 - k, arrived_row(k), width, 0)
    for k in range(m_rows):
        put_row(pad, 4 + k, im_m, 3 - k if first else 1 - k, arrived_row(4 + k), width, 0)
    if first:
        for k in range(4):
            put_frame(pad, 24 + k, im_x, 3 - k, arrived_row(10), k, moment, width_in)
    for k in range(2):
        for part in range(2):
            put_row(pad, 12 + 2 * k + part, im_i, k, low_in[part, 1 - k], 2 * width, part * width)
    add_taps(acc, acc_in, im_h, im_x, 0, 0, w_h, w_x, H_PARTS, 0, 4, 4)
    add_taps(acc_m, acc_m_in, im_m, im_x, 0, 0, w_m, w_x, M_PARTS, 0, m_rows, 4)
    copies = []
    for r in range(4):
        if first and r < 2:
            c_old, m_old = arrived[9 - r].astype(F32), arrived[5 - r].astype(F32)
        elif first:
            c_old, m_old = c_edge[r - 2], m_edge[r - 2]
        else:
            c_old, m_old = c_edge[r], m_edge[r]
        here = slice(r * cols, (r + 1) * cols)
        gates = acc[here, :]
        m_gates = (acc_m if r < m_rows else acc_m_in)[here, :]
        c_new, m_new = new_state(gates, m_gates, width, c_old, m_old)
        if r < 2:
            c_new, m_new = c_new * keep, m_new * keep
        put_row(pad, 16 + 2 * r, im_j, r, c_new.astype(BF), 2 * width, 0)
        put_row(pad, 17 + 2 * r, im_j, r, m_new.astype(BF), 2 * width, width)
        if not last:
            c_out[r] = c_new
            m_out[r] = m_new
        elif r >= 2:
            keep_c[r - 2] = c_new
            keep_m[r - 2] = m_new
    if last:
        for e in range(4):
            sources = (keep_c.at[e], keep_m.at[e]) if e < 2 else (c_mid.at[e - 2], m_mid.at[e - 2])
            for n, (source, target) in enumerate(zip(sources, (c_fin, m_fin))):
                copies.append(pltpu.make_async_copy(source, target.at[own_row(e)], sems.at[2 * e + n]))
            for t, source in enumerate((pred1, pred2)):
                target = predicted.at[t, own_row(e)]
                copies.append(pltpu.make_async_copy(source.at[e], target, sems.at[8 + 2 * e + t]))
        for copy in copies:
            copy.start()
    part = two_taps(im_j[0:4].reshape(4 * cols, -1), w_o, 0, 1)
    gate[...] = part[:, :width] + gate_in[...]
    gate[: 3 * cols] += part[cols:, width:]
    part = two_taps(im_j[2:4].reshape(2 * cols, -1), w_o, 2, 3)
    gate[: 2 * cols] += part[:, :width]
    gate[:cols] += part[cols:, width:]
    part = two_taps(im_i[...].reshape(2 * cols, -1), w_o, 4, 3)
    gate[2 * cols :] += part[:, :width]
    gate[3 * cols :] += part[:cols, width:]
    rows = []
    for e in range(4):
        if e < 2:
            joined = im_j[2 + e, :, REACH * 2 * width : (REACH + 1) * 2 * width]
        else:
            joined = jnp.concatenate([low_mid[0, e - 2], low_mid[1, e - 2]], axis=1)
        mixed = jnp.dot(joined, w_last[...], preferred_element_type=F32)
        source = acc if e < 2 else acc_in
        pre = source[(2 + e) * cols : (3 + e) * cols, 3 * width :]
        pre = pre + gate[e * cols : (e + 1) * cols]
        hidden = (sigmoid(pre) * jnp.tanh(mixed)).astype(BF)
        if last:
            rows.append(hidden)
        else:
            far[e] = hidden
            if e >= 2:
                near[e - 2] = hidden
    if not last:
        for k in range(2):
            far[4 + k] = low_mid[1, k]
        if first:
            far[6] = later[0]
    else:
        for e in range(4):
            frame[e] = lax.dot_general(
                w_out[...], rows[e], (((1,), (1,)), ((), ())), preferred_element_type=F32
            ).astype(BF)
            copies.append(pltpu.make_async_copy(frame.at[e], predicted.at[2, own_row(e)], sems.at[16 + e]))
            copies[-1].start()
        for copy in copies:
            copy.wait()


VMEM = pl.BlockSpec(memory_space=pltpu.VMEM)
HBM = pl.BlockSpec(memory_space=pltpu.HBM)


def call(body, outs, scratch, args, flops, far_args=(), far_outs=(), aliases=None):
    return pl.pallas_call(
        body,
        out_shape=[jax.ShapeDtypeStruct(shape, kind) for shape, kind in outs],
        in_specs=[HBM if i in far_args else VMEM for i in range(len(args))],
        out_specs=[HBM if i in far_outs else VMEM for i in range(len(outs))],
        scratch_shapes=scratch,
        input_output_aliases=aliases or {},
        compiler_params=pltpu.CompilerParams(vmem_limit_bytes=16 * 2**20),
        cost_estimate=pl.CostEstimate(flops=flops, bytes_accessed=4 * 2**20, transcendentals=0),
    )(*args)


def per_device(frames, coverage, h_init, c_init, m_init, w_x, w_h, w_m, w_o, w_last, w_out):
    cols, width = h_init.shape[1], h_init.shape[2]
    width_in = frames.shape[3]
    count = lax.axis_size("row")
    groups = lax.axis_size("groups")
    across = [(g * count + i, g * count + i + 1) for g in range(groups) for i in range(1, count - 1, 2)]
    if groups % 2 == 0:
        across += [(g * count + i, (g + 1) * count + i) for g in range(0, groups, 2) for i in (0, count - 1)]
    across += [(j, i) for i, j in across]
    beside = [(i, i ^ 1) for i in range(count)]
    w_x = w_x.reshape(TAPS, TAPS * width_in, -1)
    w_h = w_h.reshape(TAPS, TAPS * width, -1)
    w_m = w_m.reshape(TAPS, TAPS * width, -1)
    w_o = w_o.reshape(TAPS, TAPS * 2 * width, -1)
    w_out = w_out.T

    def rows(n, kind=BF):
        return ((n, cols, width), kind)

    def shaped(w):
        return (w.shape, w.dtype)

    flat = frames.transpose(0, 1, 3, 2)
    h_init, c_init, m_init, flat, coverage, w_x, w_h, w_m, w_o, w_last = (
        pltpu.with_memory_space_constraint(x, pltpu.HBM)
        for x in (h_init, c_init, m_init, flat, coverage, w_x, w_h, w_m, w_o, w_last)
    )
    far0, near0, c_edge, m_edge, later = call(
        pack_kernel,
        [rows(11), rows(6), rows(4, F32), rows(4, F32), rows(1)],
        [
            pltpu.VMEM(flat.shape, flat.dtype),
            pltpu.VMEM(coverage.shape, coverage.dtype),
            pltpu.SemaphoreType.DMA((16,)),
        ],
        (h_init, c_init, m_init, flat, coverage),
        10**6,
        far_args=range(5),
    )
    near0_in = lax.ppermute(near0, "row", beside)
    arrived = lax.ppermute(far0, ("groups", "row"), across)
    frames_out = []
    for moment in range(STEPS):
        first, last = moment == 0, moment == STEPS - 1
        outs = [
            ((6 * cols, 3 * width), F32),
            ((10, cols, LANES), BF),
            ((6 if first else 8, cols, TAPS * width), BF),
        ]
        scratch = [pltpu.VMEM((18, cols + 16, LANES), F32)]
        if first:
            args = (far0, near0_in, w_x, w_m, w_h, w_o, w_last)
            outs += [shaped(w) for w in args[2:]]
            scratch.append(pltpu.SemaphoreType.DMA((5,)))
            far_args = range(2, 7)
        else:
            args = (later if last else far0, near0_in, frames_in, m_edge, low_mid, low_in, w_x, w_m)
            far_args = ()
        done = call(
            functools.partial(memory_kernel, moment, width_in), outs, scratch, args, 2 * 10**9, far_args
        )
        acc_m, im_x, im_m = done[:3]
        if first:
            w_x, w_m, w_h, w_o, w_last = done[3:]
            args = (far0, near0_in, c_edge, m_edge)
        else:
            args = (far, near_in, c_mid, m_mid)
        outs = [((6 * cols, 4 * width), F32), ((2, 2, cols, width), BF), rows(2, F32), rows(2, F32)]
        outs.append(((6, cols, TAPS * width), BF))
        scratch = [pltpu.VMEM((6, cols + 16, LANES), F32)]
        acc, low_mid, c_mid, m_mid, im_h = call(
            functools.partial(hidden_kernel, first), outs, scratch, args + (acc_m, im_x, w_x, w_h), 2 * 10**9
        )
        low_in = lax.ppermute(low_mid, "row", beside)
        args = (acc, acc_m, im_h, im_m, im_x, w_x, w_h, w_m, low_mid, w_o)
        outs = [((6 * cols, 4 * width), F32), ((6 * cols, 3 * width), F32), ((4 * cols, width), F32)]
        if not first:
            args += (far, w_out)
            outs.append(((4, width_in, cols), BF))
        scratch = [pltpu.VMEM((4, cols + 16, LANES), F32), pltpu.VMEM((2, cols, 2 * TAPS * width), BF)]
        edge = call(functools.partial(inner_kernel, first), outs, scratch, args, 10**9, aliases={0: 0, 1: 1})
        acc, acc_m = edge[:2]
        frames_out += edge[3:]
        frames_in = arrived
        args = (arrived, c_edge, m_edge)
        if first:
            args += (later,)
        if not first:
            args += (im_x,)
        args += (acc, acc_m, low_mid, low_in, edge[2], w_x, w_h, w_m, w_o, w_last)
        far_outs = ()
        if last:
            args += (frames_out[0], frames_out[1], c_mid, m_mid, w_out)
            outs = [((STEPS, 4, width_in, cols), BF), rows(4, F32), rows(4, F32)]
            far_outs = (0, 1, 2)
        else:
            outs = [rows(7 if first else 6), rows(2), rows(4, F32), rows(4, F32)]
        scratch = [
            pltpu.VMEM((32, cols + 16, LANES), F32),
            pltpu.VMEM((4, cols, TAPS * width), BF),
            pltpu.VMEM((4 if first else 2, cols, TAPS * width), BF),
            pltpu.VMEM((4, cols, 2 * TAPS * width), BF),
            pltpu.VMEM((2, cols, 2 * TAPS * width), BF),
            pltpu.VMEM((4 * cols, 4 * width), F32),
            pltpu.VMEM((4 * cols, 3 * width), F32),
            pltpu.VMEM((4 * cols, width), F32),
        ]
        if first:
            scratch.append(pltpu.VMEM((4, cols, LANES), BF))
        if last:
            scratch += [
                pltpu.VMEM(*rows(2, F32)),
                pltpu.VMEM(*rows(2, F32)),
                pltpu.VMEM((4, width_in, cols), BF),
                pltpu.SemaphoreType.DMA((20,)),
            ]
        done = call(
            functools.partial(final_kernel, moment, last, width_in),
            outs, scratch, args, 3 * 10**9, far_outs=far_outs,
        )
        if last:
            predicted, c_final, m_final = done
            return predicted.transpose(0, 1, 3, 2), c_final, m_final
        far, near, c_edge, m_edge = done
        near_in = lax.ppermute(near, "row", beside)
        arrived = lax.ppermute(far, ("groups", "row"), across)


def solution(mesh):
    placed = (
        P("groups", "row", None, None),
        P("row", "groups"),
        P("row", "groups", None),
        P("row", "groups", None),
        P("row", "groups", None),
        P(),
        P(),
        P(),
        P(),
        P(),
        P(),
    )
    return jax.shard_map(
        per_device,
        mesh=mesh,
        in_specs=placed,
        out_specs=(
            P("groups", "row", None, None),
            P("row", "groups", None),
            P("row", "groups", None),
        ),
        check_vma=False,
    )
```

time: 41.8 us -> 39.6 us (0.947)
  waiting for transfers between devices: 1.38 us -> 0.02 us
  Pallas kernels: 30.6 us -> 29.6 us
    ppermute x3, waiting for transfers between devices: 1.37 us -> 0.01 us  [per_device(): low_in = lax.ppermute(low_mid, 'row', beside)]
    pallas_call x10 -> x13, Pallas kernels: 30.6 us -> 29.6 us  [call(): pl.pallas_call(body, out_shape=[jax.ShapeDtypeStruct(shape, kind) for sha...]
  transfers between devices with their start and end apart: 9 -> 9, of which waited for: 3 -> 0; matrix products, arithmetic and copies ran while one was open for 0% -> 0% of each run, Pallas kernels for 46% -> 47%
where the time goes in v3:
time: 39.6 us; the launch traced here: 39.5 us
  Pallas kernels  29.6 us (75%)
  starting transfers between devices  8.96 us (23%)
  between operations  0.91 us (2%)
    pallas_call x13, Pallas kernels, call(): pl.pallas_call(body, out_shape=[jax.ShapeDtypeStruct(shape, kind) for sha...  29.6 us
    ppermute x2, starting transfers between devices, per_device(): arrived = lax.ppermute(far, ('groups', 'row'), across)  3.04 us
    ppermute x1, starting transfers between devices, per_device(): arrived = lax.ppermute(far0, ('groups', 'row'), across)  2.56 us
    ppermute x3, starting transfers between devices, per_device(): low_in = lax.ppermute(low_mid, 'row', beside)  2.08 us
  transfers between devices with their start and end apart: 9, of which 0 were waited for; matrix products, arithmetic and copies ran while one was open for 0% of the time, Pallas kernels for 47%

profile of v3, /device:TPU:0, one launch (start us, length us, event | category | flops | bytes accessed | tf_op | source)
XLA Modules:
  0.0 39.5 jit_solution(1787601065045266736)
XLA Ops:
  0.6 1.4 %shard_map.130 = (bf16[11,128,128]{2,1,0:T(8,128)(2,1)S(1)}, bf16[6,128,128]{2,1,0:T(8,128)(2,1)S(1)}, f32[4,128,128]{2,1,0:T(8,128)S(1)}, f32[4,128,128]{2,1,0:T(8,128)S(1)}, bf16[1,128,128]{2,1,0:T(8,128)(2,1)S(1)}) custom-call(bf16[4,128,128]{2,1,0:T(8,128)(2,1)} %h_hbm.1, f32[4,128,128]{2,1,0:T(8,128)} %c_hbm.1, f32[4,128,128]{2,1,0:T(8,128)} %m_hbm.1, ...), custom_call_target="tpu_custom_call" | custom-call | flops 1000000 | bytes 4194304 | tf_op jit(solution)/shard_map/pallas_call | solution.py:461
  2.0 0.5 %collective-permute-start.1 = (bf16[6,128,128]{2,1,0:T(8,128)(2,1)S(1)}, bf16[6,128,128]{2,1,0:T(8,128)(2,1)S(1)}, u32[]{:S(2)}, u32[]{:S(2)}) collective-permute-start(bf16[6,128,128]{2,1,0:T(8,128)(2,1)S(1)} %get-tuple-element.63), channel_id=1, source_target_pairs={{0,1},{1,0},{2,3},{3,2},{4,5},{5,4},{6,7},{7,6},{8,9},{9,8},{10,11... | collective-permute-start | bytes 589832 | tf_op jit(solution)/shard_map/ppermute | solution.py:512
  2.6 2.6 %collective-permute-start = (bf16[11,128,128]{2,1,0:T(8,128)(2,1)S(1)}, bf16[11,128,128]{2,1,0:T(8,128)(2,1)S(1)}, u32[]{:S(2)}, u32[]{:S(2)}) collective-permute-start(bf16[11,128,128]{2,1,0:T(8,128)(2,1)S(1)} %get-tuple-element.59.refs_0_), channel_id=1, source_target_pairs={{1,2},{3,4},{5,6},{7,8},{9,10},{11,12},{13,14},{17,18},{19,20},{21... | collective-permute-start | bytes 1081352 | tf_op jit(solution)/shard_map/ppermute | solution.py:513
  5.1 0.0 collective-permute-done.1.refs_1_
  5.1 4.2 %shard_map.131 = (f32[768,384]{1,0:T(8,128)S(1)}, bf16[10,128,128]{2,1,0:T(8,128)(2,1)S(1)}, bf16[6,128,640]{2,1,0:T(8,128)(2,1)S(1)}, bf16[5,80,896]{2,1,0:T(8,...) custom-call(bf16[11,128,128]{2,1,0:T(8,128)(2,1)S(1)} %get-tuple-ele, ...), custom_call_target="tpu_custom_call" | custom-call | flops 2000000000 | bytes 4194304 | tf_op jit(solution)/shard_map/pallas_call | solution.py:461
  9.3 1.9 %shard_map.132 = (f32[768,512]{1,0:T(8,128)S(1)}, bf16[2,2,128,128]{3,2,1,0:T(8,128)(2,1)S(1)}, f32[2,128,128]{2,1,0:T(8,128)S(1)}, f32[2,128,128]{2,1,0:T(8,128)S(1)}, bf16[6,128,640]{2,1,0:T(8,128)(2,1)S(1)}) custom-call(bf16[11,128,128]{2,1,0:T(8,128)(2,1)S(1)} %get-tuple-element.59.refs_0_, bf16[6,128,128]{2,1,0:T(8,128)(2,1)S(1)} %collective-permute-done.1.refs_1_, ...), custom_call_target="tpu_custom_call" | custom-call | flops 2000000000 | bytes 4194304 | tf_op jit(solution)/shard_map/pallas_call | solution.py:461
  11.3 0.2 collective-permute-start.2
  11.5 1.4 %shard_map.133 = (f32[768,512]{1,0:T(8,128)S(1)}, f32[768,384]{1,0:T(8,128)S(1)}, f32[512,128]{1,0:T(8,128)S(1)}) custom-call(f32[768,512]{1,0:T(8,128)S(1)} %get-tuple-element.68.refs_0_, f32[768,384]{1,0:T(8,128)S(1)} %get-tuple-element.64.refs_4_.refs_1_, ...), custom_call_target="tpu_custom_call", output_to_operand_aliasing={{0}: (0, {}), {1}: (1, {})} | custom-call | flops 1000000000 | bytes 4194304 | tf_op jit(solution)/shard_map/pallas_call | solution.py:461
  12.9 0.0 collective-permute-done.2.refs_7_.refs_5_
  12.9 0.0 collective-permute-done.refs_0_.refs_2_
  12.9 3.2 %shard_map.134 = (bf16[7,128,128]{2,1,0:T(8,128)(2,1)S(1)}, bf16[2,128,128]{2,1,0:T(8,128)(2,1)S(1)}, f32[4,128,128]{2,1,0:T(8,128)S(1)}, f32[4,128,128]{2,1,0:T(8,128)S(1)}) custom-call(bf16[11,128,128]{2,1,0:T(8,128)(2,1)S(1)} %collective-permute-done.refs_0_.refs_2_, f32[4,128,128]{2,1,0:T(8,128)S(1)} %get-tuple-element.60.refs_2_.refs_1_, ...), custom_call_target="tpu_custom_call" | custom-call | flops 3000000000 | bytes 4194304 | tf_op jit(solution)/shard_map/pallas_call | solution.py:461
  16.1 0.7 %collective-permute-start.4 = (bf16[2,128,128]{2,1,0:T(8,128)(2,1)S(1)}, bf16[2,128,128]{2,1,0:T(8,128)(2,1)S(1)}, u32[]{:S(2)}, u32[]{:S(2)}) collective-permute-start(bf16[2,128,128]{2,1,0:T(8,128)(2,1)S(1)} %get-tuple-element.82), channel_id=1, source_target_pairs={{0,1},{1,0},{2,3},{3,2},{4,5},{5,4},{6,7},{7,6},{8,9},{9,8},{10,11... | collective-permute-start | bytes 196616 | tf_op jit(solution)/shard_map/ppermute | solution.py:597
  16.8 1.5 %collective-permute-start.3 = (bf16[7,128,128]{2,1,0:T(8,128)(2,1)S(1)}, bf16[7,128,128]{2,1,0:T(8,128)(2,1)S(1)}, u32[]{:S(2)}, u32[]{:S(2)}) collective-permute-start(bf16[7,128,128]{2,1,0:T(8,128)(2,1)S(1)} %get-tuple-element.78.refs_0_.refs_10_), channel_id=1, source_target_pairs={{1,2},{3,4},{5,6},{7,8},{9,10},{11,12},{13,14},{17,18},{19,20},{21... | collective-permute-start | bytes 688136 | tf_op jit(solution)/shard_map/ppermute | solution.py:598
  18.3 2.3 %shard_map.135 = (f32[768,384]{1,0:T(8,128)S(1)}, bf16[10,128,128]{2,1,0:T(8,128)(2,1)S(1)}, bf16[8,128,640]{2,1,0:T(8,128)(2,1)S(1)}) custom-call(bf16[11,128,128]{2,1,0:T(8,128)(2,1)S(1)} %get-tuple-element.59.refs_0_, bf16[6,128,128]{2,1,0:T(8,128)(2,1)S(1)} %collective-permute-done.1.refs_1_, ...), custom_call_target="tpu_custom_call" | custom-call | flops 2000000000 | bytes 4194304 | tf_op jit(solution)/shard_map/pallas_call | solution.py:461
  20.6 0.0 collective-permute-done.4.refs_1_
  20.6 0.0 copy-start
  20.6 1.9 %shard_map.136 = (f32[768,512]{1,0:T(8,128)S(1)}, bf16[2,2,128,128]{3,2,1,0:T(8,128)(2,1)S(1)}, f32[2,128,128]{2,1,0:T(8,128)S(1)}, f32[2,128,128]{2,1,0:T(8,128)S(1)}, bf16[6,128,640]{2,1,0:T(8,128)(2,1)S(1)}) custom-call(bf16[7,128,128]{2,1,0:T(8,128)(2,1)S(1)} %get-tuple-element.78.refs_0_.refs_10_, ...), custom_call_target="tpu_custom_call" | custom-call | flops 2000000000 | bytes 4194304 | tf_op jit(solution)/shard_map/pallas_call | solution.py:461
  22.5 1.1 %collective-permute-start.5 = (bf16[2,2,128,128]{3,2,1,0:T(8,128)(2,1)S(1)}, bf16[2,2,128,128]{3,2,1,0:T(8,128)(2,1)S(1)}, u32[]{:S(2)}, u32[]{:S(2)}) collective-permute-start(bf16[2,2,128,128]{3,2,1,0:T(8,128)(2,1)S(1)} %get-tuple-element.89.refs_8_.refs_6_.refs_4_), channel_id=1, source_target_pairs={{0,1},{1,0},{2,3},{3,2},{4,5},{5,4},{6,7},{7,6},{8,9},{9,8},{10,11... | collective-permute-start | bytes 393224 | tf_op jit(solution)/shard_map/ppermute | solution.py:546
  23.7 0.0 copy-done
  23.7 1.4 %shard_map.137 = (f32[768,512]{1,0:T(8,128)S(1)}, f32[768,384]{1,0:T(8,128)S(1)}, f32[512,128]{1,0:T(8,128)S(1)}, bf16[4,16,128]{2,1,0:T(8,128)(2,1)S(1)}) custom-call(f32[768,512]{1,0:T(8,128)S(1)} %get-tuple-element.86.refs_0_, f32[768,384]{1,0:T(8,128)S(1)} %get-tuple-element.85.refs_4_.refs_1_, ...), custom_call_target="tpu_custom_call", output_to_operand_aliasing={{0}: (0, {}), {1}: (1, {})} | custom-call | flops 1000000000 | bytes 4194304 | tf_op jit(solution)/shard_map/pallas_call | solution.py:461
  25.1 0.0 collective-permute-done.5.refs_7_.refs_5_
  25.1 0.0 collective-permute-done.3.refs_0_.refs_2_
  25.1 2.8 %shard_map.138 = (bf16[6,128,128]{2,1,0:T(8,128)(2,1)S(1)}, bf16[2,128,128]{2,1,0:T(8,128)(2,1)S(1)}, f32[4,128,128]{2,1,0:T(8,128)S(1)}, f32[4,128,128]{2,1,0:T(8,128)S(1)}) custom-call(bf16[7,128,128]{2,1,0:T(8,128)(2,1)S(1)} %collective-permute-done.3.refs_0_.refs_2_, f32[4,128,128]{2,1,0:T(8,128)S(1)} %get-tuple-element.79.refs_1_, ...), custom_call_target="tpu_custom_call" | custom-call | flops 3000000000 | bytes 4194304 | tf_op jit(solution)/shard_map/pallas_call | solution.py:461
  27.9 0.1 collective-permute-start.7
  28.0 1.5 %collective-permute-start.6 = (bf16[6,128,128]{2,1,0:T(8,128)(2,1)S(1)}, bf16[6,128,128]{2,1,0:T(8,128)(2,1)S(1)}, u32[]{:S(2)}, u32[]{:S(2)}) collective-permute-start(bf16[6,128,128]{2,1,0:T(8,128)(2,1)S(1)} %get-tuple-element.93.refs_0_.refs_10_), channel_id=1, source_target_pairs={{1,2},{3,4},{5,6},{7,8},{9,10},{11,12},{13,14},{17,18},{19,20},{21... | collective-permute-start | bytes 589832 | tf_op jit(solution)/shard_map/ppermute | solution.py:598
  29.5 2.2 %shard_map.139 = (f32[768,384]{1,0:T(8,128)S(1)}, bf16[10,128,128]{2,1,0:T(8,128)(2,1)S(1)}, bf16[8,128,640]{2,1,0:T(8,128)(2,1)S(1)}) custom-call(bf16[1,128,128]{2,1,0:T(8,128)(2,1)S(1)} %get-tuple-element.62.refs_3_.refs_0_, bf16[6,128,128]{2,1,0:T(8,128)(2,1)S(1)} %collective-permute-done.1.refs_1_, ...), custom_call_target="tpu_custom_call" | custom-call | flops 2000000000 | bytes 4194304 | tf_op jit(solution)/shard_map/pallas_call | solution.py:461
  31.8 0.0 collective-permute-done.7.refs_1_
  31.8 1.9 %shard_map.140 = (f32[768,512]{1,0:T(8,128)S(1)}, bf16[2,2,128,128]{3,2,1,0:T(8,128)(2,1)S(1)}, f32[2,128,128]{2,1,0:T(8,128)S(1)}, f32[2,128,128]{2,1,0:T(8,128)S(1)}, bf16[6,128,640]{2,1,0:T(8,128)(2,1)S(1)}) custom-call(bf16[6,128,128]{2,1,0:T(8,128)(2,1)S(1)} %get-tuple-element.93.refs_0_.refs_10_, ...), custom_call_target="tpu_custom_call" | custom-call | flops 2000000000 | bytes 4194304 | tf_op jit(solution)/shard_map/pallas_call | solution.py:461
  33.7 0.7 %collective-permute-start.8 = (bf16[2,2,128,128]{3,2,1,0:T(8,128)(2,1)S(1)}, bf16[2,2,128,128]{3,2,1,0:T(8,128)(2,1)S(1)}, u32[]{:S(2)}, u32[]{:S(2)}) collective-permute-start(bf16[2,2,128,128]{3,2,1,0:T(8,128)(2,1)S(1)} %get-tuple-element.104.refs_8_.refs_6_), channel_id=1, source_target_pairs={{0,1},{1,0},{2,3},{3,2},{4,5},{5,4},{6,7},{7,6},{8,9},{9,8},{10,11... | collective-permute-start | bytes 393224 | tf_op jit(solution)/shard_map/ppermute | solution.py:546
  34.4 1.4 %shard_map.141 = (f32[768,512]{1,0:T(8,128)S(1)}, f32[768,384]{1,0:T(8,128)S(1)}, f32[512,128]{1,0:T(8,128)S(1)}, bf16[4,16,128]{2,1,0:T(8,128)(2,1)S(1)}) custom-call(f32[768,512]{1,0:T(8,128)S(1)} %get-tuple-element.101.refs_0_, f32[768,384]{1,0:T(8,128)S(1)} %get-tuple-element.100.refs_4_.refs_1_, ...), custom_call_target="tpu_custom_call", output_to_operand_aliasing={{0}: (0, {}), {1}: (1, {})} | custom-call | flops 1000000000 | bytes 4194304 | tf_op jit(solution)/shard_map/pallas_call | solution.py:461
  35.8 0.0 collective-permute-done.8.refs_7_
  35.8 0.0 collective-permute-done.6.refs_0_
  35.8 3.5 %shard_map.142 = (bf16[3,4,16,128]{3,2,1,0:T(8,128)(2,1)}, f32[4,128,128]{2,1,0:T(8,128)}, f32[4,128,128]{2,1,0:T(8,128)}) custom-call(bf16[6,128,128]{2,1,0:T(8,128)(2,1)S(1)} %collective-permute-done.6.refs_0_, f32[4,128,128]{2,1,0:T(8,128)S(1)} %get-tuple-element.94.refs_1_, f32[4,128,128]{2,1,0:T(8,128)S(1)} %get-tuple-element.95.refs_3_.refs_2_, ...), custom_call_target="tpu_custom_call" | custom-call | flops 3000000000 | bytes 4194304 | tf_op jit(solution)/shard_map/pallas_call | solution.py:461
Async XLA Ops:
  2.0 3.1 %collective-permute-start.1 = (bf16[6,128,128]{2,1,0:T(8,128)(2,1)S(1)}, bf16[6,128,128]{2,1,0:T(8,128)(2,1)S(1)}, u32[]{:S(2)}, u32[]{:S(2)}) collective-permute-start(bf16[6,128,128]{2,1,0:T(8,128)(2,1)S(1)} %get-tuple-element.63), channel_id=1, source_target_pairs={{0,1},{1,0},{2,3},{3,2},{4,5},{5,4},{6,7},{7,6},{8,9},{9,8},{10,11... | collective-permute-start | bytes 589832 | tf_op jit(solution)/shard_map/ppermute | solution.py:512
  2.6 10.3 %collective-permute-start = (bf16[11,128,128]{2,1,0:T(8,128)(2,1)S(1)}, bf16[11,128,128]{2,1,0:T(8,128)(2,1)S(1)}, u32[]{:S(2)}, u32[]{:S(2)}) collective-permute-start(bf16[11,128,128]{2,1,0:T(8,128)(2,1)S(1)} %get-tuple-element.59.refs_0_), channel_id=1, source_target_pairs={{1,2},{3,4},{5,6},{7,8},{9,10},{11,12},{13,14},{17,18},{19,20},{21... | collective-permute-start | bytes 1081352 | tf_op jit(solution)/shard_map/ppermute | solution.py:513
  11.3 1.6 %collective-permute-start.2 = (bf16[2,2,128,128]{3,2,1,0:T(8,128)(2,1)S(1)}, bf16[2,2,128,128]{3,2,1,0:T(8,128)(2,1)S(1)}, u32[]{:S(2)}, u32[]{:S(2)}) collective-permute-start(bf16[2,2,128,128]{3,2,1,0:T(8,128)(2,1)S(1)} %get-tuple-element.72.refs_8_.refs_6_.refs_4_), channel_id=1, source_target_pairs={{0,1},{1,0},{2,3},{3,2},{4,5},{5,4},{6,7},{7,6},{8,9},{9,8},{10,11... | collective-permute-start | bytes 393224 | tf_op jit(solution)/shard_map/ppermute | solution.py:546
  16.1 4.4 %collective-permute-start.4 = (bf16[2,128,128]{2,1,0:T(8,128)(2,1)S(1)}, bf16[2,128,128]{2,1,0:T(8,128)(2,1)S(1)}, u32[]{:S(2)}, u32[]{:S(2)}) collective-permute-start(bf16[2,128,128]{2,1,0:T(8,128)(2,1)S(1)} %get-tuple-element.82), channel_id=1, source_target_pairs={{0,1},{1,0},{2,3},{3,2},{4,5},{5,4},{6,7},{7,6},{8,9},{9,8},{10,11... | collective-permute-start | bytes 196616 | tf_op jit(solution)/shard_map/ppermute | solution.py:597
  16.8 8.3 %collective-permute-start.3 = (bf16[7,128,128]{2,1,0:T(8,128)(2,1)S(1)}, bf16[7,128,128]{2,1,0:T(8,128)(2,1)S(1)}, u32[]{:S(2)}, u32[]{:S(2)}) collective-permute-start(bf16[7,128,128]{2,1,0:T(8,128)(2,1)S(1)} %get-tuple-element.78.refs_0_.refs_10_), channel_id=1, source_target_pairs={{1,2},{3,4},{5,6},{7,8},{9,10},{11,12},{13,14},{17,18},{19,20},{21... | collective-permute-start | bytes 688136 | tf_op jit(solution)/shard_map/ppermute | solution.py:598
  20.6 3.1 %copy-start = (bf16[128,16]{0,1:T(8,128)(2,1)S(1)}, bf16[128,16]{0,1:T(8,128)(2,1)}, u32[]{:S(2)}) copy-start(bf16[128,16]{0,1:T(8,128)(2,1)} %param.21) | copy-start | bytes 12292
  22.5 2.6 %collective-permute-start.5 = (bf16[2,2,128,128]{3,2,1,0:T(8,128)(2,1)S(1)}, bf16[2,2,128,128]{3,2,1,0:T(8,128)(2,1)S(1)}, u32[]{:S(2)}, u32[]{:S(2)}) collective-permute-start(bf16[2,2,128,128]{3,2,1,0:T(8,128)(2,1)S(1)} %get-tuple-element.89.refs_8_.refs_6_.refs_4_), channel_id=1, source_target_pairs={{0,1},{1,0},{2,3},{3,2},{4,5},{5,4},{6,7},{7,6},{8,9},{9,8},{10,11... | collective-permute-start | bytes 393224 | tf_op jit(solution)/shard_map/ppermute | solution.py:546
  27.9 3.9 %collective-permute-start.7 = (bf16[2,128,128]{2,1,0:T(8,128)(2,1)S(1)}, bf16[2,128,128]{2,1,0:T(8,128)(2,1)S(1)}, u32[]{:S(2)}, u32[]{:S(2)}) collective-permute-start(bf16[2,128,128]{2,1,0:T(8,128)(2,1)S(1)} %get-tuple-element.97), channel_id=1, source_target_pairs={{0,1},{1,0},{2,3},{3,2},{4,5},{5,4},{6,7},{7,6},{8,9},{9,8},{10,11... | collective-permute-start | bytes 196616 | tf_op jit(solution)/shard_map/ppermute | solution.py:597
  28.0 7.8 %collective-permute-start.6 = (bf16[6,128,128]{2,1,0:T(8,128)(2,1)S(1)}, bf16[6,128,128]{2,1,0:T(8,128)(2,1)S(1)}, u32[]{:S(2)}, u32[]{:S(2)}) collective-permute-start(bf16[6,128,128]{2,1,0:T(8,128)(2,1)S(1)} %get-tuple-element.93.refs_0_.refs_10_), channel_id=1, source_target_pairs={{1,2},{3,4},{5,6},{7,8},{9,10},{11,12},{13,14},{17,18},{19,20},{21... | collective-permute-start | bytes 589832 | tf_op jit(solution)/shard_map/ppermute | solution.py:598
  33.7 2.2 %collective-permute-start.8 = (bf16[2,2,128,128]{3,2,1,0:T(8,128)(2,1)S(1)}, bf16[2,2,128,128]{3,2,1,0:T(8,128)(2,1)S(1)}, u32[]{:S(2)}, u32[]{:S(2)}) collective-permute-start(bf16[2,2,128,128]{3,2,1,0:T(8,128)(2,1)S(1)} %get-tuple-element.104.refs_8_.refs_6_), channel_id=1, source_target_pairs={{0,1},{1,0},{2,3},{3,2},{4,5},{5,4},{6,7},{7,6},{8,9},{9,8},{10,11... | collective-permute-start | bytes 393224 | tf_op jit(solution)/shard_map/ppermute | solution.py:546

commit v4 on v3

--- a/solution.py
+++ b/solution.py
@@ -319,6 +319,8 @@
     else:
         hid, w_out, acc, acc_m, gate, predicted, pad, im = refs[10:]
     cols, width = low_mid.shape[2], low_mid.shape[3]
+    add_last_tap(acc, im_h, im_x, 4, w_h, w_x, H_PARTS, 4)
+    add_last_tap(acc_m, im_m, im_x, 4 if first else 2, w_m, w_x, M_PARTS, 4)
     clear_pad(pad)
     for k in range(2):
         for part in range(2):
@@ -330,8 +332,6 @@
     more = two_taps(lhs, w_o, 2, 1)
     gate[2 * cols : 3 * cols] = part[cols:, width:] + more[:cols, :width]
     gate[3 * cols :] = more[cols:, :width] + more[:cols, width:]
-    add_last_tap(acc, im_h, im_x, 4, w_h, w_x, H_PARTS, 4)
-    add_last_tap(acc_m, im_m, im_x, 4 if first else 2, w_m, w_x, M_PARTS, 4)
     if not first:
         predict(predicted, hid, w_out)
 

time: 39.6 us -> 39.6 us (level)
  no operation moved by 1% of the time
where the time goes in v4:
time: 39.6 us; the launch traced here: 39.4 us
  Pallas kernels  29.5 us (74%)
  starting transfers between devices  9 us (23%)
  between operations  0.91 us (2%)
    pallas_call x13, Pallas kernels, call(): pl.pallas_call(body, out_shape=[jax.ShapeDtypeStruct(shape, kind) for sha...  29.5 us
    ppermute x2, starting transfers between devices, per_device(): arrived = lax.ppermute(far, ('groups', 'row'), across)  3.01 us
    ppermute x1, starting transfers between devices, per_device(): arrived = lax.ppermute(far0, ('groups', 'row'), across)  2.56 us
    ppermute x3, starting transfers between devices, per_device(): low_in = lax.ppermute(low_mid, 'row', beside)  2.13 us
  transfers between devices with their start and end apart: 9, of which 0 were waited for; matrix products, arithmetic and copies ran while one was open for 0% of the time, Pallas kernels for 47%

profile of v4, /device:TPU:0, one launch (start us, length us, event | category | flops | bytes accessed | tf_op | source)
XLA Modules:
  0.0 39.4 jit_solution(17816013016033954807)
XLA Ops:
  0.6 1.4 %shard_map.130 = (bf16[11,128,128]{2,1,0:T(8,128)(2,1)S(1)}, bf16[6,128,128]{2,1,0:T(8,128)(2,1)S(1)}, f32[4,128,128]{2,1,0:T(8,128)S(1)}, f32[4,128,128]{2,1,0:T(8,128)S(1)}, bf16[1,128,128]{2,1,0:T(8,128)(2,1)S(1)}) custom-call(bf16[4,128,128]{2,1,0:T(8,128)(2,1)} %h_hbm.1, f32[4,128,128]{2,1,0:T(8,128)} %c_hbm.1, f32[4,128,128]{2,1,0:T(8,128)} %m_hbm.1, ...), custom_call_target="tpu_custom_call" | custom-call | flops 1000000 | bytes 4194304 | tf_op jit(solution)/shard_map/pallas_call | solution.py:461
  2.0 0.5 %collective-permute-start.1 = (bf16[6,128,128]{2,1,0:T(8,128)(2,1)S(1)}, bf16[6,128,128]{2,1,0:T(8,128)(2,1)S(1)}, u32[]{:S(2)}, u32[]{:S(2)}) collective-permute-start(bf16[6,128,128]{2,1,0:T(8,128)(2,1)S(1)} %get-tuple-element.63), channel_id=1, source_target_pairs={{0,1},{1,0},{2,3},{3,2},{4,5},{5,4},{6,7},{7,6},{8,9},{9,8},{10,11... | collective-permute-start | bytes 589832 | tf_op jit(solution)/shard_map/ppermute | solution.py:512
  2.6 2.6 %collective-permute-start = (bf16[11,128,128]{2,1,0:T(8,128)(2,1)S(1)}, bf16[11,128,128]{2,1,0:T(8,128)(2,1)S(1)}, u32[]{:S(2)}, u32[]{:S(2)}) collective-permute-start(bf16[11,128,128]{2,1,0:T(8,128)(2,1)S(1)} %get-tuple-element.59.refs_0_), channel_id=1, source_target_pairs={{1,2},{3,4},{5,6},{7,8},{9,10},{11,12},{13,14},{17,18},{19,20},{21... | collective-permute-start | bytes 1081352 | tf_op jit(solution)/shard_map/ppermute | solution.py:513
  5.1 0.0 collective-permute-done.1.refs_1_
  5.1 4.2 %shard_map.131 = (f32[768,384]{1,0:T(8,128)S(1)}, bf16[10,128,128]{2,1,0:T(8,128)(2,1)S(1)}, bf16[6,128,640]{2,1,0:T(8,128)(2,1)S(1)}, bf16[5,80,896]{2,1,0:T(8,...) custom-call(bf16[11,128,128]{2,1,0:T(8,128)(2,1)S(1)} %get-tuple-ele, ...), custom_call_target="tpu_custom_call" | custom-call | flops 2000000000 | bytes 4194304 | tf_op jit(solution)/shard_map/pallas_call | solution.py:461
  9.3 1.9 %shard_map.132 = (f32[768,512]{1,0:T(8,128)S(1)}, bf16[2,2,128,128]{3,2,1,0:T(8,128)(2,1)S(1)}, f32[2,128,128]{2,1,0:T(8,128)S(1)}, f32[2,128,128]{2,1,0:T(8,128)S(1)}, bf16[6,128,640]{2,1,0:T(8,128)(2,1)S(1)}) custom-call(bf16[11,128,128]{2,1,0:T(8,128)(2,1)S(1)} %get-tuple-element.59.refs_0_, bf16[6,128,128]{2,1,0:T(8,128)(2,1)S(1)} %collective-permute-done.1.refs_1_, ...), custom_call_target="tpu_custom_call" | custom-call | flops 2000000000 | bytes 4194304 | tf_op jit(solution)/shard_map/pallas_call | solution.py:461
  11.3 0.2 collective-permute-start.2
  11.5 1.4 %shard_map.133 = (f32[768,512]{1,0:T(8,128)S(1)}, f32[768,384]{1,0:T(8,128)S(1)}, f32[512,128]{1,0:T(8,128)S(1)}) custom-call(f32[768,512]{1,0:T(8,128)S(1)} %get-tuple-element.68.refs_0_, f32[768,384]{1,0:T(8,128)S(1)} %get-tuple-element.64.refs_4_.refs_1_, ...), custom_call_target="tpu_custom_call", output_to_operand_aliasing={{0}: (0, {}), {1}: (1, {})} | custom-call | flops 1000000000 | bytes 4194304 | tf_op jit(solution)/shard_map/pallas_call | solution.py:461
  12.9 0.0 collective-permute-done.2.refs_7_.refs_5_
  12.9 0.0 collective-permute-done.refs_0_.refs_2_
  12.9 3.2 %shard_map.134 = (bf16[7,128,128]{2,1,0:T(8,128)(2,1)S(1)}, bf16[2,128,128]{2,1,0:T(8,128)(2,1)S(1)}, f32[4,128,128]{2,1,0:T(8,128)S(1)}, f32[4,128,128]{2,1,0:T(8,128)S(1)}) custom-call(bf16[11,128,128]{2,1,0:T(8,128)(2,1)S(1)} %collective-permute-done.refs_0_.refs_2_, f32[4,128,128]{2,1,0:T(8,128)S(1)} %get-tuple-element.60.refs_2_.refs_1_, ...), custom_call_target="tpu_custom_call" | custom-call | flops 3000000000 | bytes 4194304 | tf_op jit(solution)/shard_map/pallas_call | solution.py:461
  16.1 0.7 %collective-permute-start.4 = (bf16[2,128,128]{2,1,0:T(8,128)(2,1)S(1)}, bf16[2,128,128]{2,1,0:T(8,128)(2,1)S(1)}, u32[]{:S(2)}, u32[]{:S(2)}) collective-permute-start(bf16[2,128,128]{2,1,0:T(8,128)(2,1)S(1)} %get-tuple-element.82), channel_id=1, source_target_pairs={{0,1},{1,0},{2,3},{3,2},{4,5},{5,4},{6,7},{7,6},{8,9},{9,8},{10,11... | collective-permute-start | bytes 196616 | tf_op jit(solution)/shard_map/ppermute | solution.py:597
  16.8 1.5 %collective-permute-start.3 = (bf16[7,128,128]{2,1,0:T(8,128)(2,1)S(1)}, bf16[7,128,128]{2,1,0:T(8,128)(2,1)S(1)}, u32[]{:S(2)}, u32[]{:S(2)}) collective-permute-start(bf16[7,128,128]{2,1,0:T(8,128)(2,1)S(1)} %get-tuple-element.78.refs_0_.refs_10_), channel_id=1, source_target_pairs={{1,2},{3,4},{5,6},{7,8},{9,10},{11,12},{13,14},{17,18},{19,20},{21... | collective-permute-start | bytes 688136 | tf_op jit(solution)/shard_map/ppermute | solution.py:598
  18.3 2.3 %shard_map.135 = (f32[768,384]{1,0:T(8,128)S(1)}, bf16[10,128,128]{2,1,0:T(8,128)(2,1)S(1)}, bf16[8,128,640]{2,1,0:T(8,128)(2,1)S(1)}) custom-call(bf16[11,128,128]{2,1,0:T(8,128)(2,1)S(1)} %get-tuple-element.59.refs_0_, bf16[6,128,128]{2,1,0:T(8,128)(2,1)S(1)} %collective-permute-done.1.refs_1_, ...), custom_call_target="tpu_custom_call" | custom-call | flops 2000000000 | bytes 4194304 | tf_op jit(solution)/shard_map/pallas_call | solution.py:461
  20.6 0.0 collective-permute-done.4.refs_1_
  20.6 0.0 copy-start
  20.6 1.9 %shard_map.136 = (f32[768,512]{1,0:T(8,128)S(1)}, bf16[2,2,128,128]{3,2,1,0:T(8,128)(2,1)S(1)}, f32[2,128,128]{2,1,0:T(8,128)S(1)}, f32[2,128,128]{2,1,0:T(8,128)S(1)}, bf16[6,128,640]{2,1,0:T(8,128)(2,1)S(1)}) custom-call(bf16[7,128,128]{2,1,0:T(8,128)(2,1)S(1)} %get-tuple-element.78.refs_0_.refs_10_, ...), custom_call_target="tpu_custom_call" | custom-call | flops 2000000000 | bytes 4194304 | tf_op jit(solution)/shard_map/pallas_call | solution.py:461
  22.5 1.1 %collective-permute-start.5 = (bf16[2,2,128,128]{3,2,1,0:T(8,128)(2,1)S(1)}, bf16[2,2,128,128]{3,2,1,0:T(8,128)(2,1)S(1)}, u32[]{:S(2)}, u32[]{:S(2)}) collective-permute-start(bf16[2,2,128,128]{3,2,1,0:T(8,128)(2,1)S(1)} %get-tuple-element.89.refs_8_.refs_6_.refs_4_), channel_id=1, source_target_pairs={{0,1},{1,0},{2,3},{3,2},{4,5},{5,4},{6,7},{7,6},{8,9},{9,8},{10,11... | collective-permute-start | bytes 393224 | tf_op jit(solution)/shard_map/ppermute | solution.py:546
  23.7 0.0 copy-done
  23.7 1.4 %shard_map.137 = (f32[768,512]{1,0:T(8,128)S(1)}, f32[768,384]{1,0:T(8,128)S(1)}, f32[512,128]{1,0:T(8,128)S(1)}, bf16[4,16,128]{2,1,0:T(8,128)(2,1)S(1)}) custom-call(f32[768,512]{1,0:T(8,128)S(1)} %get-tuple-element.86.refs_0_, f32[768,384]{1,0:T(8,128)S(1)} %get-tuple-element.85.refs_4_.refs_1_, ...), custom_call_target="tpu_custom_call", output_to_operand_aliasing={{0}: (0, {}), {1}: (1, {})} | custom-call | flops 1000000000 | bytes 4194304 | tf_op jit(solution)/shard_map/pallas_call | solution.py:461
  25.1 0.0 collective-permute-done.5.refs_7_.refs_5_
  25.1 0.0 collective-permute-done.3.refs_0_.refs_2_
  25.1 2.8 %shard_map.138 = (bf16[6,128,128]{2,1,0:T(8,128)(2,1)S(1)}, bf16[2,128,128]{2,1,0:T(8,128)(2,1)S(1)}, f32[4,128,128]{2,1,0:T(8,128)S(1)}, f32[4,128,128]{2,1,0:T(8,128)S(1)}) custom-call(bf16[7,128,128]{2,1,0:T(8,128)(2,1)S(1)} %collective-permute-done.3.refs_0_.refs_2_, f32[4,128,128]{2,1,0:T(8,128)S(1)} %get-tuple-element.79.refs_1_, ...), custom_call_target="tpu_custom_call" | custom-call | flops 3000000000 | bytes 4194304 | tf_op jit(solution)/shard_map/pallas_call | solution.py:461
  27.9 0.1 collective-permute-start.7
  28.0 1.5 %collective-permute-start.6 = (bf16[6,128,128]{2,1,0:T(8,128)(2,1)S(1)}, bf16[6,128,128]{2,1,0:T(8,128)(2,1)S(1)}, u32[]{:S(2)}, u32[]{:S(2)}) collective-permute-start(bf16[6,128,128]{2,1,0:T(8,128)(2,1)S(1)} %get-tuple-element.93.refs_0_.refs_10_), channel_id=1, source_target_pairs={{1,2},{3,4},{5,6},{7,8},{9,10},{11,12},{13,14},{17,18},{19,20},{21... | collective-permute-start | bytes 589832 | tf_op jit(solution)/shard_map/ppermute | solution.py:598
  29.5 2.2 %shard_map.139 = (f32[768,384]{1,0:T(8,128)S(1)}, bf16[10,128,128]{2,1,0:T(8,128)(2,1)S(1)}, bf16[8,128,640]{2,1,0:T(8,128)(2,1)S(1)}) custom-call(bf16[1,128,128]{2,1,0:T(8,128)(2,1)S(1)} %get-tuple-element.62.refs_3_.refs_0_, bf16[6,128,128]{2,1,0:T(8,128)(2,1)S(1)} %collective-permute-done.1.refs_1_, ...), custom_call_target="tpu_custom_call" | custom-call | flops 2000000000 | bytes 4194304 | tf_op jit(solution)/shard_map/pallas_call | solution.py:461
  31.7 0.0 collective-permute-done.7.refs_1_
  31.7 1.9 %shard_map.140 = (f32[768,512]{1,0:T(8,128)S(1)}, bf16[2,2,128,128]{3,2,1,0:T(8,128)(2,1)S(1)}, f32[2,128,128]{2,1,0:T(8,128)S(1)}, f32[2,128,128]{2,1,0:T(8,128)S(1)}, bf16[6,128,640]{2,1,0:T(8,128)(2,1)S(1)}) custom-call(bf16[6,128,128]{2,1,0:T(8,128)(2,1)S(1)} %get-tuple-element.93.refs_0_.refs_10_, ...), custom_call_target="tpu_custom_call" | custom-call | flops 2000000000 | bytes 4194304 | tf_op jit(solution)/shard_map/pallas_call | solution.py:461
  33.6 0.8 %collective-permute-start.8 = (bf16[2,2,128,128]{3,2,1,0:T(8,128)(2,1)S(1)}, bf16[2,2,128,128]{3,2,1,0:T(8,128)(2,1)S(1)}, u32[]{:S(2)}, u32[]{:S(2)}) collective-permute-start(bf16[2,2,128,128]{3,2,1,0:T(8,128)(2,1)S(1)} %get-tuple-element.104.refs_8_.refs_6_), channel_id=1, source_target_pairs={{0,1},{1,0},{2,3},{3,2},{4,5},{5,4},{6,7},{7,6},{8,9},{9,8},{10,11... | collective-permute-start | bytes 393224 | tf_op jit(solution)/shard_map/ppermute | solution.py:546
  34.4 1.4 %shard_map.141 = (f32[768,512]{1,0:T(8,128)S(1)}, f32[768,384]{1,0:T(8,128)S(1)}, f32[512,128]{1,0:T(8,128)S(1)}, bf16[4,16,128]{2,1,0:T(8,128)(2,1)S(1)}) custom-call(f32[768,512]{1,0:T(8,128)S(1)} %get-tuple-element.101.refs_0_, f32[768,384]{1,0:T(8,128)S(1)} %get-tuple-element.100.refs_4_.refs_1_, ...), custom_call_target="tpu_custom_call", output_to_operand_aliasing={{0}: (0, {}), {1}: (1, {})} | custom-call | flops 1000000000 | bytes 4194304 | tf_op jit(solution)/shard_map/pallas_call | solution.py:461
  35.8 0.0 collective-permute-done.8.refs_7_
  35.8 0.0 collective-permute-done.6.refs_0_
  35.8 3.5 %shard_map.142 = (bf16[3,4,16,128]{3,2,1,0:T(8,128)(2,1)}, f32[4,128,128]{2,1,0:T(8,128)}, f32[4,128,128]{2,1,0:T(8,128)}) custom-call(bf16[6,128,128]{2,1,0:T(8,128)(2,1)S(1)} %collective-permute-done.6.refs_0_, f32[4,128,128]{2,1,0:T(8,128)S(1)} %get-tuple-element.94.refs_1_, f32[4,128,128]{2,1,0:T(8,128)S(1)} %get-tuple-element.95.refs_3_.refs_2_, ...), custom_call_target="tpu_custom_call" | custom-call | flops 3000000000 | bytes 4194304 | tf_op jit(solution)/shard_map/pallas_call | solution.py:461
Async XLA Ops:
  2.0 3.1 %collective-permute-start.1 = (bf16[6,128,128]{2,1,0:T(8,128)(2,1)S(1)}, bf16[6,128,128]{2,1,0:T(8,128)(2,1)S(1)}, u32[]{:S(2)}, u32[]{:S(2)}) collective-permute-start(bf16[6,128,128]{2,1,0:T(8,128)(2,1)S(1)} %get-tuple-element.63), channel_id=1, source_target_pairs={{0,1},{1,0},{2,3},{3,2},{4,5},{5,4},{6,7},{7,6},{8,9},{9,8},{10,11... | collective-permute-start | bytes 589832 | tf_op jit(solution)/shard_map/ppermute | solution.py:512
  2.6 10.3 %collective-permute-start = (bf16[11,128,128]{2,1,0:T(8,128)(2,1)S(1)}, bf16[11,128,128]{2,1,0:T(8,128)(2,1)S(1)}, u32[]{:S(2)}, u32[]{:S(2)}) collective-permute-start(bf16[11,128,128]{2,1,0:T(8,128)(2,1)S(1)} %get-tuple-element.59.refs_0_), channel_id=1, source_target_pairs={{1,2},{3,4},{5,6},{7,8},{9,10},{11,12},{13,14},{17,18},{19,20},{21... | collective-permute-start | bytes 1081352 | tf_op jit(solution)/shard_map/ppermute | solution.py:513
  11.3 1.6 %collective-permute-start.2 = (bf16[2,2,128,128]{3,2,1,0:T(8,128)(2,1)S(1)}, bf16[2,2,128,128]{3,2,1,0:T(8,128)(2,1)S(1)}, u32[]{:S(2)}, u32[]{:S(2)}) collective-permute-start(bf16[2,2,128,128]{3,2,1,0:T(8,128)(2,1)S(1)} %get-tuple-element.72.refs_8_.refs_6_.refs_4_), channel_id=1, source_target_pairs={{0,1},{1,0},{2,3},{3,2},{4,5},{5,4},{6,7},{7,6},{8,9},{9,8},{10,11... | collective-permute-start | bytes 393224 | tf_op jit(solution)/shard_map/ppermute | solution.py:546
  16.1 4.4 %collective-permute-start.4 = (bf16[2,128,128]{2,1,0:T(8,128)(2,1)S(1)}, bf16[2,128,128]{2,1,0:T(8,128)(2,1)S(1)}, u32[]{:S(2)}, u32[]{:S(2)}) collective-permute-start(bf16[2,128,128]{2,1,0:T(8,128)(2,1)S(1)} %get-tuple-element.82), channel_id=1, source_target_pairs={{0,1},{1,0},{2,3},{3,2},{4,5},{5,4},{6,7},{7,6},{8,9},{9,8},{10,11... | collective-permute-start | bytes 196616 | tf_op jit(solution)/shard_map/ppermute | solution.py:597
  16.8 8.3 %collective-permute-start.3 = (bf16[7,128,128]{2,1,0:T(8,128)(2,1)S(1)}, bf16[7,128,128]{2,1,0:T(8,128)(2,1)S(1)}, u32[]{:S(2)}, u32[]{:S(2)}) collective-permute-start(bf16[7,128,128]{2,1,0:T(8,128)(2,1)S(1)} %get-tuple-element.78.refs_0_.refs_10_), channel_id=1, source_target_pairs={{1,2},{3,4},{5,6},{7,8},{9,10},{11,12},{13,14},{17,18},{19,20},{21... | collective-permute-start | bytes 688136 | tf_op jit(solution)/shard_map/ppermute | solution.py:598
  20.6 3.1 %copy-start = (bf16[128,16]{0,1:T(8,128)(2,1)S(1)}, bf16[128,16]{0,1:T(8,128)(2,1)}, u32[]{:S(2)}) copy-start(bf16[128,16]{0,1:T(8,128)(2,1)} %param.21) | copy-start | bytes 12292
  22.5 2.5 %collective-permute-start.5 = (bf16[2,2,128,128]{3,2,1,0:T(8,128)(2,1)S(1)}, bf16[2,2,128,128]{3,2,1,0:T(8,128)(2,1)S(1)}, u32[]{:S(2)}, u32[]{:S(2)}) collective-permute-start(bf16[2,2,128,128]{3,2,1,0:T(8,128)(2,1)S(1)} %get-tuple-element.89.refs_8_.refs_6_.refs_4_), channel_id=1, source_target_pairs={{0,1},{1,0},{2,3},{3,2},{4,5},{5,4},{6,7},{7,6},{8,9},{9,8},{10,11... | collective-permute-start | bytes 393224 | tf_op jit(solution)/shard_map/ppermute | solution.py:546
  27.9 3.9 %collective-permute-start.7 = (bf16[2,128,128]{2,1,0:T(8,128)(2,1)S(1)}, bf16[2,128,128]{2,1,0:T(8,128)(2,1)S(1)}, u32[]{:S(2)}, u32[]{:S(2)}) collective-permute-start(bf16[2,128,128]{2,1,0:T(8,128)(2,1)S(1)} %get-tuple-element.97), channel_id=1, source_target_pairs={{0,1},{1,0},{2,3},{3,2},{4,5},{5,4},{6,7},{7,6},{8,9},{9,8},{10,11... | collective-permute-start | bytes 196616 | tf_op jit(solution)/shard_map/ppermute | solution.py:597
  28.0 7.8 %collective-permute-start.6 = (bf16[6,128,128]{2,1,0:T(8,128)(2,1)S(1)}, bf16[6,128,128]{2,1,0:T(8,128)(2,1)S(1)}, u32[]{:S(2)}, u32[]{:S(2)}) collective-permute-start(bf16[6,128,128]{2,1,0:T(8,128)(2,1)S(1)} %get-tuple-element.93.refs_0_.refs_10_), channel_id=1, source_target_pairs={{1,2},{3,4},{5,6},{7,8},{9,10},{11,12},{13,14},{17,18},{19,20},{21... | collective-permute-start | bytes 589832 | tf_op jit(solution)/shard_map/ppermute | solution.py:598
  33.6 2.2 %collective-permute-start.8 = (bf16[2,2,128,128]{3,2,1,0:T(8,128)(2,1)S(1)}, bf16[2,2,128,128]{3,2,1,0:T(8,128)(2,1)S(1)}, u32[]{:S(2)}, u32[]{:S(2)}) collective-permute-start(bf16[2,2,128,128]{3,2,1,0:T(8,128)(2,1)S(1)} %get-tuple-element.104.refs_8_.refs_6_), channel_id=1, source_target_pairs={{0,1},{1,0},{2,3},{3,2},{4,5},{5,4},{6,7},{7,6},{8,9},{9,8},{10,11... | collective-permute-start | bytes 393224 | tf_op jit(solution)/shard_map/ppermute | solution.py:546

commit v5 on v4

--- a/solution.py
+++ b/solution.py
@@ -73,7 +73,7 @@
     im[row] = total.astype(BF)
 
 
-H_PARTS = ((0, 256, ((0, 256),)), (256, 512, ((256, 384), (768, 896))))
+H_PARTS = ((0, 512, ((0, 384), (768, 896))),)
 M_PARTS = ((0, 256, ((384, 640),)), (256, 384, ((640, 768),)))
 
 

time: 39.6 us -> 39.6 us (level)
  no operation moved by 1% of the time
where the time goes in v5:
time: 39.6 us; the launch traced here: 39.4 us
  Pallas kernels  29.5 us (74%)
  starting transfers between devices  9 us (23%)
  between operations  0.91 us (2%)
    pallas_call x13, Pallas kernels, call(): pl.pallas_call(body, out_shape=[jax.ShapeDtypeStruct(shape, kind) for sha...  29.5 us
    ppermute x2, starting transfers between devices, per_device(): arrived = lax.ppermute(far, ('groups', 'row'), across)  3.01 us
    ppermute x1, starting transfers between devices, per_device(): arrived = lax.ppermute(far0, ('groups', 'row'), across)  2.56 us
    ppermute x3, starting transfers between devices, per_device(): low_in = lax.ppermute(low_mid, 'row', beside)  2.13 us
  transfers between devices with their start and end apart: 9, of which 0 were waited for; matrix products, arithmetic and copies ran while one was open for 0% of the time, Pallas kernels for 47%

profile of v5, /device:TPU:0, one launch (start us, length us, event | category | flops | bytes accessed | tf_op | source)
XLA Modules:
  0.0 39.4 jit_solution(17816013016033954807)
XLA Ops:
  0.6 1.4 %shard_map.130 = (bf16[11,128,128]{2,1,0:T(8,128)(2,1)S(1)}, bf16[6,128,128]{2,1,0:T(8,128)(2,1)S(1)}, f32[4,128,128]{2,1,0:T(8,128)S(1)}, f32[4,128,128]{2,1,0:T(8,128)S(1)}, bf16[1,128,128]{2,1,0:T(8,128)(2,1)S(1)}) custom-call(bf16[4,128,128]{2,1,0:T(8,128)(2,1)} %h_hbm.1, f32[4,128,128]{2,1,0:T(8,128)} %c_hbm.1, f32[4,128,128]{2,1,0:T(8,128)} %m_hbm.1, ...), custom_call_target="tpu_custom_call" | custom-call | flops 1000000 | bytes 4194304 | tf_op jit(solution)/shard_map/pallas_call | solution.py:461
  2.0 0.5 %collective-permute-start.1 = (bf16[6,128,128]{2,1,0:T(8,128)(2,1)S(1)}, bf16[6,128,128]{2,1,0:T(8,128)(2,1)S(1)}, u32[]{:S(2)}, u32[]{:S(2)}) collective-permute-start(bf16[6,128,128]{2,1,0:T(8,128)(2,1)S(1)} %get-tuple-element.63), channel_id=1, source_target_pairs={{0,1},{1,0},{2,3},{3,2},{4,5},{5,4},{6,7},{7,6},{8,9},{9,8},{10,11... | collective-permute-start | bytes 589832 | tf_op jit(solution)/shard_map/ppermute | solution.py:512
  2.6 2.6 %collective-permute-start = (bf16[11,128,128]{2,1,0:T(8,128)(2,1)S(1)}, bf16[11,128,128]{2,1,0:T(8,128)(2,1)S(1)}, u32[]{:S(2)}, u32[]{:S(2)}) collective-permute-start(bf16[11,128,128]{2,1,0:T(8,128)(2,1)S(1)} %get-tuple-element.59.refs_0_), channel_id=1, source_target_pairs={{1,2},{3,4},{5,6},{7,8},{9,10},{11,12},{13,14},{17,18},{19,20},{21... | collective-permute-start | bytes 1081352 | tf_op jit(solution)/shard_map/ppermute | solution.py:513
  5.1 0.0 collective-permute-done.1.refs_1_
  5.1 4.2 %shard_map.131 = (f32[768,384]{1,0:T(8,128)S(1)}, bf16[10,128,128]{2,1,0:T(8,128)(2,1)S(1)}, bf16[6,128,640]{2,1,0:T(8,128)(2,1)S(1)}, bf16[5,80,896]{2,1,0:T(8,...) custom-call(bf16[11,128,128]{2,1,0:T(8,128)(2,1)S(1)} %get-tuple-ele, ...), custom_call_target="tpu_custom_call" | custom-call | flops 2000000000 | bytes 4194304 | tf_op jit(solution)/shard_map/pallas_call | solution.py:461
  9.3 1.9 %shard_map.132 = (f32[768,512]{1,0:T(8,128)S(1)}, bf16[2,2,128,128]{3,2,1,0:T(8,128)(2,1)S(1)}, f32[2,128,128]{2,1,0:T(8,128)S(1)}, f32[2,128,128]{2,1,0:T(8,128)S(1)}, bf16[6,128,640]{2,1,0:T(8,128)(2,1)S(1)}) custom-call(bf16[11,128,128]{2,1,0:T(8,128)(2,1)S(1)} %get-tuple-element.59.refs_0_, bf16[6,128,128]{2,1,0:T(8,128)(2,1)S(1)} %collective-permute-done.1.refs_1_, ...), custom_call_target="tpu_custom_call" | custom-call | flops 2000000000 | bytes 4194304 | tf_op jit(solution)/shard_map/pallas_call | solution.py:461
  11.3 0.2 collective-permute-start.2
  11.5 1.4 %shard_map.133 = (f32[768,512]{1,0:T(8,128)S(1)}, f32[768,384]{1,0:T(8,128)S(1)}, f32[512,128]{1,0:T(8,128)S(1)}) custom-call(f32[768,512]{1,0:T(8,128)S(1)} %get-tuple-element.68.refs_0_, f32[768,384]{1,0:T(8,128)S(1)} %get-tuple-element.64.refs_4_.refs_1_, ...), custom_call_target="tpu_custom_call", output_to_operand_aliasing={{0}: (0, {}), {1}: (1, {})} | custom-call | flops 1000000000 | bytes 4194304 | tf_op jit(solution)/shard_map/pallas_call | solution.py:461
  12.9 0.0 collective-permute-done.2.refs_7_.refs_5_
  12.9 0.0 collective-permute-done.refs_0_.refs_2_
  12.9 3.2 %shard_map.134 = (bf16[7,128,128]{2,1,0:T(8,128)(2,1)S(1)}, bf16[2,128,128]{2,1,0:T(8,128)(2,1)S(1)}, f32[4,128,128]{2,1,0:T(8,128)S(1)}, f32[4,128,128]{2,1,0:T(8,128)S(1)}) custom-call(bf16[11,128,128]{2,1,0:T(8,128)(2,1)S(1)} %collective-permute-done.refs_0_.refs_2_, f32[4,128,128]{2,1,0:T(8,128)S(1)} %get-tuple-element.60.refs_2_.refs_1_, ...), custom_call_target="tpu_custom_call" | custom-call | flops 3000000000 | bytes 4194304 | tf_op jit(solution)/shard_map/pallas_call | solution.py:461
  16.1 0.7 %collective-permute-start.4 = (bf16[2,128,128]{2,1,0:T(8,128)(2,1)S(1)}, bf16[2,128,128]{2,1,0:T(8,128)(2,1)S(1)}, u32[]{:S(2)}, u32[]{:S(2)}) collective-permute-start(bf16[2,128,128]{2,1,0:T(8,128)(2,1)S(1)} %get-tuple-element.82), channel_id=1, source_target_pairs={{0,1},{1,0},{2,3},{3,2},{4,5},{5,4},{6,7},{7,6},{8,9},{9,8},{10,11... | collective-permute-start | bytes 196616 | tf_op jit(solution)/shard_map/ppermute | solution.py:597
  16.8 1.5 %collective-permute-start.3 = (bf16[7,128,128]{2,1,0:T(8,128)(2,1)S(1)}, bf16[7,128,128]{2,1,0:T(8,128)(2,1)S(1)}, u32[]{:S(2)}, u32[]{:S(2)}) collective-permute-start(bf16[7,128,128]{2,1,0:T(8,128)(2,1)S(1)} %get-tuple-element.78.refs_0_.refs_10_), channel_id=1, source_target_pairs={{1,2},{3,4},{5,6},{7,8},{9,10},{11,12},{13,14},{17,18},{19,20},{21... | collective-permute-start | bytes 688136 | tf_op jit(solution)/shard_map/ppermute | solution.py:598
  18.3 2.3 %shard_map.135 = (f32[768,384]{1,0:T(8,128)S(1)}, bf16[10,128,128]{2,1,0:T(8,128)(2,1)S(1)}, bf16[8,128,640]{2,1,0:T(8,128)(2,1)S(1)}) custom-call(bf16[11,128,128]{2,1,0:T(8,128)(2,1)S(1)} %get-tuple-element.59.refs_0_, bf16[6,128,128]{2,1,0:T(8,128)(2,1)S(1)} %collective-permute-done.1.refs_1_, ...), custom_call_target="tpu_custom_call" | custom-call | flops 2000000000 | bytes 4194304 | tf_op jit(solution)/shard_map/pallas_call | solution.py:461
  20.6 0.0 collective-permute-done.4.refs_1_
  20.6 0.0 copy-start
  20.6 1.9 %shard_map.136 = (f32[768,512]{1,0:T(8,128)S(1)}, bf16[2,2,128,128]{3,2,1,0:T(8,128)(2,1)S(1)}, f32[2,128,128]{2,1,0:T(8,128)S(1)}, f32[2,128,128]{2,1,0:T(8,128)S(1)}, bf16[6,128,640]{2,1,0:T(8,128)(2,1)S(1)}) custom-call(bf16[7,128,128]{2,1,0:T(8,128)(2,1)S(1)} %get-tuple-element.78.refs_0_.refs_10_, ...), custom_call_target="tpu_custom_call" | custom-call | flops 2000000000 | bytes 4194304 | tf_op jit(solution)/shard_map/pallas_call | solution.py:461
  22.5 1.1 %collective-permute-start.5 = (bf16[2,2,128,128]{3,2,1,0:T(8,128)(2,1)S(1)}, bf16[2,2,128,128]{3,2,1,0:T(8,128)(2,1)S(1)}, u32[]{:S(2)}, u32[]{:S(2)}) collective-permute-start(bf16[2,2,128,128]{3,2,1,0:T(8,128)(2,1)S(1)} %get-tuple-element.89.refs_8_.refs_6_.refs_4_), channel_id=1, source_target_pairs={{0,1},{1,0},{2,3},{3,2},{4,5},{5,4},{6,7},{7,6},{8,9},{9,8},{10,11... | collective-permute-start | bytes 393224 | tf_op jit(solution)/shard_map/ppermute | solution.py:546
  23.7 0.0 copy-done
  23.7 1.4 %shard_map.137 = (f32[768,512]{1,0:T(8,128)S(1)}, f32[768,384]{1,0:T(8,128)S(1)}, f32[512,128]{1,0:T(8,128)S(1)}, bf16[4,16,128]{2,1,0:T(8,128)(2,1)S(1)}) custom-call(f32[768,512]{1,0:T(8,128)S(1)} %get-tuple-element.86.refs_0_, f32[768,384]{1,0:T(8,128)S(1)} %get-tuple-element.85.refs_4_.refs_1_, ...), custom_call_target="tpu_custom_call", output_to_operand_aliasing={{0}: (0, {}), {1}: (1, {})} | custom-call | flops 1000000000 | bytes 4194304 | tf_op jit(solution)/shard_map/pallas_call | solution.py:461
  25.1 0.0 collective-permute-done.5.refs_7_.refs_5_
  25.1 0.0 collective-permute-done.3.refs_0_.refs_2_
  25.1 2.8 %shard_map.138 = (bf16[6,128,128]{2,1,0:T(8,128)(2,1)S(1)}, bf16[2,128,128]{2,1,0:T(8,128)(2,1)S(1)}, f32[4,128,128]{2,1,0:T(8,128)S(1)}, f32[4,128,128]{2,1,0:T(8,128)S(1)}) custom-call(bf16[7,128,128]{2,1,0:T(8,128)(2,1)S(1)} %collective-permute-done.3.refs_0_.refs_2_, f32[4,128,128]{2,1,0:T(8,128)S(1)} %get-tuple-element.79.refs_1_, ...), custom_call_target="tpu_custom_call" | custom-call | flops 3000000000 | bytes 4194304 | tf_op jit(solution)/shard_map/pallas_call | solution.py:461
  27.9 0.1 collective-permute-start.7
  28.0 1.5 %collective-permute-start.6 = (bf16[6,128,128]{2,1,0:T(8,128)(2,1)S(1)}, bf16[6,128,128]{2,1,0:T(8,128)(2,1)S(1)}, u32[]{:S(2)}, u32[]{:S(2)}) collective-permute-start(bf16[6,128,128]{2,1,0:T(8,128)(2,1)S(1)} %get-tuple-element.93.refs_0_.refs_10_), channel_id=1, source_target_pairs={{1,2},{3,4},{5,6},{7,8},{9,10},{11,12},{13,14},{17,18},{19,20},{21... | collective-permute-start | bytes 589832 | tf_op jit(solution)/shard_map/ppermute | solution.py:598
  29.5 2.2 %shard_map.139 = (f32[768,384]{1,0:T(8,128)S(1)}, bf16[10,128,128]{2,1,0:T(8,128)(2,1)S(1)}, bf16[8,128,640]{2,1,0:T(8,128)(2,1)S(1)}) custom-call(bf16[1,128,128]{2,1,0:T(8,128)(2,1)S(1)} %get-tuple-element.62.refs_3_.refs_0_, bf16[6,128,128]{2,1,0:T(8,128)(2,1)S(1)} %collective-permute-done.1.refs_1_, ...), custom_call_target="tpu_custom_call" | custom-call | flops 2000000000 | bytes 4194304 | tf_op jit(solution)/shard_map/pallas_call | solution.py:461
  31.7 0.0 collective-permute-done.7.refs_1_
  31.7 1.9 %shard_map.140 = (f32[768,512]{1,0:T(8,128)S(1)}, bf16[2,2,128,128]{3,2,1,0:T(8,128)(2,1)S(1)}, f32[2,128,128]{2,1,0:T(8,128)S(1)}, f32[2,128,128]{2,1,0:T(8,128)S(1)}, bf16[6,128,640]{2,1,0:T(8,128)(2,1)S(1)}) custom-call(bf16[6,128,128]{2,1,0:T(8,128)(2,1)S(1)} %get-tuple-element.93.refs_0_.refs_10_, ...), custom_call_target="tpu_custom_call" | custom-call | flops 2000000000 | bytes 4194304 | tf_op jit(solution)/shard_map/pallas_call | solution.py:461
  33.6 0.8 %collective-permute-start.8 = (bf16[2,2,128,128]{3,2,1,0:T(8,128)(2,1)S(1)}, bf16[2,2,128,128]{3,2,1,0:T(8,128)(2,1)S(1)}, u32[]{:S(2)}, u32[]{:S(2)}) collective-permute-start(bf16[2,2,128,128]{3,2,1,0:T(8,128)(2,1)S(1)} %get-tuple-element.104.refs_8_.refs_6_), channel_id=1, source_target_pairs={{0,1},{1,0},{2,3},{3,2},{4,5},{5,4},{6,7},{7,6},{8,9},{9,8},{10,11... | collective-permute-start | bytes 393224 | tf_op jit(solution)/shard_map/ppermute | solution.py:546
  34.4 1.4 %shard_map.141 = (f32[768,512]{1,0:T(8,128)S(1)}, f32[768,384]{1,0:T(8,128)S(1)}, f32[512,128]{1,0:T(8,128)S(1)}, bf16[4,16,128]{2,1,0:T(8,128)(2,1)S(1)}) custom-call(f32[768,512]{1,0:T(8,128)S(1)} %get-tuple-element.101.refs_0_, f32[768,384]{1,0:T(8,128)S(1)} %get-tuple-element.100.refs_4_.refs_1_, ...), custom_call_target="tpu_custom_call", output_to_operand_aliasing={{0}: (0, {}), {1}: (1, {})} | custom-call | flops 1000000000 | bytes 4194304 | tf_op jit(solution)/shard_map/pallas_call | solution.py:461
  35.8 0.0 collective-permute-done.8.refs_7_
  35.8 0.0 collective-permute-done.6.refs_0_
  35.8 3.5 %shard_map.142 = (bf16[3,4,16,128]{3,2,1,0:T(8,128)(2,1)}, f32[4,128,128]{2,1,0:T(8,128)}, f32[4,128,128]{2,1,0:T(8,128)}) custom-call(bf16[6,128,128]{2,1,0:T(8,128)(2,1)S(1)} %collective-permute-done.6.refs_0_, f32[4,128,128]{2,1,0:T(8,128)S(1)} %get-tuple-element.94.refs_1_, f32[4,128,128]{2,1,0:T(8,128)S(1)} %get-tuple-element.95.refs_3_.refs_2_, ...), custom_call_target="tpu_custom_call" | custom-call | flops 3000000000 | bytes 4194304 | tf_op jit(solution)/shard_map/pallas_call | solution.py:461
Async XLA Ops:
  2.0 3.1 %collective-permute-start.1 = (bf16[6,128,128]{2,1,0:T(8,128)(2,1)S(1)}, bf16[6,128,128]{2,1,0:T(8,128)(2,1)S(1)}, u32[]{:S(2)}, u32[]{:S(2)}) collective-permute-start(bf16[6,128,128]{2,1,0:T(8,128)(2,1)S(1)} %get-tuple-element.63), channel_id=1, source_target_pairs={{0,1},{1,0},{2,3},{3,2},{4,5},{5,4},{6,7},{7,6},{8,9},{9,8},{10,11... | collective-permute-start | bytes 589832 | tf_op jit(solution)/shard_map/ppermute | solution.py:512
  2.6 10.3 %collective-permute-start = (bf16[11,128,128]{2,1,0:T(8,128)(2,1)S(1)}, bf16[11,128,128]{2,1,0:T(8,128)(2,1)S(1)}, u32[]{:S(2)}, u32[]{:S(2)}) collective-permute-start(bf16[11,128,128]{2,1,0:T(8,128)(2,1)S(1)} %get-tuple-element.59.refs_0_), channel_id=1, source_target_pairs={{1,2},{3,4},{5,6},{7,8},{9,10},{11,12},{13,14},{17,18},{19,20},{21... | collective-permute-start | bytes 1081352 | tf_op jit(solution)/shard_map/ppermute | solution.py:513
  11.3 1.6 %collective-permute-start.2 = (bf16[2,2,128,128]{3,2,1,0:T(8,128)(2,1)S(1)}, bf16[2,2,128,128]{3,2,1,0:T(8,128)(2,1)S(1)}, u32[]{:S(2)}, u32[]{:S(2)}) collective-permute-start(bf16[2,2,128,128]{3,2,1,0:T(8,128)(2,1)S(1)} %get-tuple-element.72.refs_8_.refs_6_.refs_4_), channel_id=1, source_target_pairs={{0,1},{1,0},{2,3},{3,2},{4,5},{5,4},{6,7},{7,6},{8,9},{9,8},{10,11... | collective-permute-start | bytes 393224 | tf_op jit(solution)/shard_map/ppermute | solution.py:546
  16.1 4.4 %collective-permute-start.4 = (bf16[2,128,128]{2,1,0:T(8,128)(2,1)S(1)}, bf16[2,128,128]{2,1,0:T(8,128)(2,1)S(1)}, u32[]{:S(2)}, u32[]{:S(2)}) collective-permute-start(bf16[2,128,128]{2,1,0:T(8,128)(2,1)S(1)} %get-tuple-element.82), channel_id=1, source_target_pairs={{0,1},{1,0},{2,3},{3,2},{4,5},{5,4},{6,7},{7,6},{8,9},{9,8},{10,11... | collective-permute-start | bytes 196616 | tf_op jit(solution)/shard_map/ppermute | solution.py:597
  16.8 8.3 %collective-permute-start.3 = (bf16[7,128,128]{2,1,0:T(8,128)(2,1)S(1)}, bf16[7,128,128]{2,1,0:T(8,128)(2,1)S(1)}, u32[]{:S(2)}, u32[]{:S(2)}) collective-permute-start(bf16[7,128,128]{2,1,0:T(8,128)(2,1)S(1)} %get-tuple-element.78.refs_0_.refs_10_), channel_id=1, source_target_pairs={{1,2},{3,4},{5,6},{7,8},{9,10},{11,12},{13,14},{17,18},{19,20},{21... | collective-permute-start | bytes 688136 | tf_op jit(solution)/shard_map/ppermute | solution.py:598
  20.6 3.1 %copy-start = (bf16[128,16]{0,1:T(8,128)(2,1)S(1)}, bf16[128,16]{0,1:T(8,128)(2,1)}, u32[]{:S(2)}) copy-start(bf16[128,16]{0,1:T(8,128)(2,1)} %param.21) | copy-start | bytes 12292
  22.5 2.5 %collective-permute-start.5 = (bf16[2,2,128,128]{3,2,1,0:T(8,128)(2,1)S(1)}, bf16[2,2,128,128]{3,2,1,0:T(8,128)(2,1)S(1)}, u32[]{:S(2)}, u32[]{:S(2)}) collective-permute-start(bf16[2,2,128,128]{3,2,1,0:T(8,128)(2,1)S(1)} %get-tuple-element.89.refs_8_.refs_6_.refs_4_), channel_id=1, source_target_pairs={{0,1},{1,0},{2,3},{3,2},{4,5},{5,4},{6,7},{7,6},{8,9},{9,8},{10,11... | collective-permute-start | bytes 393224 | tf_op jit(solution)/shard_map/ppermute | solution.py:546
  27.9 3.9 %collective-permute-start.7 = (bf16[2,128,128]{2,1,0:T(8,128)(2,1)S(1)}, bf16[2,128,128]{2,1,0:T(8,128)(2,1)S(1)}, u32[]{:S(2)}, u32[]{:S(2)}) collective-permute-start(bf16[2,128,128]{2,1,0:T(8,128)(2,1)S(1)} %get-tuple-element.97), channel_id=1, source_target_pairs={{0,1},{1,0},{2,3},{3,2},{4,5},{5,4},{6,7},{7,6},{8,9},{9,8},{10,11... | collective-permute-start | bytes 196616 | tf_op jit(solution)/shard_map/ppermute | solution.py:597
  28.0 7.8 %collective-permute-start.6 = (bf16[6,128,128]{2,1,0:T(8,128)(2,1)S(1)}, bf16[6,128,128]{2,1,0:T(8,128)(2,1)S(1)}, u32[]{:S(2)}, u32[]{:S(2)}) collective-permute-start(bf16[6,128,128]{2,1,0:T(8,128)(2,1)S(1)} %get-tuple-element.93.refs_0_.refs_10_), channel_id=1, source_target_pairs={{1,2},{3,4},{5,6},{7,8},{9,10},{11,12},{13,14},{17,18},{19,20},{21... | collective-permute-start | bytes 589832 | tf_op jit(solution)/shard_map/ppermute | solution.py:598
  33.6 2.2 %collective-permute-start.8 = (bf16[2,2,128,128]{3,2,1,0:T(8,128)(2,1)S(1)}, bf16[2,2,128,128]{3,2,1,0:T(8,128)(2,1)S(1)}, u32[]{:S(2)}, u32[]{:S(2)}) collective-permute-start(bf16[2,2,128,128]{3,2,1,0:T(8,128)(2,1)S(1)} %get-tuple-element.104.refs_8_.refs_6_), channel_id=1, source_target_pairs={{0,1},{1,0},{2,3},{3,2},{4,5},{5,4},{6,7},{7,6},{8,9},{9,8},{10,11... | collective-permute-start | bytes 393224 | tf_op jit(solution)/shard_map/ppermute | solution.py:546
